TPU v7x, 512 devices: a whole 4x8x8 slice. The times are simulated.
512 devices in a mesh: space: 64 (over x, z, core), snap: 8 (over y).
Axes of the slice: x: 4, y: 8, z: 8, core: 2. Of those that a mesh axis runs over, the one named last changes fastest.
Arguments:
- snapshots: bfloat16 [32768, 3, 1024], P('space', None, 'snap'), may hold values from -16 to 16
- mass_blocks: bfloat16 [512, 7, 4096], P('space'), may hold values from -0.25 to 0.25
- block_cols: int32 [512, 7], P('space'), may hold values from 0 to 511, as said below
- coefficients: bfloat16 [1024, 64], P('snap'), may hold values from -0.1875 to 0.1875
- lumped: float32 [32768], P('space'), may hold values from 0.3 to 9
Outputs:
- gram: float32 [1024, 1024], P('snap', 'space')
- modes: bfloat16 [32768, 3, 64], P('space')
Inputs may be any that keep to these rules, and one draw needn't show every extreme that they name: `block_cols`: entries 0, 1, 2 of row b are b, b - 1, b + 1 (b itself where that block does not exist); every entry lies within 3 blocks of its row; entries may repeat.
All inputs are finite; a program needn't handle non-finite values.
Results may differ from a plain program's by a relative error of at most 0.0029.
Values may be sent and summed in bfloat16 or wider, within the bound.
No kernel may reach another device: no remote copies, remote signals or barrier semaphores. Data moves between devices by JAX's collectives and lax.ppermute only.
A program may use at most 128 MiB of HBM per device.

v0:
```python
import jax
import jax.numpy as jnp
from jax import lax
from jax.sharding import PartitionSpec as P

BLOCK = 64
BPR = 7
REACH = 3


def padded(block, sides, width):
    for axis, dim in sides:
        count = lax.axis_size(axis)
        forward = [(i, i + 1) for i in range(count - 1)]
        backward = [(target, source) for source, target in forward]
        low = lax.ppermute(
            lax.slice_in_dim(block, block.shape[dim] - width, None, axis=dim), axis, forward
        )
        high = lax.ppermute(lax.slice_in_dim(block, 0, width, axis=dim), axis, backward)
        block = jnp.concatenate([low, block, high], axis=dim)
    return block


def local(snapshots, mass_blocks, block_cols, coefficients, lumped):
    node_rows = snapshots.shape[0]
    snap_cols = snapshots.shape[2]
    block_count = mass_blocks.shape[0]
    square_mass = mass_blocks.reshape(block_count, BPR, BLOCK, BLOCK)
    space_count = lax.axis_size("space")
    snap_count = lax.axis_size("snap")
    flat_rows = snapshots.reshape(node_rows, 3 * snap_cols)
    extended = padded(flat_rows, (("space", 0),), REACH * BLOCK)
    ext_blocks = extended.reshape(-1, BLOCK, 3 * snap_cols)
    first_block = lax.axis_index("space") * block_count - REACH
    local_cols = block_cols - first_block
    summed = jnp.zeros((block_count, BLOCK, 3 * snap_cols), jnp.float32)
    for column in range(BPR):
        near_blocks = jnp.take(ext_blocks, local_cols[:, column], axis=0)
        summed = summed + jnp.einsum(
            "bnm,bmw->bnw", square_mass[:, column], near_blocks, preferred_element_type=jnp.float32
        )
    mass_image = summed.astype(jnp.bfloat16).reshape(node_rows, 3, snap_cols)
    total_nodes = node_rows * space_count
    gram_scale = (3.0 * total_nodes) ** (-0.5)
    all_snaps = snap_cols * snap_count
    out_cols = all_snaps // space_count
    left_rows, right_rows = (
        lax.all_to_all(snapshots, "snap", split_axis=0, concat_axis=2, tiled=True),
        lax.all_to_all(mass_image, "snap", split_axis=0, concat_axis=2, tiled=True),
    )
    few_rows = left_rows.shape[0]
    left_split = left_rows.reshape(few_rows, 3, snap_count, snap_cols)
    right_split = right_rows.reshape(few_rows, 3, space_count, out_cols)
    partial_gram = jnp.einsum(
        "rcta,rcsb->stab", left_split, right_split, preferred_element_type=jnp.float32
    )
    partial_gram = partial_gram.reshape(space_count * snap_count, snap_cols * out_cols)
    tile_sum = lax.psum_scatter(partial_gram, ("space", "snap"), scatter_dimension=0, tiled=True)
    gram = tile_sum.reshape(snap_cols, out_cols) * gram_scale
    entries = 3.0 * total_nodes
    mode_terms = jnp.einsum(
        "nca,ak->nck", snapshots, coefficients, preferred_element_type=jnp.float32
    )
    raw_modes = lax.psum(mode_terms, "snap")
    norm_sums = lax.psum(
        jnp.sum(lumped[:, None, None] * raw_modes * raw_modes, axis=(0, 1)), "space"
    )
    modes = (raw_modes * lax.rsqrt(norm_sums / entries + 1e-06)).astype(jnp.bfloat16)
    return (gram, modes)


def solution(mesh):
    return jax.shard_map(
        local,
        mesh=mesh,
        in_specs=(
            P("space", None, "snap"),
            P("space", None, None),
            P("space", None),
            P("snap", None),
            P("space"),
        ),
        out_specs=(P("snap", "space"), P("space", None, None)),
        check_vma=False,
    )
```

profile of v0, /device:TPU:1, one launch (start us, length us, event | category | flops | bytes accessed | tf_op | source)
XLA Modules:
  0.0 445.9 jit_solution(3125048373646565530)
XLA Ops:
  7.2 1.0 slice_bitcast_fusion
  8.2 5.4 %collective-permute-start = (bf16[192,384]{1,0:T(8,128)(2,1)S(1)}, bf16[192,384]{1,0:T(8,128)(2,1)S(1)}, u32[]{:S(2)}, u32[]{:S(2)}) collective-permute-start(bf16[192,384]{1,0:T(8,128)(2,1)S(1)} %bitcast.68), channel_id=1, source_target_pairs={{0,8},{8,16},{16,24},{24,32},{32,40},{40,48},{48,56},{56,64},{64,7... | collective-permute-start | bytes 442376 | tf_op jit(solution)/shard_map/ppermute | solution.py:16
  13.6 0.1 copy.43
  13.8 4.7 %collective-permute-start.1 = (bf16[192,384]{0,1:T(8,128)(2,1)S(1)}, bf16[192,384]{0,1:T(8,128)(2,1)S(1)}, u32[]{:S(2)}, u32[]{:S(2)}) collective-permute-start(bf16[192,384]{0,1:T(8,128)(2,1)S(1)} %bitcast.67), channel_id=1, source_target_pairs={{8,0},{16,8},{24,16},{32,24},{40,32},{48,40},{56,48},{64,56},{72,6... | collective-permute-start | bytes 442376 | tf_op jit(solution)/shard_map/ppermute | solution.py:19
  18.5 0.7 broadcast_subtract_fusion
  19.2 0.3 slice_reduce_fusion
  19.7 1.2 copy.29
  20.8 1.9 reshape.39
  22.8 0.1 copy.32
  23.0 0.3 pad_maximum_fusion
  23.3 0.4 copy.33
  23.7 1.3 gather_fusion
  25.0 1.3 gather_fusion.1
  26.3 0.6 gather_fusion.2
  27.0 0.6 gather_fusion.3
  27.6 0.6 gather_fusion.4
  28.3 0.6 gather_fusion.5
  28.9 1.3 gather_fusion.6
  30.2 1.3 fusion.12
  31.6 1.3 convolution_add_fusion.5
  32.9 0.3 convolution_add_fusion.4
  33.2 0.3 convolution_add_fusion.3
  33.6 0.3 convolution_add_fusion.2
  33.9 0.3 convolution_add_fusion.1
  34.2 0.3 fusion.1
  34.6 0.9 reshape.40
  35.5 4.6 %all-to-all-start = ((bf16[512,3,128]{2,1,0:T(4,128)(2,1)}), bf16[512,3,128]{2,1,0:T(4,128)(2,1)S(1)}, u32[]{:S(2)}, u32[]{:S(2)}) async-start(bf16[512,3,128]{2,1,0:T(4,128)(2,1)} %reshape.40), calls=%async_computation | async-start | bytes 1048576 | tf_op jit(solution)/shard_map/all_to_all | solution.py:49
  40.1 1.1 copy.35
  41.3 15.3 %all-to-all-done = bf16[512,3,128]{2,1,0:T(4,128)(2,1)S(1)} async-done(((bf16[512,3,128]{2,1,0:T(4,128)(2,1)}), bf16[512,3,128]{2,1,0:T(4,128)(2,1)S(1)}, u32[]{:S(2)}, u32[]{:S(2)}) %all-to-all-start) | async-done | bytes 393248 | tf_op jit(solution)/shard_map/all_to_all | solution.py:49
  56.5 3.5 all-to-all-start.1
  60.0 0.0 all-reduce.4.cloned.1.call-start
  60.1 1.0 fusion.28
  61.1 0.0 all-reduce.4.cloned.1.call-update
  61.1 0.0 all-reduce.6.cloned.1.call-start
  61.2 0.6 copy.34
  61.8 16.2 %all-to-all-done.1 = bf16[512,3,128]{2,1,0:T(4,128)(2,1)S(1)} async-done(((bf16[512,3,128]{2,1,0:T(4,128)(2,1)}), bf16[512,3,128]{2,1,0:T(4,128)(2,1)S(1)}, u32[]{:S(2)}, u32[]{:S(2)}) %all-to-all-start.1) | async-done | bytes 393248 | tf_op jit(solution)/shard_map/all_to_all | solution.py:48
  78.0 2.8 convolution_bitcast_fusion
  80.8 16.9 %copy.39 = f32[64,8,128,16]{3,2,1,0:T(8,128)} copy(f32[64,8,128,16]{2,3,1,0:T(8,128)} %convolution_bitcast_fusion) | data formatting | bytes 8388608 | tf_op jit(solution)/shard_map/rcta,rcsb->stab/transpose | solution.py:54
  97.6 28.3 %reshape.42 = f32[512,2048]{1,0:T(8,128)} reshape(f32[64,8,128,16]{3,2,1,0:T(8,128)} %copy.39) | data formatting | bytes 8388608 | tf_op jit(solution)/shard_map/reshape | solution.py:57
  126.0 0.0 all-reduce.6.cloned.1.call-update
  126.0 16.3 %all-reduce.4.cloned.1.call-done = f32[512,3,64]{0,2,1:T(8,128)} async-done(((f32[512,3,64]{0,2,1:T(8,128)}), f32[512,3,64]{0,2,1:T(8,128)}) %all-reduce.4.cloned.1.call-update) | async-done | bytes 393232 | tf_op jit(solution)/shard_map/psum | solution.py:64
  142.3 1.1 fusion.3
  143.5 130.0 %psum.15 = f32[64]{0:T(128)S(1)} all-reduce(f32[64]{0:T(128)S(1)} %fusion.3), channel_id=1, replica_groups=mesh['space'=64,'snap'=8] {'space'}, use_global_device_ids=true, to_apply=%region_3.5 | all-reduce | flops 64 | bytes 512 | tf_op jit(solution)/shard_map/psum | solution.py:65
  273.5 1.8 multiply_convert_fusion
  275.3 162.2 %all-reduce.6.cloned.1.call-done = f32[512,2048]{1,0:T(8,128)} async-done(((f32[512,2048]{1,0:T(8,128)}), f32[512,2048]{1,0:T(8,128)}) %all-reduce.6.cloned.1.call-update) | async-done | bytes 4194320
  437.5 0.9 fusion.30
  438.3 0.1 mul.34
  438.4 0.7 copy.40
  (27 shorter events, 0.2 us)
Async XLA Ops:
  7.2 52.9 %copy-start = (bf16[128,64]{0,1:T(8,128)(2,1)S(1)}, bf16[128,64]{0,1:T(8,128)(2,1)}, u32[]{:S(2)}) copy-start(bf16[128,64]{0,1:T(8,128)(2,1)} %param.10) | copy-start | bytes 49156
  8.2 14.6 %collective-permute-start = (bf16[192,384]{1,0:T(8,128)(2,1)S(1)}, bf16[192,384]{1,0:T(8,128)(2,1)S(1)}, u32[]{:S(2)}, u32[]{:S(2)}) collective-permute-start(bf16[192,384]{1,0:T(8,128)(2,1)S(1)} %bitcast.68), channel_id=1, source_target_pairs={{0,8},{8,16},{16,24},{24,32},{32,40},{40,48},{48,56},{56,64},{64,7... | collective-permute-start | bytes 442376 | tf_op jit(solution)/shard_map/ppermute | solution.py:16
  13.8 9.2 %collective-permute-start.1 = (bf16[192,384]{0,1:T(8,128)(2,1)S(1)}, bf16[192,384]{0,1:T(8,128)(2,1)S(1)}, u32[]{:S(2)}, u32[]{:S(2)}) collective-permute-start(bf16[192,384]{0,1:T(8,128)(2,1)S(1)} %bitcast.67), channel_id=1, source_target_pairs={{8,0},{16,8},{24,16},{32,24},{40,32},{48,40},{56,48},{64,56},{72,6... | collective-permute-start | bytes 442376 | tf_op jit(solution)/shard_map/ppermute | solution.py:19
  32.9 1.4 copy-start.2
  33.6 6.6 %copy-start.1 = (bf16[512,3,128]{2,0,1:T(8,128)(2,1)S(1)}, bf16[512,3,128]{2,0,1:T(8,128)(2,1)}, u32[]{:S(2)}) copy-start(bf16[512,3,128]{2,0,1:T(8,128)(2,1)} %param.7) | copy-start | bytes 1179652
  35.5 21.0 %all-to-all-start = ((bf16[512,3,128]{2,1,0:T(4,128)(2,1)}), bf16[512,3,128]{2,1,0:T(4,128)(2,1)S(1)}, u32[]{:S(2)}, u32[]{:S(2)}) async-start(bf16[512,3,128]{2,1,0:T(4,128)(2,1)} %reshape.40), calls=%async_computation | async-start | bytes 1048576 | tf_op jit(solution)/shard_map/all_to_all | solution.py:49
  56.5 21.4 %all-to-all-start.1 = ((bf16[512,3,128]{2,1,0:T(4,128)(2,1)}), bf16[512,3,128]{2,1,0:T(4,128)(2,1)S(1)}, u32[]{:S(2)}, u32[]{:S(2)}) async-start(bf16[512,3,128]{2,1,0:T(4,128)(2,1)} %copy.35), calls=%async_computation.1 | async-start | bytes 1048576 | tf_op jit(solution)/shard_map/all_to_all | solution.py:48
  60.0 82.3 %all-reduce.4.cloned.1.call-start = ((), (), s32[]{:S(2)}) async-start(), calls=%async_computation.2 | async-start | bytes 786432 | tf_op jit(solution)/shard_map/psum | solution.py:64
  61.1 376.4 %all-reduce.6.cloned.1.call-start = ((), (), s32[]{:S(2)}) async-start(), calls=%async_computation.3 | async-start | bytes 8388608
  126.0 16.4 %copy-start.3 = (f32[512]{0:T(512)S(1)}, f32[512]{0:T(512)}, u32[]{:S(2)}) copy-start(f32[512]{0:T(512)} %param.11) | copy-start | bytes 6148
Sparse Core Ops, SparseCore 0:
  63.2 79.1 all-reduce.3
  148.1 289.3 all-reduce.5
where the time goes:
time: 448 us; the launch traced here: 446 us
  waiting for transfers between devices  210 us (47%)
  blocking collectives  130 us (29%)
  local copies, waits for them, and re-layouts  60.2 us (13%)
  starting transfers between devices  18.3 us (4%)
  between operations  14.4 us (3%)
  matrix products  8.06 us (2%)
  other arithmetic  4.91 us (1%)
    unnamed x3, waiting for transfers between devices  162 us
    psum x1, blocking collectives, local(): lax.psum(jnp.sum(lumped[:, None, None] * raw_modes * raw_modes, axis=(0,...  130 us
    reshape x1, local copies, waits for them, and re-layouts, local(): partial_gram.reshape(space_count * snap_count, snap_cols * out_cols)  28.3 us
    transpose x1, local copies, waits for them, and re-layouts, local(): jnp.einsum('rcta,rcsb->stab', left_split, right_split, preferred_element_...  16.9 us
    psum x1, waiting for transfers between devices, local(): raw_modes = lax.psum(mode_terms, 'snap')  16.3 us
    all_to_all x1, waiting for transfers between devices, local(): lax.all_to_all(snapshots, 'snap', split_axis=0, concat_axis=2, tiled=True)  16.2 us
    all_to_all x1, waiting for transfers between devices, local(): lax.all_to_all(mass_image, 'snap', split_axis=0, concat_axis=2, tiled=True)  15.3 us
  transfers between devices with their start and end apart: 6, of which 4 were waited for; matrix products, arithmetic and copies ran while one was open for 13% of the time, Pallas kernels for 0%

commit v1 on v0

v1 whole, which is shorter than its diff:
```python
import jax
import jax.numpy as jnp
from jax import lax
from jax.experimental import pallas as pl
from jax.experimental.pallas import tpu as pltpu
from jax.sharding import Mesh, PartitionSpec as P

BLOCK = 64
BPR = 7
REACH = 3
NX, NZ, NC, NY = 4, 8, 2, 8
ROWS = 3 * BLOCK
MODES = 64
TILE = 128
NROW = 16
F32 = jnp.float32
BF16 = jnp.bfloat16
SPACE = ("x", "z", "core")


def image_kernel(cols, mass, own, low, high, out, ext):
    blocks = own.shape[1] // BLOCK
    index = (lax.axis_index("x") * NZ + lax.axis_index("z")) * NC + lax.axis_index("core")
    first = index * blocks - REACH
    for c in range(3):
        lanes = pl.ds(c * TILE, TILE)
        ext[:REACH, :, lanes] = low[c].reshape(REACH, BLOCK, TILE)
        ext[REACH : REACH + blocks, :, lanes] = own[c].reshape(blocks, BLOCK, TILE)
        ext[REACH + blocks :, :, lanes] = high[c].reshape(REACH, BLOCK, TILE)
    for b in range(blocks):
        near = jnp.concatenate([ext[cols[b, j] - first] for j in range(BPR)], axis=0)
        total = jnp.dot(mass[b], near, preferred_element_type=F32).astype(BF16)
        for c in range(3):
            out[b, c * BLOCK : (c + 1) * BLOCK, :] = total[:, c * TILE : (c + 1) * TILE]


def raw_kernel(snaps, lumped, raw_out, norm_out):
    raw = jnp.zeros((MODES, ROWS), F32)
    for t in range(NY):
        raw = raw + lax.dot_general(
            snaps[t, ROWS:, :], snaps[t, :ROWS, :], (((1,), (1,)), ((), ())), preferred_element_type=F32
        )
    column = jnp.zeros((MODES, 1), F32)
    for c in range(3):
        part = raw[:, c * BLOCK : (c + 1) * BLOCK]
        column = column + jnp.sum(lumped[...] * part * part, axis=1, keepdims=True)
        raw_out[c * 32 : (c + 1) * 32, :] = jnp.concatenate([part[:32], part[32:]], axis=1)
    k = lax.broadcasted_iota(jnp.int32, (MODES, TILE), 0)
    lane = lax.broadcasted_iota(jnp.int32, (MODES, TILE), 1)
    row = jnp.sum(jnp.where(lane % MODES == k, column, 0.0), axis=0, keepdims=True)
    norm_out[...] = split_row(row, NROW)


def split_row(row, count):
    high = row.astype(BF16)
    rest = (row - high.astype(F32)).astype(BF16)
    lane = lax.broadcasted_iota(jnp.int32, (1, TILE), 1)
    both = jnp.where(lane < MODES, high.astype(F32), rest.astype(F32))
    return jnp.broadcast_to(both, (count, TILE)).astype(BF16)


def join_row(row):
    return row + pltpu.roll(row, MODES, 1)


def gram_kernel(snaps, other_snaps, image, other_image, norm, out):
    core = lax.axis_index("core")
    half = NY // NC
    mine = [snaps[core * half + q, :ROWS, :] for q in range(half)]
    right = jnp.concatenate(
        [jnp.concatenate(mine, axis=1), jnp.concatenate([other_snaps[q] for q in range(half)], axis=1)], axis=0
    )
    per = NY // NX
    for t in range(NY):
        left = jnp.concatenate([image[t], other_image[t]], axis=0)
        tile = lax.dot_general(left, right, (((0,), (0,)), ((), ())), preferred_element_type=F32).astype(BF16)
        for q in range(half):
            base = q * per * TILE + (t % per) * TILE
            out[t // per, base : base + TILE, :] = tile[:, q * TILE : (q + 1) * TILE]
    for x in range(NX):
        out[x, half * per * TILE :, :] = norm[...]


def sum_x_kernel(parts, out):
    half = NY // NC
    per = 32
    total = parts[0].astype(F32)
    for x in range(1, NX):
        total = total + parts[x].astype(F32)
    rows = half * NZ * per
    for q in range(half):
        for z in range(NZ):
            base = (q * NZ + z) * per
            out[z, q * per : (q + 1) * per, :] = total[base : base + per].astype(BF16)
    row = split_row(join_row(total[rows : rows + 1]), NROW)
    for z in range(NZ):
        out[z, half * per :, :] = row


def sum_z_kernel(parts, out):
    core = lax.axis_index("core")
    half = NY // NC
    per = 32
    total = parts[0].astype(F32)
    for z in range(1, NZ):
        total = total + parts[z].astype(F32)
    rows = half * per
    row = jnp.broadcast_to(join_row(total[rows : rows + 1]), (8, TILE))
    for c in range(NC):
        for q in range(half):
            base = q * per + c * 16
            out[c * NY + core * half + q, :16, :] = total[base : base + 16]
            out[c * NY + (1 - core) * half + q, :16, :] = jnp.zeros((16, TILE), F32)
    for i in range(NC * NY):
        out[i, 16:, :] = row


def final_kernel(nodes, parts, raw, gram, modes):
    total = parts[0]
    for i in range(1, NC * NY):
        total = total + parts[i]
    gram[...] = total[:16] * (3.0 * nodes) ** (-0.5)
    row = lax.rsqrt(total[16:17] / (3.0 * nodes) + 1e-06)
    k = lax.broadcasted_iota(jnp.int32, (MODES, TILE), 0)
    lane = lax.broadcasted_iota(jnp.int32, (MODES, TILE), 1)
    column = jnp.sum(jnp.where(lane == k, row, 0.0), axis=1, keepdims=True)
    low, high = column[:32], column[32:]
    for c in range(3):
        rows = slice(c * 32, (c + 1) * 32)
        for u in range(NY // 2):
            a, b = raw[2 * u, rows, :], raw[2 * u + 1, rows, :]
            lanes = slice(u * TILE, (u + 1) * TILE)
            first = jnp.concatenate([a[:, :MODES], b[:, :MODES]], axis=1)
            second = jnp.concatenate([a[:, MODES:], b[:, MODES:]], axis=1)
            modes[c, :32, lanes] = (first * low).astype(BF16)
            modes[c, 32:, lanes] = (second * high).astype(BF16)


def call(kernel, shapes, *args, scratch=(), smem=0):
    specs = [pl.BlockSpec(memory_space=pltpu.SMEM)] * smem
    specs += [pl.BlockSpec(memory_space=pltpu.VMEM)] * (len(args) - smem)
    single = not isinstance(shapes, list)
    outs = [shapes] if single else shapes
    result = pl.pallas_call(
        kernel,
        out_shape=[jax.ShapeDtypeStruct(*s) for s in outs],
        in_specs=specs,
        out_specs=[pl.BlockSpec(memory_space=pltpu.VMEM)] * len(outs),
        scratch_shapes=list(scratch),
        compiler_params=pltpu.CompilerParams(vmem_limit_bytes=32 * 1024 * 1024),
    )(*args)
    return result[0] if single else result


def spread(value, axes):
    return lax.all_to_all(value, axes, split_axis=0, concat_axis=0, tiled=True)


def local(snapshots, mass_blocks, block_cols, coefficients, lumped):
    nodes = snapshots.shape[0]
    total_nodes = nodes * NX * NZ * NC
    own = jnp.transpose(snapshots, (1, 0, 2))
    width = REACH * BLOCK
    count = NX * NZ * NC
    forward = [(i, i + 1) for i in range(count - 1)]
    backward = [(i + 1, i) for i in range(count - 1)]
    low = lax.ppermute(own[:, nodes - width :, :], SPACE, forward)
    high = lax.ppermute(own[:, :width, :], SPACE, backward)

    weights = jnp.broadcast_to(coefficients.T[None], (NY, MODES, TILE))
    slots = own.reshape(3, NY, BLOCK, TILE).transpose(1, 0, 2, 3).reshape(NY, ROWS, TILE)
    snaps = spread(jnp.concatenate([slots, weights], axis=1), "y")

    mass = mass_blocks.reshape(NY, BPR, BLOCK, BLOCK).transpose(0, 2, 1, 3).reshape(NY, BLOCK, BPR * BLOCK)
    image = call(
        image_kernel,
        ((NY, ROWS, TILE), BF16),
        block_cols,
        mass,
        own,
        low,
        high,
        scratch=[pltpu.VMEM((NY + 2 * REACH, BLOCK, 3 * TILE), BF16)],
        smem=1,
    )
    image = spread(image, "y")

    swap = [(0, 1), (1, 0)]
    core = lax.axis_index("core")
    half = NY // NC
    theirs = lax.dynamic_slice(snaps, ((1 - core) * half, 0, 0), (half, ROWS, TILE))
    other_snaps = lax.ppermute(theirs, "core", swap)
    weight = lax.dynamic_slice(lumped, (lax.axis_index("y") * BLOCK,), (BLOCK,)).reshape(1, BLOCK)
    raw, norm = call(raw_kernel, [((96, TILE), F32), ((NROW, TILE), BF16)], snaps, weight)
    raw = spread(jnp.broadcast_to(raw[None], (NY, 96, TILE)), "y")

    other_image = lax.ppermute(image, "core", swap)
    parts = call(
        gram_kernel, ((NX, 1024 + NROW, TILE), BF16), snaps, other_snaps, image, other_image, norm
    )
    parts = spread(parts, "x")
    parts = call(sum_x_kernel, ((NZ, 128 + NROW, TILE), BF16), parts)
    parts = spread(parts, "z")
    parts = call(sum_z_kernel, ((NC * NY, 24, TILE), F32), parts)
    parts = spread(parts, ("core", "y"))
    gram, modes = call(
        lambda *refs: final_kernel(total_nodes, *refs),
        [((16, TILE), F32), ((3, MODES, nodes), BF16)],
        parts,
        raw,
    )
    return gram.T, jnp.transpose(modes, (2, 0, 1))


def solution(mesh):
    fine = Mesh(mesh.devices.reshape(NX, NZ, NC, NY), ("x", "z", "core", "y"))
    return jax.shard_map(
        local,
        mesh=fine,
        in_specs=(
            P(SPACE, None, "y"),
            P(SPACE, None, None),
            P(SPACE, None),
            P("y", None),
            P(SPACE),
        ),
        out_specs=(P("y", SPACE), P(SPACE, None, None)),
        check_vma=False,
    )
```

time: 448 us -> 134 us (0.30)
  waiting for transfers between devices: 210 us -> 38.4 us
  blocking collectives: 130 us -> 56.5 us
  local copies, waits for them, and re-layouts: 60.2 us -> 5.46 us
  between operations: 14.4 us -> 0.8 us
  starting transfers between devices: 18.3 us -> 26.4 us
  matrix products: 8.06 us -> 0 us
  Pallas kernels: 0 us -> 4.6 us
    unnamed x3 -> x0, waiting for transfers between devices: 162 us -> none
    psum x1 -> x0, blocking collectives: 130 us -> none  [local(): lax.psum(jnp.sum(lumped[:, None, None] * raw_modes * raw_modes, axis=(0,...]
    all_to_all x0 -> x3, blocking collectives: none -> 56.5 us  [spread(): return lax.all_to_all(value, axes, split_axis=0, concat_axis=0, tiled=True)]
    reshape x3 -> x5, local copies, waits for them, and re-layouts: 31.2 us -> 3.2 us  [the longest x3 3.1 us: local(): mass_blocks.reshape(NY, BPR, BLOCK, BLOCK).transpose(0, 2, 1, 3)]
    transpose x1 -> x0, local copies, waits for them, and re-layouts: 16.9 us -> none  [local(): jnp.einsum('rcta,rcsb->stab', left_split, right_split, preferred_element_...]
    psum x1 -> x0, waiting for transfers between devices: 16.3 us -> none  [local(): raw_modes = lax.psum(mode_terms, 'snap')]
    dot_general x9 -> x0, matrix products: 8.06 us -> none  [the longest x7 4.26 us: local(): jnp.einsum('bnm,bmw->bnw', square_mass[:, column], near_blocks, preferred...]
    gather x7 -> x0, local copies, waits for them, and re-layouts: 6.55 us -> none  [local(): near_blocks = jnp.take(ext_blocks, local_cols[:, column], axis=0)]
  transfers between devices with their start and end apart: 6 -> 7, of which waited for: 4 -> 4; matrix products, arithmetic and copies ran while one was open for 13% -> 3% of each run, Pallas kernels for 0% -> 0%
where the time goes in v1:
time: 134 us; the launch traced here: 133 us
  blocking collectives  56.5 us (42%)
  waiting for transfers between devices  38.4 us (29%)
  starting transfers between devices  26.4 us (20%)
  local copies, waits for them, and re-layouts  5.46 us (4%)
  Pallas kernels  4.6 us (3%)
    all_to_all x3, blocking collectives, spread(): return lax.all_to_all(value, axes, split_axis=0, concat_axis=0, tiled=True)  56.5 us
    all_to_all x3, waiting for transfers between devices, spread(): return lax.all_to_all(value, axes, split_axis=0, concat_axis=0, tiled=True)  37.9 us
    all_to_all x3, starting transfers between devices, spread(): return lax.all_to_all(value, axes, split_axis=0, concat_axis=0, tiled=True)  12.1 us
    ppermute x1, starting transfers between devices, local(): low = lax.ppermute(own[:, nodes - width:, :], SPACE, forward)  5.39 us
    ppermute x1, starting transfers between devices, local(): high = lax.ppermute(own[:, :width, :], SPACE, backward)  4.69 us
    pallas_call x6, Pallas kernels, call(): pl.pallas_call(kernel, out_shape=[jax.ShapeDtypeStruct(*s) for s in outs]...  4.6 us
    reshape x3, local copies, waits for them, and re-layouts, local(): mass_blocks.reshape(NY, BPR, BLOCK, BLOCK).transpose(0, 2, 1, 3)  3.1 us
  transfers between devices with their start and end apart: 7, of which 4 were waited for; matrix products, arithmetic and copies ran while one was open for 3% of the time, Pallas kernels for 0%

profile of v1, /device:TPU:1, one launch (start us, length us, event | category | flops | bytes accessed | tf_op | source)
XLA Modules:
  0.0 133.0 jit_solution(6038392653298881599)
XLA Ops:
  0.6 0.0 copy-start
  0.6 1.0 fusion
  1.7 5.4 %collective-permute-start.1 = (bf16[3,192,128]{2,1,0:T(8,128)(2,1)S(1)}, bf16[3,192,128]{2,1,0:T(8,128)(2,1)S(1)}, u32[]{:S(2)}, u32[]{:S(2)}) collective-permute-start(bf16[3,192,128]{2,1,0:T(8,128)(2,1)S(1)} %get-tuple-element.11), channel_id=1, source_target_pairs={{0,8},{8,16},{16,24},{24,32},{32,40},{40,48},{48,56},{56,64},{64,7... | collective-permute-start | bytes 442376 | tf_op jit(solution)/shard_map/ppermute | solution.py:167
  7.1 4.7 %collective-permute-start.2 = (bf16[3,192,128]{2,1,0:T(8,128)(2,1)S(1)}, bf16[3,192,128]{2,1,0:T(8,128)(2,1)S(1)}, u32[]{:S(2)}, u32[]{:S(2)}) collective-permute-start(bf16[3,192,128]{2,1,0:T(8,128)(2,1)S(1)} %get-tuple-element.10), channel_id=1, source_target_pairs={{8,0},{16,8},{24,16},{32,24},{40,32},{48,40},{56,48},{64,56},{72,6... | collective-permute-start | bytes 442376 | tf_op jit(solution)/shard_map/ppermute | solution.py:168
  11.8 1.9 %reshape.23 = bf16[8,7,64,64]{3,2,0,1:T(8,128)(2,1)S(1)} reshape(bf16[8,7,4096]{2,0,1:T(8,128)(2,1)} %param.6) | data formatting | bytes 917504 | tf_op jit(solution)/shard_map/reshape | solution.py:174
  13.7 0.6 copy.12
  14.3 0.0 copy-start.1
  14.3 0.0 copy-start.2
  14.4 0.5 reshape.24.mass
  14.9 0.0 collective-permute-done.1.low
  14.9 0.0 collective-permute-done.2.high
  14.9 0.4 copy-done.1
  15.3 0.0 copy-done.2
  15.3 2.1 %shard_map.68 = bf16[8,192,128]{2,1,0:T(8,128)(2,1)} custom-call(s32[8,7]{1,0:T(8,128)S(1)} %copy-done.2, bf16[8,64,448]{2,1,0:T(8,128)(2,1)S(1)} %reshape.24.mass, bf16[3,512,128]{2,1,0:T(8,128)(2,1)S(1)} %bitcast.17, bf16[3,192,128]{2,1,0:T(8,128)(2,1)S(1)} %collective-permute-done.1.low, bf16[3,192,128]{2,1,0:T(8,128)(2,1)S(1)} %collective-permute-done.2.high), custom_call_target="tpu_custom_call" | custom-call | tf_op jit(solution)/shard_map/pallas_call | solution.py:144
  17.4 0.0 copy-start.3
  17.4 5.1 %all-to-all-start.1 = ((bf16[8,192,128]{2,1,0:T(8,128)(2,1)}), bf16[8,192,128]{2,1,0:T(8,128)(2,1)S(1)}, u32[]{:S(2)}, u32[]{:S(2)}) async-start(bf16[8,192,128]{2,1,0:T(8,128)(2,1)} %shard_map.68), calls=%async_computation.1 | async-start | bytes 786432 | tf_op jit(solution)/shard_map/all_to_all | solution.py:156
  22.6 0.0 copy-done.3
  22.6 0.8 pad_maximum_fusion
  23.4 12.3 %all-to-all-done.1.image = bf16[8,192,128]{2,1,0:T(8,128)(2,1)S(1)} async-done(((bf16[8,192,128]{2,1,0:T(8,128)(2,1)}), bf16[8,192,128]{2,1,0:T(8,128)(2,1)S(1)}, u32[]{:S(2)}, u32[]{:S(2)}) %all-to-all-start.1) | async-done | bytes 393248 | tf_op jit(solution)/shard_map/all_to_all | solution.py:156
  35.7 3.5 %all-to-all-start = ((bf16[8,256,128]{2,1,0:T(8,128)(2,1)}), bf16[8,256,128]{2,1,0:T(8,128)(2,1)S(1)}, u32[]{:S(2)}, u32[]{:S(2)}) async-start(bf16[8,256,128]{2,1,0:T(8,128)(2,1)} %pad_maximum_fusion), calls=%async_computation | async-start | bytes 1048576 | tf_op jit(solution)/shard_map/all_to_all | solution.py:156
  39.2 1.9 %collective-permute-start.3 = (bf16[8,192,128]{2,1,0:T(8,128)(2,1)S(1)}, bf16[8,192,128]{2,1,0:T(8,128)(2,1)S(1)}, u32[]{:S(2)}, u32[]{:S(2)}) collective-permute-start(bf16[8,192,128]{2,1,0:T(8,128)(2,1)S(1)} %all-to-all-done.1.image), channel_id=1, source_target_pairs={{0,8},{8,0},{1,9},{9,1},{2,10},{10,2},{3,11},{11,3},{4,12},{12,4},... | collective-permute-start | bytes 1179656 | tf_op jit(solution)/shard_map/ppermute | solution.py:197
  41.1 15.3 %all-to-all-done.snaps = bf16[8,256,128]{2,1,0:T(8,128)(2,1)S(1)} async-done(((bf16[8,256,128]{2,1,0:T(8,128)(2,1)}), bf16[8,256,128]{2,1,0:T(8,128)(2,1)S(1)}, u32[]{:S(2)}, u32[]{:S(2)}) %all-to-all-start) | async-done | bytes 524320 | tf_op jit(solution)/shard_map/all_to_all | solution.py:156
  56.5 2.3 %collective-permute-start = (bf16[4,192,128]{2,1,0:T(8,128)(2,1)S(1)}, bf16[4,192,128]{2,1,0:T(8,128)(2,1)S(1)}, u32[]{:S(2)}, u32[]{:S(2)}) collective-permute-start(bf16[4,192,128]{2,1,0:T(8,128)(2,1)S(1)} %constant_dynamic-slice_fusion), channel_id=1, source_target_pairs={{0,8},{8,0},{1,9},{9,1},{2,10},{10,2},{3,11},{11,3},{4,12},{12,4},... | collective-permute-start | bytes 589832 | tf_op jit(solution)/shard_map/ppermute | solution.py:192
  58.8 0.0 copy-done
  58.8 0.1 dynamic-slice_bitcast_fusion.lumped
  58.9 0.5 shard_map.69
  59.4 0.4 collective-permute-done.other_snaps
  59.8 0.0 collective-permute-done.3.other_image
  59.8 0.7 shard_map.70
  60.6 18.6 %all_to_all.30.parts = bf16[4,1040,128]{2,1,0:T(8,128)(2,1)S(1)} all-to-all(bf16[4,1040,128]{2,1,0:T(8,128)(2,1)S(1)} %shard_map.70), channel_id=1, replica_groups=mesh['x'=4,'z'=8,'core'=2,'y'=8] {'x'}, dimensions={0} | all-to-all | bytes 2129920 | tf_op jit(solution)/shard_map/all_to_all | solution.py:156
  79.2 0.3 shard_map.71
  79.5 22.1 %all_to_all.31.parts = bf16[8,144,128]{2,1,0:T(8,128)(2,1)S(1)} all-to-all(bf16[8,144,128]{2,1,0:T(8,128)(2,1)S(1)} %shard_map.71), channel_id=1, replica_groups=mesh['x'=4,'z'=8,'core'=2,'y'=8] {'z'}, dimensions={0} | all-to-all | bytes 589824 | tf_op jit(solution)/shard_map/all_to_all | solution.py:156
  101.6 0.8 broadcast_in_dim.5
  102.4 3.5 %all-to-all-start.5 = ((f32[8,96,128]{2,1,0:T(8,128)}), f32[8,96,128]{2,1,0:T(8,128)S(1)}, u32[]{:S(2)}, u32[]{:S(2)}) async-start(f32[8,96,128]{2,1,0:T(8,128)} %broadcast_in_dim.5), calls=%async_computation.5 | async-start | bytes 786432 | tf_op jit(solution)/shard_map/all_to_all | solution.py:156
  105.8 0.1 shard_map.72
  105.9 10.3 %all-to-all-done.5.refs_1_ = f32[8,96,128]{2,1,0:T(8,128)S(1)} async-done(((f32[8,96,128]{2,1,0:T(8,128)}), f32[8,96,128]{2,1,0:T(8,128)S(1)}, u32[]{:S(2)}, u32[]{:S(2)}) %all-to-all-start.5) | async-done | bytes 393248 | tf_op jit(solution)/shard_map/all_to_all | solution.py:156
  116.3 15.8 %all_to_all.32.refs_0_ = f32[16,24,128]{2,1,0:T(8,128)S(1)} all-to-all(f32[16,24,128]{2,1,0:T(8,128)S(1)} %shard_map.72), channel_id=1, replica_groups=mesh['x'=4,'z'=8,'core'=2,'y'=8] {'core','y'}, dimensions={0} | all-to-all | bytes 393216 | tf_op jit(solution)/shard_map/all_to_all | solution.py:156
  132.1 0.9 shard_map.73
  (3 shorter events, 0.1 us)
Async XLA Ops:
  0.6 58.2 %copy-start = (f32[512]{0:T(512)S(1)}, f32[512]{0:T(512)}, u32[]{:S(2)}) copy-start(f32[512]{0:T(512)} %param.9) | copy-start | bytes 6148
  1.7 13.2 %collective-permute-start.1 = (bf16[3,192,128]{2,1,0:T(8,128)(2,1)S(1)}, bf16[3,192,128]{2,1,0:T(8,128)(2,1)S(1)}, u32[]{:S(2)}, u32[]{:S(2)}) collective-permute-start(bf16[3,192,128]{2,1,0:T(8,128)(2,1)S(1)} %get-tuple-element.11), channel_id=1, source_target_pairs={{0,8},{8,16},{16,24},{24,32},{32,40},{40,48},{48,56},{56,64},{64,7... | collective-permute-start | bytes 442376 | tf_op jit(solution)/shard_map/ppermute | solution.py:167
  7.1 7.9 %collective-permute-start.2 = (bf16[3,192,128]{2,1,0:T(8,128)(2,1)S(1)}, bf16[3,192,128]{2,1,0:T(8,128)(2,1)S(1)}, u32[]{:S(2)}, u32[]{:S(2)}) collective-permute-start(bf16[3,192,128]{2,1,0:T(8,128)(2,1)S(1)} %get-tuple-element.10), channel_id=1, source_target_pairs={{8,0},{16,8},{24,16},{32,24},{40,32},{48,40},{56,48},{64,56},{72,6... | collective-permute-start | bytes 442376 | tf_op jit(solution)/shard_map/ppermute | solution.py:168
  14.3 1.0 copy-start.1
  14.3 1.0 copy-start.2
  17.4 5.2 %copy-start.3 = (bf16[128,64]{0,1:T(8,128)(2,1)S(1)}, bf16[128,64]{0,1:T(8,128)(2,1)}, u32[]{:S(2)}) copy-start(bf16[128,64]{0,1:T(8,128)(2,1)} %param.8) | copy-start | bytes 49156
  17.4 18.3 %all-to-all-start.1 = ((bf16[8,192,128]{2,1,0:T(8,128)(2,1)}), bf16[8,192,128]{2,1,0:T(8,128)(2,1)S(1)}, u32[]{:S(2)}, u32[]{:S(2)}) async-start(bf16[8,192,128]{2,1,0:T(8,128)(2,1)} %shard_map.68), calls=%async_computation.1 | async-start | bytes 786432 | tf_op jit(solution)/shard_map/all_to_all | solution.py:156
  35.7 20.8 %all-to-all-start = ((bf16[8,256,128]{2,1,0:T(8,128)(2,1)}), bf16[8,256,128]{2,1,0:T(8,128)(2,1)S(1)}, u32[]{:S(2)}, u32[]{:S(2)}) async-start(bf16[8,256,128]{2,1,0:T(8,128)(2,1)} %pad_maximum_fusion), calls=%async_computation | async-start | bytes 1048576 | tf_op jit(solution)/shard_map/all_to_all | solution.py:156
  39.2 20.7 %collective-permute-start.3 = (bf16[8,192,128]{2,1,0:T(8,128)(2,1)S(1)}, bf16[8,192,128]{2,1,0:T(8,128)(2,1)S(1)}, u32[]{:S(2)}, u32[]{:S(2)}) collective-permute-start(bf16[8,192,128]{2,1,0:T(8,128)(2,1)S(1)} %all-to-all-done.1.image), channel_id=1, source_target_pairs={{0,8},{8,0},{1,9},{9,1},{2,10},{10,2},{3,11},{11,3},{4,12},{12,4},... | collective-permute-start | bytes 1179656 | tf_op jit(solution)/shard_map/ppermute | solution.py:197
  56.5 3.4 %collective-permute-start = (bf16[4,192,128]{2,1,0:T(8,128)(2,1)S(1)}, bf16[4,192,128]{2,1,0:T(8,128)(2,1)S(1)}, u32[]{:S(2)}, u32[]{:S(2)}) collective-permute-start(bf16[4,192,128]{2,1,0:T(8,128)(2,1)S(1)} %constant_dynamic-slice_fusion), channel_id=1, source_target_pairs={{0,8},{8,0},{1,9},{9,1},{2,10},{10,2},{3,11},{11,3},{4,12},{12,4},... | collective-permute-start | bytes 589832 | tf_op jit(solution)/shard_map/ppermute | solution.py:192
  102.4 13.9 %all-to-all-start.5 = ((f32[8,96,128]{2,1,0:T(8,128)}), f32[8,96,128]{2,1,0:T(8,128)S(1)}, u32[]{:S(2)}, u32[]{:S(2)}) async-start(f32[8,96,128]{2,1,0:T(8,128)} %broadcast_in_dim.5), calls=%async_computation.5 | async-start | bytes 786432 | tf_op jit(solution)/shard_map/all_to_all | solution.py:156

commit v2 on v0

v2 whole, which is shorter than its diff:
```python
import jax
import jax.numpy as jnp
from jax import lax
from jax.experimental import pallas as pl
from jax.experimental.pallas import tpu as pltpu
from jax.sharding import Mesh, PartitionSpec as P

BLOCK = 64
BPR = 7
REACH = 3
NX, NZ, NC, NY = 4, 8, 2, 8
NSPACE = NX * NZ * NC
MODES = 64
TILE = 128
OWN = 16
SLOT = 24
F32 = jnp.float32
BF16 = jnp.bfloat16
SPACE = ("x", "z", "core")
ALONG = (((0,), (0,)), ((), ()))


def dual_kernel(cols, mass, own, low, mid, high, acc):
    blocks = own.shape[1] // BLOCK
    index = (lax.axis_index("x") * NZ + lax.axis_index("z")) * NC + lax.axis_index("core")
    first = index * blocks - REACH
    acc[...] = jnp.zeros_like(acc)
    for b in range(blocks):
        rows = slice(b * BLOCK, (b + 1) * BLOCK)
        right = jnp.concatenate([own[c, rows, :] for c in range(3)], axis=1)
        terms = lax.dot_general(mass[b], right, ALONG, preferred_element_type=F32)
        for j in range(BPR):
            place = cols[b, j] - first
            acc[place] += terms[j * BLOCK : (j + 1) * BLOCK]
    low[...] = acc[:REACH]
    mid[...] = acc[REACH : REACH + blocks]
    high[...] = acc[REACH + blocks :]


def join_kernel(mid, from_prev, from_next, out):
    blocks = mid.shape[0]
    for b in range(blocks):
        value = mid[b]
        if b < REACH:
            value = value + from_prev[b]
        if b >= blocks - REACH:
            value = value + from_next[b - blocks + REACH]
        high = value.astype(BF16)
        rest = (value - high.astype(F32)).astype(BF16)
        for c in range(3):
            rows = slice((c * blocks + b) * BLOCK, (c * blocks + b + 1) * BLOCK)
            lanes = slice(c * TILE, (c + 1) * TILE)
            out[rows, :TILE] = high[:, lanes]
            out[rows, TILE:] = rest[:, lanes]


def tile_products(tile, dual):
    rows = dual.shape[0]
    snaps = tile[:rows, :]
    both = lax.dot_general(snaps, dual, ALONG, preferred_element_type=F32)
    raw = lax.dot_general(
        tile[rows:, :], snaps, (((1,), (1,)), ((), ())), preferred_element_type=F32
    )
    return (both[:, :TILE] + both[:, TILE:]).astype(BF16), raw


def early_kernel(count, dual, lumped, *refs):
    tiles, gram, raw_out, lumped_out = refs[:count], refs[count], refs[count + 1], refs[count + 2]
    lumped_out[...] = lumped[...]
    for i in range(count):
        part, raw = tile_products(tiles[i][...], dual[...])
        gram[i] = part
        if i:
            raw_out[...] += raw
        else:
            raw_out[...] = raw


def late_kernel(near, dual, early, raw_in, lumped, forward, backward, half_a, half_b, slots, raw_out):
    me = lax.axis_index("y")
    nodes = raw_out.shape[2]
    far = jnp.concatenate([half_a[...], half_b[...]], axis=0)
    raw = raw_in[...]
    products = []
    for tile in (forward[...], backward[...], far):
        part, term = tile_products(tile, dual[...])
        products.append(part)
        raw = raw + term
    column = jnp.zeros((MODES, 1), F32)
    for c in range(3):
        part = raw[:, c * nodes : (c + 1) * nodes]
        raw_out[c] = part
        column = column + jnp.sum(lumped[...] * part * part, axis=1, keepdims=True)
    k = lax.broadcasted_iota(jnp.int32, (MODES, TILE), 0)
    lane = lax.broadcasted_iota(jnp.int32, (MODES, TILE), 1)
    row = jnp.sum(jnp.where(lane % MODES == k, column, 0.0), axis=0, keepdims=True)
    high = row.astype(BF16)
    rest = (row - high.astype(F32)).astype(BF16)
    lane = lax.broadcasted_iota(jnp.int32, (1, TILE), 1)
    both = jnp.where(lane < MODES, high.astype(F32), rest.astype(F32))
    norm = jnp.broadcast_to(both, (SLOT - OWN, TILE)).astype(BF16)
    steps = near + [3, NY - 3, 4]
    for i, step in enumerate(steps):
        source = lax.rem(me + step, NY)
        for o in range(TILE // OWN):
            rows = slice(o * OWN, (o + 1) * OWN)
            part = early[i, rows, :] if i < len(near) else products[i - len(near)][rows]
            slots[source * (TILE // OWN) + o] = jnp.concatenate([part, norm], axis=0)


def final_kernel(count, parts, raw, gram, modes):
    total = parts[0].astype(F32)
    for i in range(1, NSPACE):
        total = total + parts[i].astype(F32)
    gram[...] = total[:OWN] * count ** (-0.5)
    row = total[OWN : OWN + 1]
    row = row + pltpu.roll(row, MODES, 1)
    row = lax.rsqrt(row / count + 1e-06)
    k = lax.broadcasted_iota(jnp.int32, (MODES, TILE), 0)
    lane = lax.broadcasted_iota(jnp.int32, (MODES, TILE), 1)
    column = jnp.sum(jnp.where(lane == k, row, 0.0), axis=1, keepdims=True)
    for c in range(3):
        modes[c] = (raw[c] * column).astype(BF16)


def call(kernel, shapes, *args, scratch=(), smem=0):
    specs = [pl.BlockSpec(memory_space=pltpu.SMEM)] * smem
    specs += [pl.BlockSpec(memory_space=pltpu.VMEM)] * (len(args) - smem)
    single = not isinstance(shapes, list)
    outs = [shapes] if single else shapes
    result = pl.pallas_call(
        kernel,
        out_shape=[jax.ShapeDtypeStruct(*s) for s in outs],
        in_specs=specs,
        out_specs=[pl.BlockSpec(memory_space=pltpu.VMEM)] * len(outs),
        scratch_shapes=list(scratch),
        compiler_params=pltpu.CompilerParams(vmem_limit_bytes=32 * 1024 * 1024),
    )(*args)
    return result[0] if single else result


def shift(value, step):
    return lax.ppermute(value, "y", [(i, (i + step) % NY) for i in range(NY)])


def local(snapshots, mass_blocks, block_cols, coefficients, lumped):
    nodes = snapshots.shape[0]
    blocks = nodes // BLOCK
    own = jnp.transpose(snapshots, (1, 0, 2))
    tile = jnp.concatenate([own.reshape(3 * nodes, TILE), coefficients.T], axis=0)
    rows = tile.shape[0]

    mass = mass_blocks.reshape(blocks, BPR, BLOCK, BLOCK).transpose(0, 2, 1, 3)
    mass = mass.reshape(blocks, BLOCK, BPR * BLOCK)
    up, down = [tile], [tile]
    up.append(shift(tile, -1))
    down.append(shift(tile, 1))
    edge = ((REACH, BLOCK, 3 * TILE), F32)
    low, mid, high = call(
        dual_kernel,
        [edge, ((blocks, BLOCK, 3 * TILE), F32), edge],
        block_cols,
        mass,
        own,
        scratch=[pltpu.VMEM((blocks + 2 * REACH, BLOCK, 3 * TILE), F32)],
        smem=1,
    )
    second, third, low, high = lax.optimization_barrier((up[1], down[1], low, high))
    up.append(shift(second, -1))
    down.append(shift(third, 1))
    from_prev = lax.ppermute(high, SPACE, [(i, i + 1) for i in range(NSPACE - 1)])
    from_next = lax.ppermute(low, SPACE, [(i + 1, i) for i in range(NSPACE - 1)])
    dual = call(join_kernel, ((3 * nodes, 2 * TILE), BF16), mid, from_prev, from_next)

    up.append(shift(up[2], -1))
    down.append(shift(down[2], 1))
    half_a = shift(up[3][: rows // 2], -1)
    half_b = shift(down[3][rows // 2 :], 1)

    near = [0, 1, NY - 1, 2, NY - 2]
    early, raw, weight = call(
        lambda *refs: early_kernel(len(near), *refs),
        [((len(near), TILE, TILE), BF16), ((MODES, 3 * nodes), F32), ((1, nodes), F32)],
        dual,
        lumped.reshape(1, nodes),
        tile,
        up[1],
        down[1],
        up[2],
        down[2],
    )
    slots, raw = call(
        lambda *refs: late_kernel(near, *refs),
        [((NSPACE, SLOT, TILE), BF16), ((3, MODES, nodes), F32)],
        dual,
        early,
        raw,
        weight,
        up[3],
        down[3],
        half_a,
        half_b,
    )
    parts = lax.all_to_all(slots, SPACE, split_axis=0, concat_axis=0, tiled=True)
    gram, modes = call(
        lambda *refs: final_kernel(3.0 * nodes * NSPACE, *refs),
        [((OWN, TILE), F32), ((3, MODES, nodes), BF16)],
        parts,
        raw,
    )
    return gram.T, jnp.transpose(modes, (2, 0, 1))


def solution(mesh):
    fine = Mesh(mesh.devices.reshape(NX, NZ, NC, NY), ("x", "z", "core", "y"))
    return jax.shard_map(
        local,
        mesh=fine,
        in_specs=(
            P(SPACE, None, "y"),
            P(SPACE, None, None),
            P(SPACE, None),
            P("y", None),
            P(SPACE),
        ),
        out_specs=(P("y", SPACE), P(SPACE, None, None)),
        check_vma=False,
    )
```

time: 448 us -> 90.8 us (0.20)
  waiting for transfers between devices: 210 us -> 15.9 us
  blocking collectives: 130 us -> 27.9 us
  local copies, waits for them, and re-layouts: 60.2 us -> 3.14 us
  starting transfers between devices: 18.3 us -> 36.5 us
  between operations: 14.4 us -> 0.87 us
  matrix products: 8.06 us -> 0 us
  Pallas kernels: 0 us -> 5.05 us
    unnamed x3 -> x0, waiting for transfers between devices: 162 us -> none
    psum x1 -> x0, blocking collectives: 130 us -> none  [local(): lax.psum(jnp.sum(lumped[:, None, None] * raw_modes * raw_modes, axis=(0,...]
    all_to_all x2 -> x0, waiting for transfers between devices: 31.5 us -> none  [the longest x1 16.2 us: local(): lax.all_to_all(snapshots, 'snap', split_axis=0, concat_axis=2, tiled=True)]
    reshape x3, local copies, waits for them, and re-layouts: 31.2 us -> 2.12 us  [the longest x2 1.61 us: local(): mass = mass_blocks.reshape(blocks, BPR, BLOCK, BLOCK).transpose(0, 2, 1, 3)]
    all_to_all x0 -> x1, blocking collectives: none -> 27.9 us  [local(): lax.all_to_all(slots, SPACE, split_axis=0, concat_axis=0, tiled=True)]
    ppermute x2 -> x10, starting transfers between devices: 10.1 us -> 36.5 us  [the longest x8 26.9 us: shift(): return lax.ppermute(value, 'y', [(i, (i + step) % NY) for i in range(NY)])]
    transpose x1 -> x0, local copies, waits for them, and re-layouts: 16.9 us -> none  [local(): jnp.einsum('rcta,rcsb->stab', left_split, right_split, preferred_element_...]
    psum x1 -> x0, waiting for transfers between devices: 16.3 us -> none  [local(): raw_modes = lax.psum(mode_terms, 'snap')]
  transfers between devices with their start and end apart: 6 -> 10, of which waited for: 4 -> 4; matrix products, arithmetic and copies ran while one was open for 13% -> 2% of each run, Pallas kernels for 0% -> 3%
where the time goes in v2:
time: 90.8 us; the launch traced here: 90.4 us
  starting transfers between devices  36.5 us (40%)
  blocking collectives  27.9 us (31%)
  waiting for transfers between devices  15.9 us (18%)
  Pallas kernels  5.05 us (6%)
  local copies, waits for them, and re-layouts  3.14 us (3%)
  other arithmetic  1.1 us (1%)
    all_to_all x1, blocking collectives, local(): lax.all_to_all(slots, SPACE, split_axis=0, concat_axis=0, tiled=True)  27.9 us
    ppermute x8, starting transfers between devices, shift(): return lax.ppermute(value, 'y', [(i, (i + step) % NY) for i in range(NY)])  26.9 us
    ppermute x8, waiting for transfers between devices, shift(): return lax.ppermute(value, 'y', [(i, (i + step) % NY) for i in range(NY)])  15.8 us
    ppermute x1, starting transfers between devices, local(): lax.ppermute(high, SPACE, [(i, i + 1) for i in range(NSPACE - 1)])  7.62 us
    pallas_call x5, Pallas kernels, call(): pl.pallas_call(kernel, out_shape=[jax.ShapeDtypeStruct(*s) for s in outs]...  5.05 us
    ppermute x1, starting transfers between devices, local(): lax.ppermute(low, SPACE, [(i + 1, i) for i in range(NSPACE - 1)])  1.92 us
  transfers between devices with their start and end apart: 10, of which 4 were waited for; matrix products, arithmetic and copies ran while one was open for 2% of the time, Pallas kernels for 3%

profile of v2, /device:TPU:1, one launch (start us, length us, event | category | flops | bytes accessed | tf_op | source)
XLA Modules:
  0.0 90.4 jit_solution(12835105489202175198)
XLA Ops:
  0.6 0.0 copy-start.3
  0.6 1.1 %pad_maximum_fusion.refs_2_ = bf16[1600,128]{1,0:T(8,128)(2,1)S(1)} fusion(bf16[64,128]{1,0:T(8,128)(2,1)} %bitcast.16, bf16[1536,128]{1,0:T(8,128)(2,1)} %bitcast.12), kind=kLoop, calls=%fused_computation.1 | loop fusion | flops 819200 | bytes 819200 | tf_op jit(solution)/shard_map/concatenate | solution.py:150
  1.7 5.9 %collective-permute-start = (bf16[1600,128]{1,0:T(8,128)(2,1)S(1)}, bf16[1600,128]{1,0:T(8,128)(2,1)S(1)}, u32[]{:S(2)}, u32[]{:S(2)}) collective-permute-start(bf16[1600,128]{1,0:T(8,128)(2,1)S(1)} %pad_maximum_fusion.refs_2_), channel_id=1, source_target_pairs={{0,7},{1,0},{2,1},{3,2},{4,3},{5,4},{6,5},{7,6},{8,15},{9,8},{10,9... | collective-permute-start | bytes 1228808 | tf_op jit(solution)/shard_map/ppermute | solution.py:143
  7.7 1.9 %collective-permute-start.1 = (bf16[1600,128]{1,0:T(8,128)(2,1)S(1)}, bf16[1600,128]{1,0:T(8,128)(2,1)S(1)}, u32[]{:S(2)}, u32[]{:S(2)}) collective-permute-start(bf16[1600,128]{1,0:T(8,128)(2,1)S(1)} %pad_maximum_fusion.refs_2_), channel_id=1, source_target_pairs={{0,1},{1,2},{2,3},{3,4},{4,5},{5,6},{6,7},{7,0},{8,9},{9,10},{10,1... | collective-permute-start | bytes 1228808 | tf_op jit(solution)/shard_map/ppermute | solution.py:143
  9.6 0.0 copy-done.3
  9.6 1.0 %reshape.16 = bf16[8,7,64,64]{3,2,0,1:T(8,128)(2,1)S(1)} reshape(bf16[8,7,4096]{2,0,1:T(8,128)(2,1)S(1)} %copy-done.3) | data formatting | bytes 917504 | tf_op jit(solution)/shard_map/reshape | solution.py:153
  10.6 0.6 copy.10
  11.2 0.0 copy-start
  11.2 0.0 copy-start.1
  11.3 0.5 reshape.17.mass
  11.8 0.5 copy-done
  12.2 0.0 copy-done.1
  12.2 1.6 %shard_map.68 = (f32[3,64,384]{2,1,0:T(8,128)S(1)}, f32[8,64,384]{2,1,0:T(8,128)S(1)}, f32[3,64,384]{2,1,0:T(8,128)S(1)}) custom-call(s32[8,7]{1,0:T(8,128)S(1)} %copy-done.1, bf16[8,64,448]{2,1,0:T(8,128)(2,1)S(1)} %reshape.17.mass, bf16[3,512,128]{2,1,0:T(8,128)(2,1)S(1)} %bitcast.13), custom_call_target="tpu_custom_call" | custom-call | tf_op jit(solution)/shard_map/pallas_call | solution.py:131
  13.9 0.0 collective-permute-done.refs_3_
  13.9 5.0 %collective-permute-done.1.refs_4_ = bf16[1600,128]{1,0:T(8,128)(2,1)S(1)} collective-permute-done((bf16[1600,128]{1,0:T(8,128)(2,1)S(1)}, bf16[1600,128]{1,0:T(8,128)(2,1)S(1)}, u32[]{:S(2)}, u32[]{:S(2)}) %collective-permute-start.1) | collective-permute-done | bytes 409632 | tf_op jit(solution)/shard_map/ppermute | solution.py:143
  18.9 3.7 %collective-permute-start.4 = (bf16[1600,128]{1,0:T(8,128)(2,1)S(1)}, bf16[1600,128]{1,0:T(8,128)(2,1)S(1)}, u32[]{:S(2)}, u32[]{:S(2)}) collective-permute-start(bf16[1600,128]{1,0:T(8,128)(2,1)S(1)} %collective-permute-done.refs_3_), channel_id=1, source_target_pairs={{0,7},{1,0},{2,1},{3,2},{4,3},{5,4},{6,5},{7,6},{8,15},{9,8},{10,9... | collective-permute-start | bytes 1228808 | tf_op jit(solution)/shard_map/ppermute | solution.py:143
  22.6 1.9 %collective-permute-start.5 = (bf16[1600,128]{1,0:T(8,128)(2,1)S(1)}, bf16[1600,128]{1,0:T(8,128)(2,1)S(1)}, u32[]{:S(2)}, u32[]{:S(2)}) collective-permute-start(bf16[1600,128]{1,0:T(8,128)(2,1)S(1)} %collective-permute-done.1.refs_4_), channel_id=1, source_target_pairs={{0,1},{1,2},{2,3},{3,4},{4,5},{5,6},{6,7},{7,0},{8,9},{9,10},{10,1... | collective-permute-start | bytes 1228808 | tf_op jit(solution)/shard_map/ppermute | solution.py:143
  24.5 4.9 %collective-permute-done.4.refs_5_ = bf16[1600,128]{1,0:T(8,128)(2,1)S(1)} collective-permute-done((bf16[1600,128]{1,0:T(8,128)(2,1)S(1)}, bf16[1600,128]{1,0:T(8,128)(2,1)S(1)}, u32[]{:S(2)}, u32[]{:S(2)}) %collective-permute-start.4) | collective-permute-done | bytes 409632 | tf_op jit(solution)/shard_map/ppermute | solution.py:143
  29.4 5.3 %collective-permute-start.6 = (bf16[1600,128]{1,0:T(8,128)(2,1)S(1)}, bf16[1600,128]{1,0:T(8,128)(2,1)S(1)}, u32[]{:S(2)}, u32[]{:S(2)}) collective-permute-start(bf16[1600,128]{1,0:T(8,128)(2,1)S(1)} %collective-permute-done.4.refs_5_), channel_id=1, source_target_pairs={{0,7},{1,0},{2,1},{3,2},{4,3},{5,4},{6,5},{7,6},{8,15},{9,8},{10,9... | collective-permute-start | bytes 1228808 | tf_op jit(solution)/shard_map/ppermute | solution.py:143
  34.7 0.0 collective-permute-done.5.refs_6_
  34.8 1.9 %collective-permute-start.7 = (bf16[1600,128]{1,0:T(8,128)(2,1)S(1)}, bf16[1600,128]{1,0:T(8,128)(2,1)S(1)}, u32[]{:S(2)}, u32[]{:S(2)}) collective-permute-start(bf16[1600,128]{1,0:T(8,128)(2,1)S(1)} %collective-permute-done.5.refs_6_), channel_id=1, source_target_pairs={{0,1},{1,2},{2,3},{3,4},{4,5},{5,6},{6,7},{7,0},{8,9},{9,10},{10,1... | collective-permute-start | bytes 1228808 | tf_op jit(solution)/shard_map/ppermute | solution.py:143
  36.7 7.6 %collective-permute-start.2 = (f32[3,64,384]{2,1,0:T(8,128)S(1)}, f32[3,64,384]{2,1,0:T(8,128)S(1)}, u32[]{:S(2)}, u32[]{:S(2)}) collective-permute-start(f32[3,64,384]{2,1,0:T(8,128)S(1)} %get-tuple-element.19), channel_id=1, source_target_pairs={{0,8},{8,16},{16,24},{24,32},{32,40},{40,48},{48,56},{56,64},{64,7... | collective-permute-start | bytes 884744 | tf_op jit(solution)/shard_map/ppermute | solution.py:171
  44.3 1.9 %collective-permute-start.3 = (f32[3,64,384]{2,1,0:T(8,128)S(1)}, f32[3,64,384]{2,1,0:T(8,128)S(1)}, u32[]{:S(2)}, u32[]{:S(2)}) collective-permute-start(f32[3,64,384]{2,1,0:T(8,128)S(1)} %get-tuple-element.20), channel_id=1, source_target_pairs={{8,0},{16,8},{24,16},{32,24},{40,32},{48,40},{56,48},{64,56},{72,6... | collective-permute-start | bytes 884744 | tf_op jit(solution)/shard_map/ppermute | solution.py:172
  46.2 0.0 collective-permute-done.6.refs_4_
  46.3 4.3 %collective-permute-start.8 = (bf16[800,128]{1,0:T(8,128)(2,1)S(1)}, bf16[800,128]{1,0:T(8,128)(2,1)S(1)}, u32[]{:S(2)}, u32[]{:S(2)}) collective-permute-start(bf16[800,128]{1,0:T(8,128)(2,1)S(1)} %slice.8), channel_id=1, source_target_pairs={{0,7},{1,0},{2,1},{3,2},{4,3},{5,4},{6,5},{7,6},{8,15},{9,8},{10,9... | collective-permute-start | bytes 614408 | tf_op jit(solution)/shard_map/ppermute | solution.py:143
  50.6 0.0 collective-permute-done.7.refs_5_
  50.7 1.9 %collective-permute-start.9 = (bf16[800,128]{1,0:T(8,128)(2,1)S(1)}, bf16[800,128]{1,0:T(8,128)(2,1)S(1)}, u32[]{:S(2)}, u32[]{:S(2)}) collective-permute-start(bf16[800,128]{1,0:T(8,128)(2,1)S(1)} %slice.9), channel_id=1, source_target_pairs={{0,1},{1,2},{2,3},{3,4},{4,5},{5,6},{6,7},{7,0},{8,9},{9,10},{10,1... | collective-permute-start | bytes 614408 | tf_op jit(solution)/shard_map/ppermute | solution.py:143
  52.6 0.0 collective-permute-done.2.from_prev
  52.6 0.0 collective-permute-done.3.from_next
  52.6 0.0 copy-start.2
  52.6 0.2 shard_map.69.refs_0_
  52.8 0.5 copy-done.2
  53.3 1.4 %shard_map.70 = (bf16[5,128,128]{2,1,0:T(8,128)(2,1)S(1)}, f32[64,1536]{1,0:T(8,128)S(1)}, f32[1,512]{1,0:T(1,128)S(1)}) custom-call(bf16[1536,256]{1,0:T(8,128)(2,1)S(1)} %shard_map.69.refs_0_, f32[1,512]{1,0:T(1,128)S(1)} %bitcast.14, bf16[1600,128]{1,0:T(8,128)(2,1)S(1)} %pad_maximum_fusion.refs_2_, bf16[1600,128]{1,0:T(8,128)(2,1)S(1)} %collective-permute-done.refs_3_, ...), custom_call_target="tpu_custom_call" | custom-call | tf_op jit(solution)/shard_map/pallas_call | solution.py:131
  54.7 0.4 collective-permute-done.8.refs_6_
  55.1 5.5 %collective-permute-done.9.refs_7_ = bf16[800,128]{1,0:T(8,128)(2,1)S(1)} collective-permute-done((bf16[800,128]{1,0:T(8,128)(2,1)S(1)}, bf16[800,128]{1,0:T(8,128)(2,1)S(1)}, u32[]{:S(2)}, u32[]{:S(2)}) %collective-permute-start.9) | collective-permute-done | bytes 204832 | tf_op jit(solution)/shard_map/ppermute | solution.py:143
  60.6 1.0 %shard_map.71 = (bf16[64,24,128]{2,1,0:T(8,128)(2,1)S(1)}, f32[3,64,512]{2,1,0:T(8,128)S(1)}) custom-call(bf16[1536,256]{1,0:T(8,128)(2,1)S(1)} %shard_map.69.refs_0_, bf16[5,128,128]{2,1,0:T(8,128)(2,1)S(1)} %get-tuple-element.23.refs_1_, f32[64,1536]{1,0:T(8,128)S(1)} %get-tuple-element.24.refs_2_, f32[1,512]{1,0:T(1,128)S(1)} %get-tuple-element.25.refs_3_, ...), custom_call_target="tpu_custom_call" | custom-call | tf_op jit(solution)/shard_map/pallas_call | solution.py:131
  61.6 27.9 %all_to_all.5.refs_0_ = bf16[64,24,128]{2,1,0:T(8,128)(2,1)S(1)} all-to-all(bf16[64,24,128]{2,1,0:T(8,128)(2,1)S(1)} %get-tuple-element.26), channel_id=1, replica_groups=mesh['x'=4,'z'=8,'core'=2,'y'=8] {'x','z','core'}, dimensions={0} | all-to-all | bytes 786432 | tf_op jit(solution)/shard_map/all_to_all | solution.py:204
  89.5 0.9 %shard_map.72 = (f32[16,128]{1,0:T(8,128)}, bf16[3,64,512]{2,1,0:T(8,128)(2,1)}) custom-call(bf16[64,24,128]{2,1,0:T(8,128)(2,1)S(1)} %all_to_all.5.refs_0_, f32[3,64,512]{2,1,0:T(8,128)S(1)} %get-tuple-element.27.refs_1_), custom_call_target="tpu_custom_call" | custom-call | tf_op jit(solution)/shard_map/pallas_call | solution.py:131
  (2 shorter events, 0.0 us)
Async XLA Ops:
  0.6 9.0 %copy-start.3 = (bf16[8,7,4096]{2,0,1:T(8,128)(2,1)S(1)}, bf16[8,7,4096]{2,0,1:T(8,128)(2,1)}, u32[]{:S(2)}) copy-start(bf16[8,7,4096]{2,0,1:T(8,128)(2,1)} %param.6) | copy-start | bytes 1376260
  1.7 12.2 %collective-permute-start = (bf16[1600,128]{1,0:T(8,128)(2,1)S(1)}, bf16[1600,128]{1,0:T(8,128)(2,1)S(1)}, u32[]{:S(2)}, u32[]{:S(2)}) collective-permute-start(bf16[1600,128]{1,0:T(8,128)(2,1)S(1)} %pad_maximum_fusion.refs_2_), channel_id=1, source_target_pairs={{0,7},{1,0},{2,1},{3,2},{4,3},{5,4},{6,5},{7,6},{8,15},{9,8},{10,9... | collective-permute-start | bytes 1228808 | tf_op jit(solution)/shard_map/ppermute | solution.py:143
  7.7 11.2 %collective-permute-start.1 = (bf16[1600,128]{1,0:T(8,128)(2,1)S(1)}, bf16[1600,128]{1,0:T(8,128)(2,1)S(1)}, u32[]{:S(2)}, u32[]{:S(2)}) collective-permute-start(bf16[1600,128]{1,0:T(8,128)(2,1)S(1)} %pad_maximum_fusion.refs_2_), channel_id=1, source_target_pairs={{0,1},{1,2},{2,3},{3,4},{4,5},{5,6},{6,7},{7,0},{8,9},{9,10},{10,1... | collective-permute-start | bytes 1228808 | tf_op jit(solution)/shard_map/ppermute | solution.py:143
  11.2 1.0 %copy-start = (bf16[512,3,128]{2,0,1:T(8,128)(2,1)S(1)}, bf16[512,3,128]{2,0,1:T(8,128)(2,1)}, u32[]{:S(2)}) copy-start(bf16[512,3,128]{2,0,1:T(8,128)(2,1)} %param.5) | copy-start | bytes 1179652
  11.2 1.0 %copy-start.1 = (s32[8,7]{1,0:T(8,128)S(1)}, s32[8,7]{1,0:T(8,128)}, u32[]{:S(2)}) copy-start(s32[8,7]{1,0:T(8,128)} %cols.1) | copy-start | bytes 676
  18.9 10.6 %collective-permute-start.4 = (bf16[1600,128]{1,0:T(8,128)(2,1)S(1)}, bf16[1600,128]{1,0:T(8,128)(2,1)S(1)}, u32[]{:S(2)}, u32[]{:S(2)}) collective-permute-start(bf16[1600,128]{1,0:T(8,128)(2,1)S(1)} %collective-permute-done.refs_3_), channel_id=1, source_target_pairs={{0,7},{1,0},{2,1},{3,2},{4,3},{5,4},{6,5},{7,6},{8,15},{9,8},{10,9... | collective-permute-start | bytes 1228808 | tf_op jit(solution)/shard_map/ppermute | solution.py:143
  22.6 12.2 %collective-permute-start.5 = (bf16[1600,128]{1,0:T(8,128)(2,1)S(1)}, bf16[1600,128]{1,0:T(8,128)(2,1)S(1)}, u32[]{:S(2)}, u32[]{:S(2)}) collective-permute-start(bf16[1600,128]{1,0:T(8,128)(2,1)S(1)} %collective-permute-done.1.refs_4_), channel_id=1, source_target_pairs={{0,1},{1,2},{2,3},{3,4},{4,5},{5,6},{6,7},{7,0},{8,9},{9,10},{10,1... | collective-permute-start | bytes 1228808 | tf_op jit(solution)/shard_map/ppermute | solution.py:143
  29.4 16.8 %collective-permute-start.6 = (bf16[1600,128]{1,0:T(8,128)(2,1)S(1)}, bf16[1600,128]{1,0:T(8,128)(2,1)S(1)}, u32[]{:S(2)}, u32[]{:S(2)}) collective-permute-start(bf16[1600,128]{1,0:T(8,128)(2,1)S(1)} %collective-permute-done.4.refs_5_), channel_id=1, source_target_pairs={{0,7},{1,0},{2,1},{3,2},{4,3},{5,4},{6,5},{7,6},{8,15},{9,8},{10,9... | collective-permute-start | bytes 1228808 | tf_op jit(solution)/shard_map/ppermute | solution.py:143
  34.8 15.9 %collective-permute-start.7 = (bf16[1600,128]{1,0:T(8,128)(2,1)S(1)}, bf16[1600,128]{1,0:T(8,128)(2,1)S(1)}, u32[]{:S(2)}, u32[]{:S(2)}) collective-permute-start(bf16[1600,128]{1,0:T(8,128)(2,1)S(1)} %collective-permute-done.5.refs_6_), channel_id=1, source_target_pairs={{0,1},{1,2},{2,3},{3,4},{4,5},{5,6},{6,7},{7,0},{8,9},{9,10},{10,1... | collective-permute-start | bytes 1228808 | tf_op jit(solution)/shard_map/ppermute | solution.py:143
  36.7 15.9 %collective-permute-start.2 = (f32[3,64,384]{2,1,0:T(8,128)S(1)}, f32[3,64,384]{2,1,0:T(8,128)S(1)}, u32[]{:S(2)}, u32[]{:S(2)}) collective-permute-start(f32[3,64,384]{2,1,0:T(8,128)S(1)} %get-tuple-element.19), channel_id=1, source_target_pairs={{0,8},{8,16},{16,24},{24,32},{32,40},{40,48},{48,56},{56,64},{64,7... | collective-permute-start | bytes 884744 | tf_op jit(solution)/shard_map/ppermute | solution.py:171
  44.3 8.3 %collective-permute-start.3 = (f32[3,64,384]{2,1,0:T(8,128)S(1)}, f32[3,64,384]{2,1,0:T(8,128)S(1)}, u32[]{:S(2)}, u32[]{:S(2)}) collective-permute-start(f32[3,64,384]{2,1,0:T(8,128)S(1)} %get-tuple-element.20), channel_id=1, source_target_pairs={{8,0},{16,8},{24,16},{32,24},{40,32},{48,40},{56,48},{64,56},{72,6... | collective-permute-start | bytes 884744 | tf_op jit(solution)/shard_map/ppermute | solution.py:172
  46.3 8.8 %collective-permute-start.8 = (bf16[800,128]{1,0:T(8,128)(2,1)S(1)}, bf16[800,128]{1,0:T(8,128)(2,1)S(1)}, u32[]{:S(2)}, u32[]{:S(2)}) collective-permute-start(bf16[800,128]{1,0:T(8,128)(2,1)S(1)} %slice.8), channel_id=1, source_target_pairs={{0,7},{1,0},{2,1},{3,2},{4,3},{5,4},{6,5},{7,6},{8,15},{9,8},{10,9... | collective-permute-start | bytes 614408 | tf_op jit(solution)/shard_map/ppermute | solution.py:143
  50.7 9.9 %collective-permute-start.9 = (bf16[800,128]{1,0:T(8,128)(2,1)S(1)}, bf16[800,128]{1,0:T(8,128)(2,1)S(1)}, u32[]{:S(2)}, u32[]{:S(2)}) collective-permute-start(bf16[800,128]{1,0:T(8,128)(2,1)S(1)} %slice.9), channel_id=1, source_target_pairs={{0,1},{1,2},{2,3},{3,4},{4,5},{5,6},{6,7},{7,0},{8,9},{9,10},{10,1... | collective-permute-start | bytes 614408 | tf_op jit(solution)/shard_map/ppermute | solution.py:143
  52.6 0.7 copy-start.2

commit v3 on v2

--- a/solution.py
+++ b/solution.py
@@ -28,7 +28,8 @@
     for b in range(blocks):
         rows = slice(b * BLOCK, (b + 1) * BLOCK)
         right = jnp.concatenate([own[c, rows, :] for c in range(3)], axis=1)
-        terms = lax.dot_general(mass[b], right, ALONG, preferred_element_type=F32)
+        left = jnp.concatenate([mass[j, b] for j in range(BPR)], axis=1)
+        terms = lax.dot_general(left, right, ALONG, preferred_element_type=F32)
         for j in range(BPR):
             place = cols[b, j] - first
             acc[place] += terms[j * BLOCK : (j + 1) * BLOCK]
@@ -61,7 +62,7 @@
     raw = lax.dot_general(
         tile[rows:, :], snaps, (((1,), (1,)), ((), ())), preferred_element_type=F32
     )
-    return (both[:, :TILE] + both[:, TILE:]).astype(BF16), raw
+    return both[:, :TILE] + both[:, TILE:], raw
 
 
 def early_kernel(count, dual, lumped, *refs):
@@ -76,7 +77,7 @@
             raw_out[...] = raw
 
 
-def late_kernel(near, dual, early, raw_in, lumped, forward, backward, half_a, half_b, slots, raw_out):
+def late_kernel(near, dual, early, raw_in, lumped, forward, backward, half_a, half_b, mine, other, raw_out):
     me = lax.axis_index("y")
     nodes = raw_out.shape[2]
     far = jnp.concatenate([half_a[...], half_b[...]], axis=0)
@@ -94,23 +95,37 @@
     k = lax.broadcasted_iota(jnp.int32, (MODES, TILE), 0)
     lane = lax.broadcasted_iota(jnp.int32, (MODES, TILE), 1)
     row = jnp.sum(jnp.where(lane % MODES == k, column, 0.0), axis=0, keepdims=True)
+    norm = jnp.broadcast_to(row, (SLOT - OWN, TILE))
+    steps = near + [3, NY - 3, 4]
+    first = lax.axis_index("core") == 0
+    for i, step in enumerate(steps):
+        source = lax.rem(me + step, NY)
+        part = early[i] if i < len(near) else products[i - len(near)]
+        for o in range(TILE // OWN // NC):
+            one = part[2 * o * OWN : (2 * o + 1) * OWN]
+            two = part[(2 * o + 1) * OWN : (2 * o + 2) * OWN]
+            place = source * (TILE // OWN // NC) + o
+            mine[place, :OWN, :] = jnp.where(first, one, two)
+            other[place, :OWN, :] = jnp.where(first, two, one)
+    for i in range(NSPACE // NC):
+        mine[i, OWN:, :] = norm
+        other[i, OWN:, :] = norm
+
+
+def pair_kernel(mine, other, out):
+    lane = lax.broadcasted_iota(jnp.int32, (SLOT - OWN, TILE), 1)
+    row = mine[0, OWN:, :] + other[0, OWN:, :]
     high = row.astype(BF16)
     rest = (row - high.astype(F32)).astype(BF16)
-    lane = lax.broadcasted_iota(jnp.int32, (1, TILE), 1)
-    both = jnp.where(lane < MODES, high.astype(F32), rest.astype(F32))
-    norm = jnp.broadcast_to(both, (SLOT - OWN, TILE)).astype(BF16)
-    steps = near + [3, NY - 3, 4]
-    for i, step in enumerate(steps):
-        source = lax.rem(me + step, NY)
-        for o in range(TILE // OWN):
-            rows = slice(o * OWN, (o + 1) * OWN)
-            part = early[i, rows, :] if i < len(near) else products[i - len(near)][rows]
-            slots[source * (TILE // OWN) + o] = jnp.concatenate([part, norm], axis=0)
+    norm = jnp.where(lane < MODES, high.astype(F32), rest.astype(F32))
+    for i in range(NSPACE // NC):
+        total = mine[i, :OWN, :] + other[i, :OWN, :]
+        out[i] = jnp.concatenate([total, norm], axis=0).astype(BF16)
 
 
 def final_kernel(count, parts, raw, gram, modes):
     total = parts[0].astype(F32)
-    for i in range(1, NSPACE):
+    for i in range(1, NSPACE // NC):
         total = total + parts[i].astype(F32)
     gram[...] = total[:OWN] * count ** (-0.5)
     row = total[OWN : OWN + 1]
@@ -148,10 +163,9 @@
     blocks = nodes // BLOCK
     own = jnp.transpose(snapshots, (1, 0, 2))
     tile = jnp.concatenate([own.reshape(3 * nodes, TILE), coefficients.T], axis=0)
-    rows = tile.shape[0]
-
-    mass = mass_blocks.reshape(blocks, BPR, BLOCK, BLOCK).transpose(0, 2, 1, 3)
-    mass = mass.reshape(blocks, BLOCK, BPR * BLOCK)
+    cut = tile.shape[0] // 2
+
+    mass = mass_blocks.reshape(blocks, BPR, BLOCK, BLOCK).transpose(1, 0, 2, 3)
     up, down = [tile], [tile]
     up.append(shift(tile, -1))
     down.append(shift(tile, 1))
@@ -165,22 +179,23 @@
         scratch=[pltpu.VMEM((blocks + 2 * REACH, BLOCK, 3 * TILE), F32)],
         smem=1,
     )
-    second, third, low, high = lax.optimization_barrier((up[1], down[1], low, high))
-    up.append(shift(second, -1))
-    down.append(shift(third, 1))
+    first, low, high = lax.optimization_barrier((up[1], low, high))
+    up.append(shift(first, -1))
+    down.append(shift(down[1], 1))
+    low, high, down[1] = lax.optimization_barrier((low, high, down[1]))
     from_prev = lax.ppermute(high, SPACE, [(i, i + 1) for i in range(NSPACE - 1)])
     from_next = lax.ppermute(low, SPACE, [(i + 1, i) for i in range(NSPACE - 1)])
-    dual = call(join_kernel, ((3 * nodes, 2 * TILE), BF16), mid, from_prev, from_next)
-
     up.append(shift(up[2], -1))
     down.append(shift(down[2], 1))
-    half_a = shift(up[3][: rows // 2], -1)
-    half_b = shift(down[3][rows // 2 :], 1)
+    dual = call(join_kernel, ((3 * nodes, 2 * TILE), BF16), mid, from_prev, from_next)
+
+    half_a = shift(up[3][:cut], -1)
+    half_b = shift(down[3][cut:], 1)
 
     near = [0, 1, NY - 1, 2, NY - 2]
     early, raw, weight = call(
         lambda *refs: early_kernel(len(near), *refs),
-        [((len(near), TILE, TILE), BF16), ((MODES, 3 * nodes), F32), ((1, nodes), F32)],
+        [((len(near), TILE, TILE), F32), ((MODES, 3 * nodes), F32), ((1, nodes), F32)],
         dual,
         lumped.reshape(1, nodes),
         tile,
@@ -189,9 +204,10 @@
         up[2],
         down[2],
     )
-    slots, raw = call(
+    slot = ((NSPACE // NC, SLOT, TILE), F32)
+    mine, other, raw = call(
         lambda *refs: late_kernel(near, *refs),
-        [((NSPACE, SLOT, TILE), BF16), ((3, MODES, nodes), F32)],
+        [slot, slot, ((3, MODES, nodes), F32)],
         dual,
         early,
         raw,
@@ -201,7 +217,9 @@
         half_a,
         half_b,
     )
-    parts = lax.all_to_all(slots, SPACE, split_axis=0, concat_axis=0, tiled=True)
+    other = lax.ppermute(other, "core", [(0, 1), (1, 0)])
+    slots = call(pair_kernel, ((NSPACE // NC, SLOT, TILE), BF16), mine, other)
+    parts = lax.all_to_all(slots, ("x", "z"), split_axis=0, concat_axis=0, tiled=True)
     gram, modes = call(
         lambda *refs: final_kernel(3.0 * nodes * NSPACE, *refs),
         [((OWN, TILE), F32), ((3, MODES, nodes), BF16)],

time: 90.8 us -> 87.5 us (0.964)
  starting transfers between devices: 36.5 us -> 43.6 us
  waiting for transfers between devices: 15.9 us -> 9.99 us
  blocking collectives: 27.9 us -> 24.1 us
  local copies, waits for them, and re-layouts: 3.14 us -> 1.54 us
    ppermute x8, waiting for transfers between devices: 15.8 us -> 8.29 us  [shift(): return lax.ppermute(value, 'y', [(i, (i + step) % NY) for i in range(NY)])]
    all_to_all x1, blocking collectives: 27.9 us -> 24.1 us  [local(): lax.all_to_all(slots, ('x', 'z'), split_axis=0, concat_axis=0, tiled=True)]
    ppermute x8, starting transfers between devices: 26.9 us -> 29.6 us  [shift(): return lax.ppermute(value, 'y', [(i, (i + step) % NY) for i in range(NY)])]
    ppermute x1, starting transfers between devices: 7.62 us -> 10.2 us  [local(): lax.ppermute(high, SPACE, [(i, i + 1) for i in range(NSPACE - 1)])]
    ppermute x0 -> x1, starting transfers between devices: none -> 1.92 us  [local(): other = lax.ppermute(other, 'core', [(0, 1), (1, 0)])]
    ppermute x0 -> x1, waiting for transfers between devices: none -> 1.69 us  [local(): other = lax.ppermute(other, 'core', [(0, 1), (1, 0)])]
    reshape x3 -> x1, local copies, waits for them, and re-layouts: 2.12 us -> 0.99 us  [local(): mass = mass_blocks.reshape(blocks, BPR, BLOCK, BLOCK).transpose(1, 0, 2, 3)]
    pallas_call x5 -> x6, Pallas kernels: 5.05 us -> 5.27 us  [call(): pl.pallas_call(kernel, out_shape=[jax.ShapeDtypeStruct(*s) for s in outs]...]
  transfers between devices with their start and end apart: 10 -> 11, of which waited for: 4 -> 4; matrix products, arithmetic and copies ran while one was open for 2% -> 1% of each run, Pallas kernels for 3% -> 4%
where the time goes in v3:
time: 87.5 us; the launch traced here: 86.5 us
  starting transfers between devices  43.6 us (50%)
  blocking collectives  24.1 us (28%)
  waiting for transfers between devices  9.99 us (11%)
  Pallas kernels  5.27 us (6%)
  local copies, waits for them, and re-layouts  1.54 us (2%)
  other arithmetic  1.1 us (1%)
  between operations  0.89 us (1%)
    ppermute x8, starting transfers between devices, shift(): return lax.ppermute(value, 'y', [(i, (i + step) % NY) for i in range(NY)])  29.6 us
    all_to_all x1, blocking collectives, local(): lax.all_to_all(slots, ('x', 'z'), split_axis=0, concat_axis=0, tiled=True)  24.1 us
    ppermute x1, starting transfers between devices, local(): lax.ppermute(high, SPACE, [(i, i + 1) for i in range(NSPACE - 1)])  10.2 us
    ppermute x8, waiting for transfers between devices, shift(): return lax.ppermute(value, 'y', [(i, (i + step) % NY) for i in range(NY)])  8.29 us
    pallas_call x6, Pallas kernels, call(): pl.pallas_call(kernel, out_shape=[jax.ShapeDtypeStruct(*s) for s in outs]...  5.27 us
    ppermute x1, starting transfers between devices, local(): lax.ppermute(low, SPACE, [(i + 1, i) for i in range(NSPACE - 1)])  1.92 us
    ppermute x1, starting transfers between devices, local(): other = lax.ppermute(other, 'core', [(0, 1), (1, 0)])  1.92 us
  transfers between devices with their start and end apart: 11, of which 4 were waited for; matrix products, arithmetic and copies ran while one was open for 1% of the time, Pallas kernels for 4%

profile of v3, /device:TPU:1, one launch (start us, length us, event | category | flops | bytes accessed | tf_op | source)
XLA Modules:
  0.0 86.5 jit_solution(9045874299192530647)
XLA Ops:
  0.6 0.0 copy-start.3
  0.6 1.1 %pad_maximum_fusion.refs_2_ = bf16[1600,128]{1,0:T(8,128)(2,1)S(1)} fusion(bf16[64,128]{1,0:T(8,128)(2,1)} %bitcast.14, bf16[1536,128]{1,0:T(8,128)(2,1)} %bitcast.11), kind=kLoop, calls=%fused_computation | loop fusion | flops 819200 | bytes 819200 | tf_op jit(solution)/shard_map/concatenate | solution.py:165
  1.7 0.0 copy-start
  1.8 6.1 %collective-permute-start = (bf16[1600,128]{1,0:T(8,128)(2,1)S(1)}, bf16[1600,128]{1,0:T(8,128)(2,1)S(1)}, u32[]{:S(2)}, u32[]{:S(2)}) collective-permute-start(bf16[1600,128]{1,0:T(8,128)(2,1)S(1)} %pad_maximum_fusion.refs_2_), channel_id=1, source_target_pairs={{0,7},{1,0},{2,1},{3,2},{4,3},{5,4},{6,5},{7,6},{8,15},{9,8},{10,9... | collective-permute-start | bytes 1228808 | tf_op jit(solution)/shard_map/ppermute | solution.py:158
  7.8 1.9 %collective-permute-start.1 = (bf16[1600,128]{1,0:T(8,128)(2,1)S(1)}, bf16[1600,128]{1,0:T(8,128)(2,1)S(1)}, u32[]{:S(2)}, u32[]{:S(2)}) collective-permute-start(bf16[1600,128]{1,0:T(8,128)(2,1)S(1)} %pad_maximum_fusion.refs_2_), channel_id=1, source_target_pairs={{0,1},{1,2},{2,3},{3,4},{4,5},{5,6},{6,7},{7,0},{8,9},{9,10},{10,1... | collective-permute-start | bytes 1228808 | tf_op jit(solution)/shard_map/ppermute | solution.py:158
  9.7 0.0 copy-done.3
  9.8 0.0 copy-start.1
  9.8 1.0 %reshape.13 = bf16[8,7,64,64]{3,2,0,1:T(8,128)(2,1)S(1)} reshape(bf16[8,7,4096]{2,0,1:T(8,128)(2,1)S(1)} %copy-done.3) | data formatting | bytes 917504 | tf_op jit(solution)/shard_map/reshape | solution.py:168
  10.8 0.0 copy-done
  10.8 0.0 copy-done.1
  10.8 1.8 %shard_map.68 = (f32[3,64,384]{2,1,0:T(8,128)S(1)}, f32[8,64,384]{2,1,0:T(8,128)S(1)}, f32[3,64,384]{2,1,0:T(8,128)S(1)}) custom-call(s32[8,7]{1,0:T(8,128)S(1)} %copy-done.1, bf16[7,8,64,64]{3,2,1,0:T(8,128)(2,1)S(1)} %bitcast.10, bf16[3,512,128]{2,1,0:T(8,128)(2,1)S(1)} %bitcast.12), custom_call_target="tpu_custom_call" | custom-call | tf_op jit(solution)/shard_map/pallas_call | solution.py:146
  12.6 1.3 %collective-permute-done.refs_3_ = bf16[1600,128]{1,0:T(8,128)(2,1)S(1)} collective-permute-done((bf16[1600,128]{1,0:T(8,128)(2,1)S(1)}, bf16[1600,128]{1,0:T(8,128)(2,1)S(1)}, u32[]{:S(2)}, u32[]{:S(2)}) %collective-permute-start) | collective-permute-done | bytes 409632 | tf_op jit(solution)/shard_map/ppermute | solution.py:158
  14.0 5.3 %collective-permute-start.4 = (bf16[1600,128]{1,0:T(8,128)(2,1)S(1)}, bf16[1600,128]{1,0:T(8,128)(2,1)S(1)}, u32[]{:S(2)}, u32[]{:S(2)}) collective-permute-start(bf16[1600,128]{1,0:T(8,128)(2,1)S(1)} %collective-permute-done.refs_3_), channel_id=1, source_target_pairs={{0,7},{1,0},{2,1},{3,2},{4,3},{5,4},{6,5},{7,6},{8,15},{9,8},{10,9... | collective-permute-start | bytes 1228808 | tf_op jit(solution)/shard_map/ppermute | solution.py:158
  19.3 0.0 collective-permute-done.1.refs_4_
  19.3 1.9 %collective-permute-start.5 = (bf16[1600,128]{1,0:T(8,128)(2,1)S(1)}, bf16[1600,128]{1,0:T(8,128)(2,1)S(1)}, u32[]{:S(2)}, u32[]{:S(2)}) collective-permute-start(bf16[1600,128]{1,0:T(8,128)(2,1)S(1)} %collective-permute-done.1.refs_4_), channel_id=1, source_target_pairs={{0,1},{1,2},{2,3},{3,4},{4,5},{5,6},{6,7},{7,0},{8,9},{9,10},{10,1... | collective-permute-start | bytes 1228808 | tf_op jit(solution)/shard_map/ppermute | solution.py:158
  21.2 3.3 %collective-permute-done.4.refs_5_ = bf16[1600,128]{1,0:T(8,128)(2,1)S(1)} collective-permute-done((bf16[1600,128]{1,0:T(8,128)(2,1)S(1)}, bf16[1600,128]{1,0:T(8,128)(2,1)S(1)}, u32[]{:S(2)}, u32[]{:S(2)}) %collective-permute-start.4) | collective-permute-done | bytes 409632 | tf_op jit(solution)/shard_map/ppermute | solution.py:158
  24.5 5.7 %collective-permute-start.6 = (bf16[1600,128]{1,0:T(8,128)(2,1)S(1)}, bf16[1600,128]{1,0:T(8,128)(2,1)S(1)}, u32[]{:S(2)}, u32[]{:S(2)}) collective-permute-start(bf16[1600,128]{1,0:T(8,128)(2,1)S(1)} %collective-permute-done.4.refs_5_), channel_id=1, source_target_pairs={{0,7},{1,0},{2,1},{3,2},{4,3},{5,4},{6,5},{7,6},{8,15},{9,8},{10,9... | collective-permute-start | bytes 1228808 | tf_op jit(solution)/shard_map/ppermute | solution.py:158
  30.2 0.0 collective-permute-done.5.refs_6_
  30.2 1.9 %collective-permute-start.7 = (bf16[1600,128]{1,0:T(8,128)(2,1)S(1)}, bf16[1600,128]{1,0:T(8,128)(2,1)S(1)}, u32[]{:S(2)}, u32[]{:S(2)}) collective-permute-start(bf16[1600,128]{1,0:T(8,128)(2,1)S(1)} %collective-permute-done.5.refs_6_), channel_id=1, source_target_pairs={{0,1},{1,2},{2,3},{3,4},{4,5},{5,6},{6,7},{7,0},{8,9},{9,10},{10,1... | collective-permute-start | bytes 1228808 | tf_op jit(solution)/shard_map/ppermute | solution.py:158
  32.1 10.2 %collective-permute-start.2 = (f32[3,64,384]{2,1,0:T(8,128)S(1)}, f32[3,64,384]{2,1,0:T(8,128)S(1)}, u32[]{:S(2)}, u32[]{:S(2)}) collective-permute-start(f32[3,64,384]{2,1,0:T(8,128)S(1)} %get-tuple-element.24), channel_id=1, source_target_pairs={{0,8},{8,16},{16,24},{24,32},{32,40},{40,48},{48,56},{56,64},{64,7... | collective-permute-start | bytes 884744 | tf_op jit(solution)/shard_map/ppermute | solution.py:186
  42.3 1.9 %collective-permute-start.3 = (f32[3,64,384]{2,1,0:T(8,128)S(1)}, f32[3,64,384]{2,1,0:T(8,128)S(1)}, u32[]{:S(2)}, u32[]{:S(2)}) collective-permute-start(f32[3,64,384]{2,1,0:T(8,128)S(1)} %get-tuple-element.25), channel_id=1, source_target_pairs={{8,0},{16,8},{24,16},{32,24},{40,32},{48,40},{56,48},{64,56},{72,6... | collective-permute-start | bytes 884744 | tf_op jit(solution)/shard_map/ppermute | solution.py:187
  44.3 0.0 collective-permute-done.6.refs_4_
  44.3 4.9 %collective-permute-start.8 = (bf16[800,128]{1,0:T(8,128)(2,1)S(1)}, bf16[800,128]{1,0:T(8,128)(2,1)S(1)}, u32[]{:S(2)}, u32[]{:S(2)}) collective-permute-start(bf16[800,128]{1,0:T(8,128)(2,1)S(1)} %slice.8), channel_id=1, source_target_pairs={{0,7},{1,0},{2,1},{3,2},{4,3},{5,4},{6,5},{7,6},{8,15},{9,8},{10,9... | collective-permute-start | bytes 614408 | tf_op jit(solution)/shard_map/ppermute | solution.py:158
  49.2 0.0 collective-permute-done.7.refs_5_
  49.2 1.9 %collective-permute-start.9 = (bf16[800,128]{1,0:T(8,128)(2,1)S(1)}, bf16[800,128]{1,0:T(8,128)(2,1)S(1)}, u32[]{:S(2)}, u32[]{:S(2)}) collective-permute-start(bf16[800,128]{1,0:T(8,128)(2,1)S(1)} %slice.9), channel_id=1, source_target_pairs={{0,1},{1,2},{2,3},{3,4},{4,5},{5,6},{6,7},{7,0},{8,9},{9,10},{10,1... | collective-permute-start | bytes 614408 | tf_op jit(solution)/shard_map/ppermute | solution.py:158
  51.1 0.0 collective-permute-done.2.from_prev
  51.1 0.0 collective-permute-done.3.from_next
  51.1 0.0 copy-start.2
  51.1 0.2 shard_map.69.refs_0_
  51.3 0.5 copy-done.2
  51.8 1.4 %shard_map.70 = (f32[5,128,128]{2,1,0:T(8,128)S(1)}, f32[64,1536]{1,0:T(8,128)S(1)}, f32[1,512]{1,0:T(1,128)S(1)}) custom-call(bf16[1536,256]{1,0:T(8,128)(2,1)S(1)} %shard_map.69.refs_0_, f32[1,512]{1,0:T(1,128)S(1)} %bitcast.13, bf16[1600,128]{1,0:T(8,128)(2,1)S(1)} %pad_maximum_fusion.refs_2_, bf16[1600,128]{1,0:T(8,128)(2,1)S(1)} %collective-permute-done.refs_3_, ...), custom_call_target="tpu_custom_call" | custom-call | tf_op jit(solution)/shard_map/pallas_call | solution.py:146
  53.2 0.0 collective-permute-done.8.refs_6_
  53.2 3.7 %collective-permute-done.9.refs_7_ = bf16[800,128]{1,0:T(8,128)(2,1)S(1)} collective-permute-done((bf16[800,128]{1,0:T(8,128)(2,1)S(1)}, bf16[800,128]{1,0:T(8,128)(2,1)S(1)}, u32[]{:S(2)}, u32[]{:S(2)}) %collective-permute-start.9) | collective-permute-done | bytes 204832 | tf_op jit(solution)/shard_map/ppermute | solution.py:158
  56.9 0.9 %shard_map.71 = (f32[32,24,128]{2,1,0:T(8,128)S(1)}, f32[32,24,128]{2,1,0:T(8,128)S(1)}, f32[3,64,512]{2,1,0:T(8,128)S(1)}) custom-call(bf16[1536,256]{1,0:T(8,128)(2,1)S(1)} %shard_map.69.refs_0_, f32[5,128,128]{2,1,0:T(8,128)S(1)} %get-tuple-element.28.refs_1_, f32[64,1536]{1,0:T(8,128)S(1)} %get-tuple-element.29.refs_2_, ...), custom_call_target="tpu_custom_call" | custom-call | tf_op jit(solution)/shard_map/pallas_call | solution.py:146
  57.9 1.9 %collective-permute-start.10 = (f32[32,24,128]{2,1,0:T(8,128)S(1)}, f32[32,24,128]{2,1,0:T(8,128)S(1)}, u32[]{:S(2)}, u32[]{:S(2)}) collective-permute-start(f32[32,24,128]{2,1,0:T(8,128)S(1)} %get-tuple-element.32), channel_id=1, source_target_pairs={{0,8},{8,0},{1,9},{9,1},{2,10},{10,2},{3,11},{11,3},{4,12},{12,4},... | collective-permute-start | bytes 1179656 | tf_op jit(solution)/shard_map/ppermute | solution.py:220
  59.8 1.7 %collective-permute-done.10.other = f32[32,24,128]{2,1,0:T(8,128)S(1)} collective-permute-done((f32[32,24,128]{2,1,0:T(8,128)S(1)}, f32[32,24,128]{2,1,0:T(8,128)S(1)}, u32[]{:S(2)}, u32[]{:S(2)}) %collective-permute-start.10) | collective-permute-done | bytes 393248 | tf_op jit(solution)/shard_map/ppermute | solution.py:220
  61.5 24.1 %all_to_all.5.refs_0_ = bf16[32,24,128]{2,1,0:T(8,128)(2,1)S(1)} all-to-all(bf16[32,24,128]{2,1,0:T(8,128)(2,1)S(1)} %shard_map.72), channel_id=1, replica_groups=mesh['x'=4,'z'=8,'core'=2,'y'=8] {'x','z'}, dimensions={0} | all-to-all | bytes 393216 | tf_op jit(solution)/shard_map/all_to_all | solution.py:222
  85.6 0.9 %shard_map.73 = (f32[16,128]{1,0:T(8,128)}, bf16[3,64,512]{2,1,0:T(8,128)(2,1)}) custom-call(bf16[32,24,128]{2,1,0:T(8,128)(2,1)S(1)} %all_to_all.5.refs_0_, f32[3,64,512]{2,1,0:T(8,128)S(1)} %get-tuple-element.33.refs_1_), custom_call_target="tpu_custom_call" | custom-call | tf_op jit(solution)/shard_map/pallas_call | solution.py:146
  (3 shorter events, 0.1 us)
Async XLA Ops:
  0.6 9.1 %copy-start.3 = (bf16[8,7,4096]{2,0,1:T(8,128)(2,1)S(1)}, bf16[8,7,4096]{2,0,1:T(8,128)(2,1)}, u32[]{:S(2)}) copy-start(bf16[8,7,4096]{2,0,1:T(8,128)(2,1)} %param.6) | copy-start | bytes 1376260
  1.7 9.0 %copy-start = (bf16[512,3,128]{2,0,1:T(8,128)(2,1)S(1)}, bf16[512,3,128]{2,0,1:T(8,128)(2,1)}, u32[]{:S(2)}) copy-start(bf16[512,3,128]{2,0,1:T(8,128)(2,1)} %param.5) | copy-start | bytes 1179652
  1.8 12.2 %collective-permute-start = (bf16[1600,128]{1,0:T(8,128)(2,1)S(1)}, bf16[1600,128]{1,0:T(8,128)(2,1)S(1)}, u32[]{:S(2)}, u32[]{:S(2)}) collective-permute-start(bf16[1600,128]{1,0:T(8,128)(2,1)S(1)} %pad_maximum_fusion.refs_2_), channel_id=1, source_target_pairs={{0,7},{1,0},{2,1},{3,2},{4,3},{5,4},{6,5},{7,6},{8,15},{9,8},{10,9... | collective-permute-start | bytes 1228808 | tf_op jit(solution)/shard_map/ppermute | solution.py:158
  7.8 11.5 %collective-permute-start.1 = (bf16[1600,128]{1,0:T(8,128)(2,1)S(1)}, bf16[1600,128]{1,0:T(8,128)(2,1)S(1)}, u32[]{:S(2)}, u32[]{:S(2)}) collective-permute-start(bf16[1600,128]{1,0:T(8,128)(2,1)S(1)} %pad_maximum_fusion.refs_2_), channel_id=1, source_target_pairs={{0,1},{1,2},{2,3},{3,4},{4,5},{5,6},{6,7},{7,0},{8,9},{9,10},{10,1... | collective-permute-start | bytes 1228808 | tf_op jit(solution)/shard_map/ppermute | solution.py:158
  9.8 1.0 %copy-start.1 = (s32[8,7]{1,0:T(8,128)S(1)}, s32[8,7]{1,0:T(8,128)}, u32[]{:S(2)}) copy-start(s32[8,7]{1,0:T(8,128)} %cols.1) | copy-start | bytes 676
  14.0 10.5 %collective-permute-start.4 = (bf16[1600,128]{1,0:T(8,128)(2,1)S(1)}, bf16[1600,128]{1,0:T(8,128)(2,1)S(1)}, u32[]{:S(2)}, u32[]{:S(2)}) collective-permute-start(bf16[1600,128]{1,0:T(8,128)(2,1)S(1)} %collective-permute-done.refs_3_), channel_id=1, source_target_pairs={{0,7},{1,0},{2,1},{3,2},{4,3},{5,4},{6,5},{7,6},{8,15},{9,8},{10,9... | collective-permute-start | bytes 1228808 | tf_op jit(solution)/shard_map/ppermute | solution.py:158
  19.3 10.9 %collective-permute-start.5 = (bf16[1600,128]{1,0:T(8,128)(2,1)S(1)}, bf16[1600,128]{1,0:T(8,128)(2,1)S(1)}, u32[]{:S(2)}, u32[]{:S(2)}) collective-permute-start(bf16[1600,128]{1,0:T(8,128)(2,1)S(1)} %collective-permute-done.1.refs_4_), channel_id=1, source_target_pairs={{0,1},{1,2},{2,3},{3,4},{4,5},{5,6},{6,7},{7,0},{8,9},{9,10},{10,1... | collective-permute-start | bytes 1228808 | tf_op jit(solution)/shard_map/ppermute | solution.py:158
  24.5 19.8 %collective-permute-start.6 = (bf16[1600,128]{1,0:T(8,128)(2,1)S(1)}, bf16[1600,128]{1,0:T(8,128)(2,1)S(1)}, u32[]{:S(2)}, u32[]{:S(2)}) collective-permute-start(bf16[1600,128]{1,0:T(8,128)(2,1)S(1)} %collective-permute-done.4.refs_5_), channel_id=1, source_target_pairs={{0,7},{1,0},{2,1},{3,2},{4,3},{5,4},{6,5},{7,6},{8,15},{9,8},{10,9... | collective-permute-start | bytes 1228808 | tf_op jit(solution)/shard_map/ppermute | solution.py:158
  30.2 18.9 %collective-permute-start.7 = (bf16[1600,128]{1,0:T(8,128)(2,1)S(1)}, bf16[1600,128]{1,0:T(8,128)(2,1)S(1)}, u32[]{:S(2)}, u32[]{:S(2)}) collective-permute-start(bf16[1600,128]{1,0:T(8,128)(2,1)S(1)} %collective-permute-done.5.refs_6_), channel_id=1, source_target_pairs={{0,1},{1,2},{2,3},{3,4},{4,5},{5,6},{6,7},{7,0},{8,9},{9,10},{10,1... | collective-permute-start | bytes 1228808 | tf_op jit(solution)/shard_map/ppermute | solution.py:158
  32.1 19.0 %collective-permute-start.2 = (f32[3,64,384]{2,1,0:T(8,128)S(1)}, f32[3,64,384]{2,1,0:T(8,128)S(1)}, u32[]{:S(2)}, u32[]{:S(2)}) collective-permute-start(f32[3,64,384]{2,1,0:T(8,128)S(1)} %get-tuple-element.24), channel_id=1, source_target_pairs={{0,8},{8,16},{16,24},{24,32},{32,40},{40,48},{48,56},{56,64},{64,7... | collective-permute-start | bytes 884744 | tf_op jit(solution)/shard_map/ppermute | solution.py:186
  42.3 8.8 %collective-permute-start.3 = (f32[3,64,384]{2,1,0:T(8,128)S(1)}, f32[3,64,384]{2,1,0:T(8,128)S(1)}, u32[]{:S(2)}, u32[]{:S(2)}) collective-permute-start(f32[3,64,384]{2,1,0:T(8,128)S(1)} %get-tuple-element.25), channel_id=1, source_target_pairs={{8,0},{16,8},{24,16},{32,24},{40,32},{48,40},{56,48},{64,56},{72,6... | collective-permute-start | bytes 884744 | tf_op jit(solution)/shard_map/ppermute | solution.py:187
  44.3 8.9 %collective-permute-start.8 = (bf16[800,128]{1,0:T(8,128)(2,1)S(1)}, bf16[800,128]{1,0:T(8,128)(2,1)S(1)}, u32[]{:S(2)}, u32[]{:S(2)}) collective-permute-start(bf16[800,128]{1,0:T(8,128)(2,1)S(1)} %slice.8), channel_id=1, source_target_pairs={{0,7},{1,0},{2,1},{3,2},{4,3},{5,4},{6,5},{7,6},{8,15},{9,8},{10,9... | collective-permute-start | bytes 614408 | tf_op jit(solution)/shard_map/ppermute | solution.py:158
  49.2 7.7 %collective-permute-start.9 = (bf16[800,128]{1,0:T(8,128)(2,1)S(1)}, bf16[800,128]{1,0:T(8,128)(2,1)S(1)}, u32[]{:S(2)}, u32[]{:S(2)}) collective-permute-start(bf16[800,128]{1,0:T(8,128)(2,1)S(1)} %slice.9), channel_id=1, source_target_pairs={{0,1},{1,2},{2,3},{3,4},{4,5},{5,6},{6,7},{7,0},{8,9},{9,10},{10,1... | collective-permute-start | bytes 614408 | tf_op jit(solution)/shard_map/ppermute | solution.py:158
  51.1 0.7 copy-start.2
  57.9 3.6 %collective-permute-start.10 = (f32[32,24,128]{2,1,0:T(8,128)S(1)}, f32[32,24,128]{2,1,0:T(8,128)S(1)}, u32[]{:S(2)}, u32[]{:S(2)}) collective-permute-start(f32[32,24,128]{2,1,0:T(8,128)S(1)} %get-tuple-element.32), channel_id=1, source_target_pairs={{0,8},{8,0},{1,9},{9,1},{2,10},{10,2},{3,11},{11,3},{4,12},{12,4},... | collective-permute-start | bytes 1179656 | tf_op jit(solution)/shard_map/ppermute | solution.py:220

commit v4 on v3

--- a/solution.py
+++ b/solution.py
@@ -20,7 +20,8 @@
 ALONG = (((0,), (0,)), ((), ()))
 
 
-def dual_kernel(cols, mass, own, low, mid, high, acc):
+def dual_kernel(cols, mass, own, lumped, low, mid, high, weight, acc):
+    weight[...] = lumped[...]
     blocks = own.shape[1] // BLOCK
     index = (lax.axis_index("x") * NZ + lax.axis_index("z")) * NC + lax.axis_index("core")
     first = index * blocks - REACH
@@ -55,38 +56,39 @@
             out[rows, TILE:] = rest[:, lanes]
 
 
-def tile_products(tile, dual):
-    rows = dual.shape[0]
-    snaps = tile[:rows, :]
-    both = lax.dot_general(snaps, dual, ALONG, preferred_element_type=F32)
-    raw = lax.dot_general(
-        tile[rows:, :], snaps, (((1,), (1,)), ((), ())), preferred_element_type=F32
-    )
-    return both[:, :TILE] + both[:, TILE:], raw
-
-
-def early_kernel(count, dual, lumped, *refs):
-    tiles, gram, raw_out, lumped_out = refs[:count], refs[count], refs[count + 1], refs[count + 2]
-    lumped_out[...] = lumped[...]
+def gram_product(tile, dual):
+    both = lax.dot_general(tile[: dual.shape[0], :], dual, ALONG, preferred_element_type=F32)
+    return both[:, :TILE] + both[:, TILE:]
+
+
+def raw_product(tile):
+    rows = tile.shape[0] - MODES
+    return lax.dot_general(
+        tile[rows:, :], tile[:rows, :], (((1,), (1,)), ((), ())), preferred_element_type=F32
+    )
+
+
+def first_kernel(own, one, two, raw_out):
+    raw_out[...] = raw_product(own[...]) + raw_product(one[...]) + raw_product(two[...])
+
+
+def early_kernel(count, dual, raw_in, *refs):
+    tiles, gram, raw_out = refs[:count], refs[count], refs[count + 1]
+    raw = raw_in[...]
     for i in range(count):
-        part, raw = tile_products(tiles[i][...], dual[...])
-        gram[i] = part
-        if i:
-            raw_out[...] += raw
-        else:
-            raw_out[...] = raw
-
-
-def late_kernel(near, dual, early, raw_in, lumped, forward, backward, half_a, half_b, mine, other, raw_out):
+        tile = tiles[i][...]
+        gram[i] = gram_product(tile, dual[...])
+        if i >= 3:
+            raw = raw + raw_product(tile)
+    raw_out[...] = raw
+
+
+def late_kernel(near, dual, early, raw_in, lumped, half_a, half_b, mine, other, norm_out, raw_out):
     me = lax.axis_index("y")
     nodes = raw_out.shape[2]
     far = jnp.concatenate([half_a[...], half_b[...]], axis=0)
-    raw = raw_in[...]
-    products = []
-    for tile in (forward[...], backward[...], far):
-        part, term = tile_products(tile, dual[...])
-        products.append(part)
-        raw = raw + term
+    product = gram_product(far, dual[...])
+    raw = raw_in[...] + raw_product(far)
     column = jnp.zeros((MODES, 1), F32)
     for c in range(3):
         part = raw[:, c * nodes : (c + 1) * nodes]
@@ -95,31 +97,29 @@
     k = lax.broadcasted_iota(jnp.int32, (MODES, TILE), 0)
     lane = lax.broadcasted_iota(jnp.int32, (MODES, TILE), 1)
     row = jnp.sum(jnp.where(lane % MODES == k, column, 0.0), axis=0, keepdims=True)
-    norm = jnp.broadcast_to(row, (SLOT - OWN, TILE))
-    steps = near + [3, NY - 3, 4]
+    norm_out[...] = jnp.broadcast_to(row, (SLOT - OWN, TILE))
+    other[NSPACE // NC] = jnp.broadcast_to(row, (OWN, TILE))
+    steps = near + [4]
     first = lax.axis_index("core") == 0
     for i, step in enumerate(steps):
         source = lax.rem(me + step, NY)
-        part = early[i] if i < len(near) else products[i - len(near)]
+        part = early[i] if i < len(near) else product
         for o in range(TILE // OWN // NC):
             one = part[2 * o * OWN : (2 * o + 1) * OWN]
             two = part[(2 * o + 1) * OWN : (2 * o + 2) * OWN]
             place = source * (TILE // OWN // NC) + o
-            mine[place, :OWN, :] = jnp.where(first, one, two)
-            other[place, :OWN, :] = jnp.where(first, two, one)
-    for i in range(NSPACE // NC):
-        mine[i, OWN:, :] = norm
-        other[i, OWN:, :] = norm
-
-
-def pair_kernel(mine, other, out):
+            mine[place] = jnp.where(first, one, two)
+            other[place] = jnp.where(first, two, one)
+
+
+def pair_kernel(mine, other, norm_in, out):
     lane = lax.broadcasted_iota(jnp.int32, (SLOT - OWN, TILE), 1)
-    row = mine[0, OWN:, :] + other[0, OWN:, :]
+    row = norm_in[...] + other[NSPACE // NC, : SLOT - OWN, :]
     high = row.astype(BF16)
     rest = (row - high.astype(F32)).astype(BF16)
     norm = jnp.where(lane < MODES, high.astype(F32), rest.astype(F32))
     for i in range(NSPACE // NC):
-        total = mine[i, :OWN, :] + other[i, :OWN, :]
+        total = mine[i] + other[i]
         out[i] = jnp.concatenate([total, norm], axis=0).astype(BF16)
 
 
@@ -170,12 +170,13 @@
     up.append(shift(tile, -1))
     down.append(shift(tile, 1))
     edge = ((REACH, BLOCK, 3 * TILE), F32)
-    low, mid, high = call(
+    low, mid, high, weight = call(
         dual_kernel,
-        [edge, ((blocks, BLOCK, 3 * TILE), F32), edge],
+        [edge, ((blocks, BLOCK, 3 * TILE), F32), edge, ((1, nodes), F32)],
         block_cols,
         mass,
         own,
+        lumped.reshape(1, nodes),
         scratch=[pltpu.VMEM((blocks + 2 * REACH, BLOCK, 3 * TILE), F32)],
         smem=1,
     )
@@ -185,40 +186,43 @@
     low, high, down[1] = lax.optimization_barrier((low, high, down[1]))
     from_prev = lax.ppermute(high, SPACE, [(i, i + 1) for i in range(NSPACE - 1)])
     from_next = lax.ppermute(low, SPACE, [(i + 1, i) for i in range(NSPACE - 1)])
-    up.append(shift(up[2], -1))
+    raw = call(first_kernel, ((MODES, 3 * nodes), F32), tile, up[1], down[1])
+    second, raw = lax.optimization_barrier((up[2], raw))
+    up.append(shift(second, -1))
     down.append(shift(down[2], 1))
     dual = call(join_kernel, ((3 * nodes, 2 * TILE), BF16), mid, from_prev, from_next)
 
     half_a = shift(up[3][:cut], -1)
     half_b = shift(down[3][cut:], 1)
 
-    near = [0, 1, NY - 1, 2, NY - 2]
-    early, raw, weight = call(
+    near = [0, 1, NY - 1, 2, NY - 2, 3, NY - 3]
+    early, raw = call(
         lambda *refs: early_kernel(len(near), *refs),
-        [((len(near), TILE, TILE), F32), ((MODES, 3 * nodes), F32), ((1, nodes), F32)],
+        [((len(near), TILE, TILE), F32), ((MODES, 3 * nodes), F32)],
         dual,
-        lumped.reshape(1, nodes),
+        raw,
         tile,
         up[1],
         down[1],
         up[2],
         down[2],
-    )
-    slot = ((NSPACE // NC, SLOT, TILE), F32)
-    mine, other, raw = call(
+        up[3],
+        down[3],
+    )
+    own_slots = ((NSPACE // NC, OWN, TILE), F32)
+    far_slots = ((NSPACE // NC + 1, OWN, TILE), F32)
+    mine, other, norm, raw = call(
         lambda *refs: late_kernel(near, *refs),
-        [slot, slot, ((3, MODES, nodes), F32)],
+        [own_slots, far_slots, ((SLOT - OWN, TILE), F32), ((3, MODES, nodes), F32)],
         dual,
         early,
         raw,
         weight,
-        up[3],
-        down[3],
         half_a,
         half_b,
     )
     other = lax.ppermute(other, "core", [(0, 1), (1, 0)])
-    slots = call(pair_kernel, ((NSPACE // NC, SLOT, TILE), BF16), mine, other)
+    slots = call(pair_kernel, ((NSPACE // NC, SLOT, TILE), BF16), mine, other, norm)
     parts = lax.all_to_all(slots, ("x", "z"), split_axis=0, concat_axis=0, tiled=True)
     gram, modes = call(
         lambda *refs: final_kernel(3.0 * nodes * NSPACE, *refs),

time: 87.5 us -> 86.8 us (level)
    pallas_call x6 -> x7, Pallas kernels: 5.27 us -> 5.33 us  [call(): pl.pallas_call(kernel, out_shape=[jax.ShapeDtypeStruct(*s) for s in outs]...]
  transfers between devices with their start and end apart: 11 -> 11, of which waited for: 4 -> 4; matrix products, arithmetic and copies ran while one was open for 1% -> 1% of each run, Pallas kernels for 4% -> 5%
where the time goes in v4:
time: 86.8 us; the launch traced here: 85.8 us
  starting transfers between devices  43.6 us (50%)
  blocking collectives  24.1 us (28%)
  waiting for transfers between devices  9.12 us (11%)
  Pallas kernels  5.33 us (6%)
  local copies, waits for them, and re-layouts  1.7 us (2%)
  other arithmetic  1.1 us (1%)
  between operations  0.88 us (1%)
    ppermute x8, starting transfers between devices, shift(): return lax.ppermute(value, 'y', [(i, (i + step) % NY) for i in range(NY)])  29.6 us
    all_to_all x1, blocking collectives, local(): lax.all_to_all(slots, ('x', 'z'), split_axis=0, concat_axis=0, tiled=True)  24.1 us
    ppermute x1, starting transfers between devices, local(): lax.ppermute(high, SPACE, [(i, i + 1) for i in range(NSPACE - 1)])  10.2 us
    ppermute x8, waiting for transfers between devices, shift(): return lax.ppermute(value, 'y', [(i, (i + step) % NY) for i in range(NY)])  7.6 us
    pallas_call x7, Pallas kernels, call(): pl.pallas_call(kernel, out_shape=[jax.ShapeDtypeStruct(*s) for s in outs]...  5.33 us
    ppermute x1, starting transfers between devices, local(): lax.ppermute(low, SPACE, [(i + 1, i) for i in range(NSPACE - 1)])  1.92 us
    ppermute x1, starting transfers between devices, local(): other = lax.ppermute(other, 'core', [(0, 1), (1, 0)])  1.92 us
  transfers between devices with their start and end apart: 11, of which 4 were waited for; matrix products, arithmetic and copies ran while one was open for 1% of the time, Pallas kernels for 5%

profile of v4, /device:TPU:1, one launch (start us, length us, event | category | flops | bytes accessed | tf_op | source)
XLA Modules:
  0.0 85.8 jit_solution(14032037942499150640)
XLA Ops:
  0.6 0.0 copy-start.3
  0.6 1.1 %pad_maximum_fusion.own.refs_2_ = bf16[1600,128]{1,0:T(8,128)(2,1)S(1)} fusion(bf16[64,128]{1,0:T(8,128)(2,1)} %bitcast.14, bf16[1536,128]{1,0:T(8,128)(2,1)} %bitcast.11), kind=kLoop, calls=%fused_computation | loop fusion | flops 819200 | bytes 819200 | tf_op jit(solution)/shard_map/concatenate | solution.py:165
  1.7 0.0 copy-start
  1.8 6.1 %collective-permute-start = (bf16[1600,128]{1,0:T(8,128)(2,1)S(1)}, bf16[1600,128]{1,0:T(8,128)(2,1)S(1)}, u32[]{:S(2)}, u32[]{:S(2)}) collective-permute-start(bf16[1600,128]{1,0:T(8,128)(2,1)S(1)} %pad_maximum_fusion.own.refs_2_), channel_id=1, source_target_pairs={{0,7},{1,0},{2,1},{3,2},{4,3},{5,4},{6,5},{7,6},{8,15},{9,8},{10,9... | collective-permute-start | bytes 1228808 | tf_op jit(solution)/shard_map/ppermute | solution.py:158
  7.8 1.9 %collective-permute-start.1 = (bf16[1600,128]{1,0:T(8,128)(2,1)S(1)}, bf16[1600,128]{1,0:T(8,128)(2,1)S(1)}, u32[]{:S(2)}, u32[]{:S(2)}) collective-permute-start(bf16[1600,128]{1,0:T(8,128)(2,1)S(1)} %pad_maximum_fusion.own.refs_2_), channel_id=1, source_target_pairs={{0,1},{1,2},{2,3},{3,4},{4,5},{5,6},{6,7},{7,0},{8,9},{9,10},{10,1... | collective-permute-start | bytes 1228808 | tf_op jit(solution)/shard_map/ppermute | solution.py:158
  9.7 0.0 copy-done.3
  9.8 0.0 copy-start.2
  9.8 1.0 %reshape.13 = bf16[8,7,64,64]{3,2,0,1:T(8,128)(2,1)S(1)} reshape(bf16[8,7,4096]{2,0,1:T(8,128)(2,1)S(1)} %copy-done.3) | data formatting | bytes 917504 | tf_op jit(solution)/shard_map/reshape | solution.py:168
  10.8 0.0 copy-start.1
  10.8 0.0 copy-done
  10.8 0.0 copy-done.2
  10.8 0.7 copy-done.1
  11.5 1.8 %shard_map.68 = (f32[3,64,384]{2,1,0:T(8,128)S(1)}, f32[8,64,384]{2,1,0:T(8,128)S(1)}, f32[3,64,384]{2,1,0:T(8,128)S(1)}, f32[1,512]{1,0:T(1,128)S(1)}) custom-call(s32[8,7]{1,0:T(8,128)S(1)} %copy-done.1, bf16[7,8,64,64]{3,2,1,0:T(8,128)(2,1)S(1)} %bitcast.10, bf16[3,512,128]{2,1,0:T(8,128)(2,1)S(1)} %bitcast.12, f32[1,512]{1,0:T(1,128)S(1)} %bitcast.13), custom_call_target="tpu_custom_call" | custom-call | tf_op jit(solution)/shard_map/pallas_call | solution.py:146
  13.3 0.7 collective-permute-done.one.refs_3_
  14.0 5.3 %collective-permute-start.4 = (bf16[1600,128]{1,0:T(8,128)(2,1)S(1)}, bf16[1600,128]{1,0:T(8,128)(2,1)S(1)}, u32[]{:S(2)}, u32[]{:S(2)}) collective-permute-start(bf16[1600,128]{1,0:T(8,128)(2,1)S(1)} %collective-permute-done.one.refs_3_), channel_id=1, source_target_pairs={{0,7},{1,0},{2,1},{3,2},{4,3},{5,4},{6,5},{7,6},{8,15},{9,8},{10,9... | collective-permute-start | bytes 1228808 | tf_op jit(solution)/shard_map/ppermute | solution.py:158
  19.3 0.0 collective-permute-done.1.two.refs_4_
  19.3 1.9 %collective-permute-start.5 = (bf16[1600,128]{1,0:T(8,128)(2,1)S(1)}, bf16[1600,128]{1,0:T(8,128)(2,1)S(1)}, u32[]{:S(2)}, u32[]{:S(2)}) collective-permute-start(bf16[1600,128]{1,0:T(8,128)(2,1)S(1)} %collective-permute-done.1.two.refs_4_), channel_id=1, source_target_pairs={{0,1},{1,2},{2,3},{3,4},{4,5},{5,6},{6,7},{7,0},{8,9},{9,10},{10,1... | collective-permute-start | bytes 1228808 | tf_op jit(solution)/shard_map/ppermute | solution.py:158
  21.2 0.5 shard_map.70.refs_1_
  21.7 2.8 %collective-permute-done.4.refs_5_ = bf16[1600,128]{1,0:T(8,128)(2,1)S(1)} collective-permute-done((bf16[1600,128]{1,0:T(8,128)(2,1)S(1)}, bf16[1600,128]{1,0:T(8,128)(2,1)S(1)}, u32[]{:S(2)}, u32[]{:S(2)}) %collective-permute-start.4) | collective-permute-done | bytes 409632 | tf_op jit(solution)/shard_map/ppermute | solution.py:158
  24.5 5.7 %collective-permute-start.6 = (bf16[1600,128]{1,0:T(8,128)(2,1)S(1)}, bf16[1600,128]{1,0:T(8,128)(2,1)S(1)}, u32[]{:S(2)}, u32[]{:S(2)}) collective-permute-start(bf16[1600,128]{1,0:T(8,128)(2,1)S(1)} %collective-permute-done.4.refs_5_), channel_id=1, source_target_pairs={{0,7},{1,0},{2,1},{3,2},{4,3},{5,4},{6,5},{7,6},{8,15},{9,8},{10,9... | collective-permute-start | bytes 1228808 | tf_op jit(solution)/shard_map/ppermute | solution.py:158
  30.2 0.0 collective-permute-done.5.refs_6_
  30.2 1.9 %collective-permute-start.7 = (bf16[1600,128]{1,0:T(8,128)(2,1)S(1)}, bf16[1600,128]{1,0:T(8,128)(2,1)S(1)}, u32[]{:S(2)}, u32[]{:S(2)}) collective-permute-start(bf16[1600,128]{1,0:T(8,128)(2,1)S(1)} %collective-permute-done.5.refs_6_), channel_id=1, source_target_pairs={{0,1},{1,2},{2,3},{3,4},{4,5},{5,6},{6,7},{7,0},{8,9},{9,10},{10,1... | collective-permute-start | bytes 1228808 | tf_op jit(solution)/shard_map/ppermute | solution.py:158
  32.1 10.2 %collective-permute-start.2 = (f32[3,64,384]{2,1,0:T(8,128)S(1)}, f32[3,64,384]{2,1,0:T(8,128)S(1)}, u32[]{:S(2)}, u32[]{:S(2)}) collective-permute-start(f32[3,64,384]{2,1,0:T(8,128)S(1)} %get-tuple-element.27), channel_id=1, source_target_pairs={{0,8},{8,16},{16,24},{24,32},{32,40},{40,48},{48,56},{56,64},{64,7... | collective-permute-start | bytes 884744 | tf_op jit(solution)/shard_map/ppermute | solution.py:187
  42.3 1.9 %collective-permute-start.3 = (f32[3,64,384]{2,1,0:T(8,128)S(1)}, f32[3,64,384]{2,1,0:T(8,128)S(1)}, u32[]{:S(2)}, u32[]{:S(2)}) collective-permute-start(f32[3,64,384]{2,1,0:T(8,128)S(1)} %get-tuple-element.28), channel_id=1, source_target_pairs={{8,0},{16,8},{24,16},{32,24},{40,32},{48,40},{56,48},{64,56},{72,6... | collective-permute-start | bytes 884744 | tf_op jit(solution)/shard_map/ppermute | solution.py:188
  44.3 0.0 collective-permute-done.6.refs_7_
  44.3 4.9 %collective-permute-start.8 = (bf16[800,128]{1,0:T(8,128)(2,1)S(1)}, bf16[800,128]{1,0:T(8,128)(2,1)S(1)}, u32[]{:S(2)}, u32[]{:S(2)}) collective-permute-start(bf16[800,128]{1,0:T(8,128)(2,1)S(1)} %slice.8), channel_id=1, source_target_pairs={{0,7},{1,0},{2,1},{3,2},{4,3},{5,4},{6,5},{7,6},{8,15},{9,8},{10,9... | collective-permute-start | bytes 614408 | tf_op jit(solution)/shard_map/ppermute | solution.py:158
  49.2 0.0 collective-permute-done.7.refs_8_
  49.2 1.9 %collective-permute-start.9 = (bf16[800,128]{1,0:T(8,128)(2,1)S(1)}, bf16[800,128]{1,0:T(8,128)(2,1)S(1)}, u32[]{:S(2)}, u32[]{:S(2)}) collective-permute-start(bf16[800,128]{1,0:T(8,128)(2,1)S(1)} %slice.9), channel_id=1, source_target_pairs={{0,1},{1,2},{2,3},{3,4},{4,5},{5,6},{6,7},{7,0},{8,9},{9,10},{10,1... | collective-permute-start | bytes 614408 | tf_op jit(solution)/shard_map/ppermute | solution.py:158
  51.1 0.0 collective-permute-done.2.from_prev
  51.1 0.0 collective-permute-done.3.from_next
  51.1 0.2 shard_map.69.refs_0_
  51.3 1.4 %shard_map.71 = (f32[7,128,128]{2,1,0:T(8,128)S(1)}, f32[64,1536]{1,0:T(8,128)S(1)}) custom-call(bf16[1536,256]{1,0:T(8,128)(2,1)S(1)} %shard_map.69.refs_0_, f32[64,1536]{1,0:T(8,128)S(1)} %shard_map.70.refs_1_, bf16[1600,128]{1,0:T(8,128)(2,1)S(1)} %pad_maximum_fusion.own.refs_2_, bf16[1600,128]{1,0:T(8,128)(2,1)S(1)} %collective-permute-done.one.refs_3_, ...), custom_call_target="tpu_custom_call" | custom-call | tf_op jit(solution)/shard_map/pallas_call | solution.py:146
  52.7 0.0 collective-permute-done.8.refs_4_
  52.7 4.2 %collective-permute-done.9.refs_5_ = bf16[800,128]{1,0:T(8,128)(2,1)S(1)} collective-permute-done((bf16[800,128]{1,0:T(8,128)(2,1)S(1)}, bf16[800,128]{1,0:T(8,128)(2,1)S(1)}, u32[]{:S(2)}, u32[]{:S(2)}) %collective-permute-start.9) | collective-permute-done | bytes 204832 | tf_op jit(solution)/shard_map/ppermute | solution.py:158
  56.9 0.5 shard_map.72
  57.4 1.9 %collective-permute-start.10 = (f32[33,16,128]{2,1,0:T(8,128)S(1)}, f32[33,16,128]{2,1,0:T(8,128)S(1)}, u32[]{:S(2)}, u32[]{:S(2)}) collective-permute-start(f32[33,16,128]{2,1,0:T(8,128)S(1)} %get-tuple-element.37), channel_id=1, source_target_pairs={{0,8},{8,0},{1,9},{9,1},{2,10},{10,2},{3,11},{11,3},{4,12},{12,4},... | collective-permute-start | bytes 811016 | tf_op jit(solution)/shard_map/ppermute | solution.py:224
  59.3 1.5 %collective-permute-done.10.other = f32[33,16,128]{2,1,0:T(8,128)S(1)} collective-permute-done((f32[33,16,128]{2,1,0:T(8,128)S(1)}, f32[33,16,128]{2,1,0:T(8,128)S(1)}, u32[]{:S(2)}, u32[]{:S(2)}) %collective-permute-start.10) | collective-permute-done | bytes 270368 | tf_op jit(solution)/shard_map/ppermute | solution.py:224
  60.9 24.1 %all_to_all.5.refs_0_ = bf16[32,24,128]{2,1,0:T(8,128)(2,1)S(1)} all-to-all(bf16[32,24,128]{2,1,0:T(8,128)(2,1)S(1)} %shard_map.73), channel_id=1, replica_groups=mesh['x'=4,'z'=8,'core'=2,'y'=8] {'x','z'}, dimensions={0} | all-to-all | bytes 393216 | tf_op jit(solution)/shard_map/all_to_all | solution.py:226
  84.9 0.9 %shard_map.74 = (f32[16,128]{1,0:T(8,128)}, bf16[3,64,512]{2,1,0:T(8,128)(2,1)}) custom-call(bf16[32,24,128]{2,1,0:T(8,128)(2,1)S(1)} %all_to_all.5.refs_0_, f32[3,64,512]{2,1,0:T(8,128)S(1)} %get-tuple-element.39.refs_1_), custom_call_target="tpu_custom_call" | custom-call | tf_op jit(solution)/shard_map/pallas_call | solution.py:146
  (3 shorter events, 0.1 us)
Async XLA Ops:
  0.6 9.1 %copy-start.3 = (bf16[8,7,4096]{2,0,1:T(8,128)(2,1)S(1)}, bf16[8,7,4096]{2,0,1:T(8,128)(2,1)}, u32[]{:S(2)}) copy-start(bf16[8,7,4096]{2,0,1:T(8,128)(2,1)} %param.6) | copy-start | bytes 1376260
  1.7 9.0 %copy-start = (bf16[512,3,128]{2,0,1:T(8,128)(2,1)S(1)}, bf16[512,3,128]{2,0,1:T(8,128)(2,1)}, u32[]{:S(2)}) copy-start(bf16[512,3,128]{2,0,1:T(8,128)(2,1)} %param.5) | copy-start | bytes 1179652
  1.8 12.2 %collective-permute-start = (bf16[1600,128]{1,0:T(8,128)(2,1)S(1)}, bf16[1600,128]{1,0:T(8,128)(2,1)S(1)}, u32[]{:S(2)}, u32[]{:S(2)}) collective-permute-start(bf16[1600,128]{1,0:T(8,128)(2,1)S(1)} %pad_maximum_fusion.own.refs_2_), channel_id=1, source_target_pairs={{0,7},{1,0},{2,1},{3,2},{4,3},{5,4},{6,5},{7,6},{8,15},{9,8},{10,9... | collective-permute-start | bytes 1228808 | tf_op jit(solution)/shard_map/ppermute | solution.py:158
  7.8 11.5 %collective-permute-start.1 = (bf16[1600,128]{1,0:T(8,128)(2,1)S(1)}, bf16[1600,128]{1,0:T(8,128)(2,1)S(1)}, u32[]{:S(2)}, u32[]{:S(2)}) collective-permute-start(bf16[1600,128]{1,0:T(8,128)(2,1)S(1)} %pad_maximum_fusion.own.refs_2_), channel_id=1, source_target_pairs={{0,1},{1,2},{2,3},{3,4},{4,5},{5,6},{6,7},{7,0},{8,9},{9,10},{10,1... | collective-permute-start | bytes 1228808 | tf_op jit(solution)/shard_map/ppermute | solution.py:158
  9.8 1.0 %copy-start.2 = (f32[512]{0:T(512)S(1)}, f32[512]{0:T(512)}, u32[]{:S(2)}) copy-start(f32[512]{0:T(512)} %param.9) | copy-start | bytes 6148
  10.8 0.7 copy-start.1
  14.0 10.5 %collective-permute-start.4 = (bf16[1600,128]{1,0:T(8,128)(2,1)S(1)}, bf16[1600,128]{1,0:T(8,128)(2,1)S(1)}, u32[]{:S(2)}, u32[]{:S(2)}) collective-permute-start(bf16[1600,128]{1,0:T(8,128)(2,1)S(1)} %collective-permute-done.one.refs_3_), channel_id=1, source_target_pairs={{0,7},{1,0},{2,1},{3,2},{4,3},{5,4},{6,5},{7,6},{8,15},{9,8},{10,9... | collective-permute-start | bytes 1228808 | tf_op jit(solution)/shard_map/ppermute | solution.py:158
  19.3 10.9 %collective-permute-start.5 = (bf16[1600,128]{1,0:T(8,128)(2,1)S(1)}, bf16[1600,128]{1,0:T(8,128)(2,1)S(1)}, u32[]{:S(2)}, u32[]{:S(2)}) collective-permute-start(bf16[1600,128]{1,0:T(8,128)(2,1)S(1)} %collective-permute-done.1.two.refs_4_), channel_id=1, source_target_pairs={{0,1},{1,2},{2,3},{3,4},{4,5},{5,6},{6,7},{7,0},{8,9},{9,10},{10,1... | collective-permute-start | bytes 1228808 | tf_op jit(solution)/shard_map/ppermute | solution.py:158
  24.5 19.8 %collective-permute-start.6 = (bf16[1600,128]{1,0:T(8,128)(2,1)S(1)}, bf16[1600,128]{1,0:T(8,128)(2,1)S(1)}, u32[]{:S(2)}, u32[]{:S(2)}) collective-permute-start(bf16[1600,128]{1,0:T(8,128)(2,1)S(1)} %collective-permute-done.4.refs_5_), channel_id=1, source_target_pairs={{0,7},{1,0},{2,1},{3,2},{4,3},{5,4},{6,5},{7,6},{8,15},{9,8},{10,9... | collective-permute-start | bytes 1228808 | tf_op jit(solution)/shard_map/ppermute | solution.py:158
  30.2 18.9 %collective-permute-start.7 = (bf16[1600,128]{1,0:T(8,128)(2,1)S(1)}, bf16[1600,128]{1,0:T(8,128)(2,1)S(1)}, u32[]{:S(2)}, u32[]{:S(2)}) collective-permute-start(bf16[1600,128]{1,0:T(8,128)(2,1)S(1)} %collective-permute-done.5.refs_6_), channel_id=1, source_target_pairs={{0,1},{1,2},{2,3},{3,4},{4,5},{5,6},{6,7},{7,0},{8,9},{9,10},{10,1... | collective-permute-start | bytes 1228808 | tf_op jit(solution)/shard_map/ppermute | solution.py:158
  32.1 19.0 %collective-permute-start.2 = (f32[3,64,384]{2,1,0:T(8,128)S(1)}, f32[3,64,384]{2,1,0:T(8,128)S(1)}, u32[]{:S(2)}, u32[]{:S(2)}) collective-permute-start(f32[3,64,384]{2,1,0:T(8,128)S(1)} %get-tuple-element.27), channel_id=1, source_target_pairs={{0,8},{8,16},{16,24},{24,32},{32,40},{40,48},{48,56},{56,64},{64,7... | collective-permute-start | bytes 884744 | tf_op jit(solution)/shard_map/ppermute | solution.py:187
  42.3 8.8 %collective-permute-start.3 = (f32[3,64,384]{2,1,0:T(8,128)S(1)}, f32[3,64,384]{2,1,0:T(8,128)S(1)}, u32[]{:S(2)}, u32[]{:S(2)}) collective-permute-start(f32[3,64,384]{2,1,0:T(8,128)S(1)} %get-tuple-element.28), channel_id=1, source_target_pairs={{8,0},{16,8},{24,16},{32,24},{40,32},{48,40},{56,48},{64,56},{72,6... | collective-permute-start | bytes 884744 | tf_op jit(solution)/shard_map/ppermute | solution.py:188
  44.3 8.4 %collective-permute-start.8 = (bf16[800,128]{1,0:T(8,128)(2,1)S(1)}, bf16[800,128]{1,0:T(8,128)(2,1)S(1)}, u32[]{:S(2)}, u32[]{:S(2)}) collective-permute-start(bf16[800,128]{1,0:T(8,128)(2,1)S(1)} %slice.8), channel_id=1, source_target_pairs={{0,7},{1,0},{2,1},{3,2},{4,3},{5,4},{6,5},{7,6},{8,15},{9,8},{10,9... | collective-permute-start | bytes 614408 | tf_op jit(solution)/shard_map/ppermute | solution.py:158
  49.2 7.7 %collective-permute-start.9 = (bf16[800,128]{1,0:T(8,128)(2,1)S(1)}, bf16[800,128]{1,0:T(8,128)(2,1)S(1)}, u32[]{:S(2)}, u32[]{:S(2)}) collective-permute-start(bf16[800,128]{1,0:T(8,128)(2,1)S(1)} %slice.9), channel_id=1, source_target_pairs={{0,1},{1,2},{2,3},{3,4},{4,5},{5,6},{6,7},{7,0},{8,9},{9,10},{10,1... | collective-permute-start | bytes 614408 | tf_op jit(solution)/shard_map/ppermute | solution.py:158
  57.4 3.4 %collective-permute-start.10 = (f32[33,16,128]{2,1,0:T(8,128)S(1)}, f32[33,16,128]{2,1,0:T(8,128)S(1)}, u32[]{:S(2)}, u32[]{:S(2)}) collective-permute-start(f32[33,16,128]{2,1,0:T(8,128)S(1)} %get-tuple-element.37), channel_id=1, source_target_pairs={{0,8},{8,0},{1,9},{9,1},{2,10},{10,2},{3,11},{11,3},{4,12},{12,4},... | collective-permute-start | bytes 811016 | tf_op jit(solution)/shard_map/ppermute | solution.py:224

commit v5 on v4

--- a/solution.py
+++ b/solution.py
@@ -39,7 +39,7 @@
     high[...] = acc[REACH + blocks :]
 
 
-def join_kernel(mid, from_prev, from_next, out):
+def join_kernel(mid, from_next, from_prev, out):
     blocks = mid.shape[0]
     for b in range(blocks):
         value = mid[b]
@@ -184,13 +184,13 @@
     up.append(shift(first, -1))
     down.append(shift(down[1], 1))
     low, high, down[1] = lax.optimization_barrier((low, high, down[1]))
+    from_next = lax.ppermute(low, SPACE, [(i + 1, i) for i in range(NSPACE - 1)])
     from_prev = lax.ppermute(high, SPACE, [(i, i + 1) for i in range(NSPACE - 1)])
-    from_next = lax.ppermute(low, SPACE, [(i + 1, i) for i in range(NSPACE - 1)])
     raw = call(first_kernel, ((MODES, 3 * nodes), F32), tile, up[1], down[1])
     second, raw = lax.optimization_barrier((up[2], raw))
     up.append(shift(second, -1))
     down.append(shift(down[2], 1))
-    dual = call(join_kernel, ((3 * nodes, 2 * TILE), BF16), mid, from_prev, from_next)
+    dual = call(join_kernel, ((3 * nodes, 2 * TILE), BF16), mid, from_next, from_prev)
 
     half_a = shift(up[3][:cut], -1)
     half_b = shift(down[3][cut:], 1)

time: 86.8 us -> 86.5 us (level)
    ppermute x1, starting transfers between devices: 10.2 us -> 5.87 us  [local(): lax.ppermute(high, SPACE, [(i, i + 1) for i in range(NSPACE - 1)])]
    ppermute x1, starting transfers between devices: 1.92 us -> 6.24 us  [local(): lax.ppermute(low, SPACE, [(i + 1, i) for i in range(NSPACE - 1)])]
where the time goes in v5:
time: 86.5 us; the launch traced here: 85.4 us
  starting transfers between devices  43.6 us (50%)
  blocking collectives  23.7 us (27%)
  waiting for transfers between devices  9.11 us (11%)
  Pallas kernels  5.34 us (6%)
  local copies, waits for them, and re-layouts  1.7 us (2%)
  other arithmetic  1.1 us (1%)
  between operations  0.88 us (1%)
    ppermute x8, starting transfers between devices, shift(): return lax.ppermute(value, 'y', [(i, (i + step) % NY) for i in range(NY)])  29.6 us
    all_to_all x1, blocking collectives, local(): lax.all_to_all(slots, ('x', 'z'), split_axis=0, concat_axis=0, tiled=True)  23.7 us
    ppermute x8, waiting for transfers between devices, shift(): return lax.ppermute(value, 'y', [(i, (i + step) % NY) for i in range(NY)])  7.59 us
    ppermute x1, starting transfers between devices, local(): lax.ppermute(low, SPACE, [(i + 1, i) for i in range(NSPACE - 1)])  6.24 us
    ppermute x1, starting transfers between devices, local(): lax.ppermute(high, SPACE, [(i, i + 1) for i in range(NSPACE - 1)])  5.87 us
    pallas_call x7, Pallas kernels, call(): pl.pallas_call(kernel, out_shape=[jax.ShapeDtypeStruct(*s) for s in outs]...  5.34 us
    ppermute x1, starting transfers between devices, local(): other = lax.ppermute(other, 'core', [(0, 1), (1, 0)])  1.92 us
  transfers between devices with their start and end apart: 11, of which 4 were waited for; matrix products, arithmetic and copies ran while one was open for 1% of the time, Pallas kernels for 5%

profile of v5, /device:TPU:1, one launch (start us, length us, event | category | flops | bytes accessed | tf_op | source)
XLA Modules:
  0.0 85.4 jit_solution(4621755754904232522)
XLA Ops:
  0.6 0.0 copy-start.3
  0.6 1.1 %pad_maximum_fusion.own.refs_2_ = bf16[1600,128]{1,0:T(8,128)(2,1)S(1)} fusion(bf16[64,128]{1,0:T(8,128)(2,1)} %bitcast.14, bf16[1536,128]{1,0:T(8,128)(2,1)} %bitcast.11), kind=kLoop, calls=%fused_computation | loop fusion | flops 819200 | bytes 819200 | tf_op jit(solution)/shard_map/concatenate | solution.py:165
  1.7 0.0 copy-start
  1.8 6.1 %collective-permute-start = (bf16[1600,128]{1,0:T(8,128)(2,1)S(1)}, bf16[1600,128]{1,0:T(8,128)(2,1)S(1)}, u32[]{:S(2)}, u32[]{:S(2)}) collective-permute-start(bf16[1600,128]{1,0:T(8,128)(2,1)S(1)} %pad_maximum_fusion.own.refs_2_), channel_id=1, source_target_pairs={{0,7},{1,0},{2,1},{3,2},{4,3},{5,4},{6,5},{7,6},{8,15},{9,8},{10,9... | collective-permute-start | bytes 1228808 | tf_op jit(solution)/shard_map/ppermute | solution.py:158
  7.8 1.9 %collective-permute-start.1 = (bf16[1600,128]{1,0:T(8,128)(2,1)S(1)}, bf16[1600,128]{1,0:T(8,128)(2,1)S(1)}, u32[]{:S(2)}, u32[]{:S(2)}) collective-permute-start(bf16[1600,128]{1,0:T(8,128)(2,1)S(1)} %pad_maximum_fusion.own.refs_2_), channel_id=1, source_target_pairs={{0,1},{1,2},{2,3},{3,4},{4,5},{5,6},{6,7},{7,0},{8,9},{9,10},{10,1... | collective-permute-start | bytes 1228808 | tf_op jit(solution)/shard_map/ppermute | solution.py:158
  9.7 0.0 copy-done.3
  9.8 0.0 copy-start.2
  9.8 1.0 %reshape.13 = bf16[8,7,64,64]{3,2,0,1:T(8,128)(2,1)S(1)} reshape(bf16[8,7,4096]{2,0,1:T(8,128)(2,1)S(1)} %copy-done.3) | data formatting | bytes 917504 | tf_op jit(solution)/shard_map/reshape | solution.py:168
  10.8 0.0 copy-start.1
  10.8 0.0 copy-done
  10.8 0.0 copy-done.2
  10.8 0.7 copy-done.1
  11.5 1.8 %shard_map.68 = (f32[3,64,384]{2,1,0:T(8,128)S(1)}, f32[8,64,384]{2,1,0:T(8,128)S(1)}, f32[3,64,384]{2,1,0:T(8,128)S(1)}, f32[1,512]{1,0:T(1,128)S(1)}) custom-call(s32[8,7]{1,0:T(8,128)S(1)} %copy-done.1, bf16[7,8,64,64]{3,2,1,0:T(8,128)(2,1)S(1)} %bitcast.10, bf16[3,512,128]{2,1,0:T(8,128)(2,1)S(1)} %bitcast.12, f32[1,512]{1,0:T(1,128)S(1)} %bitcast.13), custom_call_target="tpu_custom_call" | custom-call | tf_op jit(solution)/shard_map/pallas_call | solution.py:146
  13.3 0.7 collective-permute-done.one.refs_3_
  14.0 5.3 %collective-permute-start.4 = (bf16[1600,128]{1,0:T(8,128)(2,1)S(1)}, bf16[1600,128]{1,0:T(8,128)(2,1)S(1)}, u32[]{:S(2)}, u32[]{:S(2)}) collective-permute-start(bf16[1600,128]{1,0:T(8,128)(2,1)S(1)} %collective-permute-done.one.refs_3_), channel_id=1, source_target_pairs={{0,7},{1,0},{2,1},{3,2},{4,3},{5,4},{6,5},{7,6},{8,15},{9,8},{10,9... | collective-permute-start | bytes 1228808 | tf_op jit(solution)/shard_map/ppermute | solution.py:158
  19.3 0.0 collective-permute-done.1.two.refs_4_
  19.3 1.9 %collective-permute-start.5 = (bf16[1600,128]{1,0:T(8,128)(2,1)S(1)}, bf16[1600,128]{1,0:T(8,128)(2,1)S(1)}, u32[]{:S(2)}, u32[]{:S(2)}) collective-permute-start(bf16[1600,128]{1,0:T(8,128)(2,1)S(1)} %collective-permute-done.1.two.refs_4_), channel_id=1, source_target_pairs={{0,1},{1,2},{2,3},{3,4},{4,5},{5,6},{6,7},{7,0},{8,9},{9,10},{10,1... | collective-permute-start | bytes 1228808 | tf_op jit(solution)/shard_map/ppermute | solution.py:158
  21.2 0.5 shard_map.70.refs_1_
  21.7 2.8 %collective-permute-done.4.refs_5_ = bf16[1600,128]{1,0:T(8,128)(2,1)S(1)} collective-permute-done((bf16[1600,128]{1,0:T(8,128)(2,1)S(1)}, bf16[1600,128]{1,0:T(8,128)(2,1)S(1)}, u32[]{:S(2)}, u32[]{:S(2)}) %collective-permute-start.4) | collective-permute-done | bytes 409632 | tf_op jit(solution)/shard_map/ppermute | solution.py:158
  24.5 5.7 %collective-permute-start.6 = (bf16[1600,128]{1,0:T(8,128)(2,1)S(1)}, bf16[1600,128]{1,0:T(8,128)(2,1)S(1)}, u32[]{:S(2)}, u32[]{:S(2)}) collective-permute-start(bf16[1600,128]{1,0:T(8,128)(2,1)S(1)} %collective-permute-done.4.refs_5_), channel_id=1, source_target_pairs={{0,7},{1,0},{2,1},{3,2},{4,3},{5,4},{6,5},{7,6},{8,15},{9,8},{10,9... | collective-permute-start | bytes 1228808 | tf_op jit(solution)/shard_map/ppermute | solution.py:158
  30.2 0.0 collective-permute-done.5.refs_6_
  30.2 1.9 %collective-permute-start.7 = (bf16[1600,128]{1,0:T(8,128)(2,1)S(1)}, bf16[1600,128]{1,0:T(8,128)(2,1)S(1)}, u32[]{:S(2)}, u32[]{:S(2)}) collective-permute-start(bf16[1600,128]{1,0:T(8,128)(2,1)S(1)} %collective-permute-done.5.refs_6_), channel_id=1, source_target_pairs={{0,1},{1,2},{2,3},{3,4},{4,5},{5,6},{6,7},{7,0},{8,9},{9,10},{10,1... | collective-permute-start | bytes 1228808 | tf_op jit(solution)/shard_map/ppermute | solution.py:158
  32.1 6.2 %collective-permute-start.2 = (f32[3,64,384]{2,1,0:T(8,128)S(1)}, f32[3,64,384]{2,1,0:T(8,128)S(1)}, u32[]{:S(2)}, u32[]{:S(2)}) collective-permute-start(f32[3,64,384]{2,1,0:T(8,128)S(1)} %get-tuple-element.27), channel_id=1, source_target_pairs={{8,0},{16,8},{24,16},{32,24},{40,32},{48,40},{56,48},{64,56},{72,6... | collective-permute-start | bytes 884744 | tf_op jit(solution)/shard_map/ppermute | solution.py:187
  38.4 5.9 %collective-permute-start.3 = (f32[3,64,384]{2,1,0:T(8,128)S(1)}, f32[3,64,384]{2,1,0:T(8,128)S(1)}, u32[]{:S(2)}, u32[]{:S(2)}) collective-permute-start(f32[3,64,384]{2,1,0:T(8,128)S(1)} %get-tuple-element.28), channel_id=1, source_target_pairs={{0,8},{8,16},{16,24},{24,32},{32,40},{40,48},{48,56},{56,64},{64,7... | collective-permute-start | bytes 884744 | tf_op jit(solution)/shard_map/ppermute | solution.py:188
  44.3 0.0 collective-permute-done.6.refs_7_
  44.3 4.9 %collective-permute-start.8 = (bf16[800,128]{1,0:T(8,128)(2,1)S(1)}, bf16[800,128]{1,0:T(8,128)(2,1)S(1)}, u32[]{:S(2)}, u32[]{:S(2)}) collective-permute-start(bf16[800,128]{1,0:T(8,128)(2,1)S(1)} %slice.8), channel_id=1, source_target_pairs={{0,7},{1,0},{2,1},{3,2},{4,3},{5,4},{6,5},{7,6},{8,15},{9,8},{10,9... | collective-permute-start | bytes 614408 | tf_op jit(solution)/shard_map/ppermute | solution.py:158
  49.2 0.0 collective-permute-done.7.refs_8_
  49.2 1.9 %collective-permute-start.9 = (bf16[800,128]{1,0:T(8,128)(2,1)S(1)}, bf16[800,128]{1,0:T(8,128)(2,1)S(1)}, u32[]{:S(2)}, u32[]{:S(2)}) collective-permute-start(bf16[800,128]{1,0:T(8,128)(2,1)S(1)} %slice.9), channel_id=1, source_target_pairs={{0,1},{1,2},{2,3},{3,4},{4,5},{5,6},{6,7},{7,0},{8,9},{9,10},{10,1... | collective-permute-start | bytes 614408 | tf_op jit(solution)/shard_map/ppermute | solution.py:158
  51.1 0.0 collective-permute-done.2.from_next
  51.1 0.0 collective-permute-done.3.from_prev
  51.1 0.2 shard_map.69.refs_0_
  51.3 1.4 %shard_map.71 = (f32[7,128,128]{2,1,0:T(8,128)S(1)}, f32[64,1536]{1,0:T(8,128)S(1)}) custom-call(bf16[1536,256]{1,0:T(8,128)(2,1)S(1)} %shard_map.69.refs_0_, f32[64,1536]{1,0:T(8,128)S(1)} %shard_map.70.refs_1_, bf16[1600,128]{1,0:T(8,128)(2,1)S(1)} %pad_maximum_fusion.own.refs_2_, bf16[1600,128]{1,0:T(8,128)(2,1)S(1)} %collective-permute-done.one.refs_3_, ...), custom_call_target="tpu_custom_call" | custom-call | tf_op jit(solution)/shard_map/pallas_call | solution.py:146
  52.7 0.0 collective-permute-done.8.refs_4_
  52.7 4.2 %collective-permute-done.9.refs_5_ = bf16[800,128]{1,0:T(8,128)(2,1)S(1)} collective-permute-done((bf16[800,128]{1,0:T(8,128)(2,1)S(1)}, bf16[800,128]{1,0:T(8,128)(2,1)S(1)}, u32[]{:S(2)}, u32[]{:S(2)}) %collective-permute-start.9) | collective-permute-done | bytes 204832 | tf_op jit(solution)/shard_map/ppermute | solution.py:158
  56.9 0.5 shard_map.72
  57.4 1.9 %collective-permute-start.10 = (f32[33,16,128]{2,1,0:T(8,128)S(1)}, f32[33,16,128]{2,1,0:T(8,128)S(1)}, u32[]{:S(2)}, u32[]{:S(2)}) collective-permute-start(f32[33,16,128]{2,1,0:T(8,128)S(1)} %get-tuple-element.37), channel_id=1, source_target_pairs={{0,8},{8,0},{1,9},{9,1},{2,10},{10,2},{3,11},{11,3},{4,12},{12,4},... | collective-permute-start | bytes 811016 | tf_op jit(solution)/shard_map/ppermute | solution.py:224
  59.3 1.5 %collective-permute-done.10.other = f32[33,16,128]{2,1,0:T(8,128)S(1)} collective-permute-done((f32[33,16,128]{2,1,0:T(8,128)S(1)}, f32[33,16,128]{2,1,0:T(8,128)S(1)}, u32[]{:S(2)}, u32[]{:S(2)}) %collective-permute-start.10) | collective-permute-done | bytes 270368 | tf_op jit(solution)/shard_map/ppermute | solution.py:224
  60.9 23.7 %all_to_all.5.refs_0_ = bf16[32,24,128]{2,1,0:T(8,128)(2,1)S(1)} all-to-all(bf16[32,24,128]{2,1,0:T(8,128)(2,1)S(1)} %shard_map.73), channel_id=1, replica_groups=mesh['x'=4,'z'=8,'core'=2,'y'=8] {'x','z'}, dimensions={0} | all-to-all | bytes 393216 | tf_op jit(solution)/shard_map/all_to_all | solution.py:226
  84.5 0.9 %shard_map.74 = (f32[16,128]{1,0:T(8,128)}, bf16[3,64,512]{2,1,0:T(8,128)(2,1)}) custom-call(bf16[32,24,128]{2,1,0:T(8,128)(2,1)S(1)} %all_to_all.5.refs_0_, f32[3,64,512]{2,1,0:T(8,128)S(1)} %get-tuple-element.39.refs_1_), custom_call_target="tpu_custom_call" | custom-call | tf_op jit(solution)/shard_map/pallas_call | solution.py:146
  (3 shorter events, 0.1 us)
Async XLA Ops:
  0.6 9.1 %copy-start.3 = (bf16[8,7,4096]{2,0,1:T(8,128)(2,1)S(1)}, bf16[8,7,4096]{2,0,1:T(8,128)(2,1)}, u32[]{:S(2)}) copy-start(bf16[8,7,4096]{2,0,1:T(8,128)(2,1)} %param.6) | copy-start | bytes 1376260
  1.7 9.0 %copy-start = (bf16[512,3,128]{2,0,1:T(8,128)(2,1)S(1)}, bf16[512,3,128]{2,0,1:T(8,128)(2,1)}, u32[]{:S(2)}) copy-start(bf16[512,3,128]{2,0,1:T(8,128)(2,1)} %param.5) | copy-start | bytes 1179652
  1.8 12.2 %collective-permute-start = (bf16[1600,128]{1,0:T(8,128)(2,1)S(1)}, bf16[1600,128]{1,0:T(8,128)(2,1)S(1)}, u32[]{:S(2)}, u32[]{:S(2)}) collective-permute-start(bf16[1600,128]{1,0:T(8,128)(2,1)S(1)} %pad_maximum_fusion.own.refs_2_), channel_id=1, source_target_pairs={{0,7},{1,0},{2,1},{3,2},{4,3},{5,4},{6,5},{7,6},{8,15},{9,8},{10,9... | collective-permute-start | bytes 1228808 | tf_op jit(solution)/shard_map/ppermute | solution.py:158
  7.8 11.5 %collective-permute-start.1 = (bf16[1600,128]{1,0:T(8,128)(2,1)S(1)}, bf16[1600,128]{1,0:T(8,128)(2,1)S(1)}, u32[]{:S(2)}, u32[]{:S(2)}) collective-permute-start(bf16[1600,128]{1,0:T(8,128)(2,1)S(1)} %pad_maximum_fusion.own.refs_2_), channel_id=1, source_target_pairs={{0,1},{1,2},{2,3},{3,4},{4,5},{5,6},{6,7},{7,0},{8,9},{9,10},{10,1... | collective-permute-start | bytes 1228808 | tf_op jit(solution)/shard_map/ppermute | solution.py:158
  9.8 1.0 %copy-start.2 = (f32[512]{0:T(512)S(1)}, f32[512]{0:T(512)}, u32[]{:S(2)}) copy-start(f32[512]{0:T(512)} %param.9) | copy-start | bytes 6148
  10.8 0.7 copy-start.1
  14.0 10.5 %collective-permute-start.4 = (bf16[1600,128]{1,0:T(8,128)(2,1)S(1)}, bf16[1600,128]{1,0:T(8,128)(2,1)S(1)}, u32[]{:S(2)}, u32[]{:S(2)}) collective-permute-start(bf16[1600,128]{1,0:T(8,128)(2,1)S(1)} %collective-permute-done.one.refs_3_), channel_id=1, source_target_pairs={{0,7},{1,0},{2,1},{3,2},{4,3},{5,4},{6,5},{7,6},{8,15},{9,8},{10,9... | collective-permute-start | bytes 1228808 | tf_op jit(solution)/shard_map/ppermute | solution.py:158
  19.3 10.9 %collective-permute-start.5 = (bf16[1600,128]{1,0:T(8,128)(2,1)S(1)}, bf16[1600,128]{1,0:T(8,128)(2,1)S(1)}, u32[]{:S(2)}, u32[]{:S(2)}) collective-permute-start(bf16[1600,128]{1,0:T(8,128)(2,1)S(1)} %collective-permute-done.1.two.refs_4_), channel_id=1, source_target_pairs={{0,1},{1,2},{2,3},{3,4},{4,5},{5,6},{6,7},{7,0},{8,9},{9,10},{10,1... | collective-permute-start | bytes 1228808 | tf_op jit(solution)/shard_map/ppermute | solution.py:158
  24.5 19.8 %collective-permute-start.6 = (bf16[1600,128]{1,0:T(8,128)(2,1)S(1)}, bf16[1600,128]{1,0:T(8,128)(2,1)S(1)}, u32[]{:S(2)}, u32[]{:S(2)}) collective-permute-start(bf16[1600,128]{1,0:T(8,128)(2,1)S(1)} %collective-permute-done.4.refs_5_), channel_id=1, source_target_pairs={{0,7},{1,0},{2,1},{3,2},{4,3},{5,4},{6,5},{7,6},{8,15},{9,8},{10,9... | collective-permute-start | bytes 1228808 | tf_op jit(solution)/shard_map/ppermute | solution.py:158
  30.2 18.9 %collective-permute-start.7 = (bf16[1600,128]{1,0:T(8,128)(2,1)S(1)}, bf16[1600,128]{1,0:T(8,128)(2,1)S(1)}, u32[]{:S(2)}, u32[]{:S(2)}) collective-permute-start(bf16[1600,128]{1,0:T(8,128)(2,1)S(1)} %collective-permute-done.5.refs_6_), channel_id=1, source_target_pairs={{0,1},{1,2},{2,3},{3,4},{4,5},{5,6},{6,7},{7,0},{8,9},{9,10},{10,1... | collective-permute-start | bytes 1228808 | tf_op jit(solution)/shard_map/ppermute | solution.py:158
  32.1 19.0 %collective-permute-start.2 = (f32[3,64,384]{2,1,0:T(8,128)S(1)}, f32[3,64,384]{2,1,0:T(8,128)S(1)}, u32[]{:S(2)}, u32[]{:S(2)}) collective-permute-start(f32[3,64,384]{2,1,0:T(8,128)S(1)} %get-tuple-element.27), channel_id=1, source_target_pairs={{8,0},{16,8},{24,16},{32,24},{40,32},{48,40},{56,48},{64,56},{72,6... | collective-permute-start | bytes 884744 | tf_op jit(solution)/shard_map/ppermute | solution.py:187
  38.4 12.7 %collective-permute-start.3 = (f32[3,64,384]{2,1,0:T(8,128)S(1)}, f32[3,64,384]{2,1,0:T(8,128)S(1)}, u32[]{:S(2)}, u32[]{:S(2)}) collective-permute-start(f32[3,64,384]{2,1,0:T(8,128)S(1)} %get-tuple-element.28), channel_id=1, source_target_pairs={{0,8},{8,16},{16,24},{24,32},{32,40},{40,48},{48,56},{56,64},{64,7... | collective-permute-start | bytes 884744 | tf_op jit(solution)/shard_map/ppermute | solution.py:188
  44.3 8.4 %collective-permute-start.8 = (bf16[800,128]{1,0:T(8,128)(2,1)S(1)}, bf16[800,128]{1,0:T(8,128)(2,1)S(1)}, u32[]{:S(2)}, u32[]{:S(2)}) collective-permute-start(bf16[800,128]{1,0:T(8,128)(2,1)S(1)} %slice.8), channel_id=1, source_target_pairs={{0,7},{1,0},{2,1},{3,2},{4,3},{5,4},{6,5},{7,6},{8,15},{9,8},{10,9... | collective-permute-start | bytes 614408 | tf_op jit(solution)/shard_map/ppermute | solution.py:158
  49.2 7.7 %collective-permute-start.9 = (bf16[800,128]{1,0:T(8,128)(2,1)S(1)}, bf16[800,128]{1,0:T(8,128)(2,1)S(1)}, u32[]{:S(2)}, u32[]{:S(2)}) collective-permute-start(bf16[800,128]{1,0:T(8,128)(2,1)S(1)} %slice.9), channel_id=1, source_target_pairs={{0,1},{1,2},{2,3},{3,4},{4,5},{5,6},{6,7},{7,0},{8,9},{9,10},{10,1... | collective-permute-start | bytes 614408 | tf_op jit(solution)/shard_map/ppermute | solution.py:158
  57.4 3.4 %collective-permute-start.10 = (f32[33,16,128]{2,1,0:T(8,128)S(1)}, f32[33,16,128]{2,1,0:T(8,128)S(1)}, u32[]{:S(2)}, u32[]{:S(2)}) collective-permute-start(f32[33,16,128]{2,1,0:T(8,128)S(1)} %get-tuple-element.37), channel_id=1, source_target_pairs={{0,8},{8,0},{1,9},{9,1},{2,10},{10,2},{3,11},{11,3},{4,12},{12,4},... | collective-permute-start | bytes 811016 | tf_op jit(solution)/shard_map/ppermute | solution.py:224

commit v6 on v5

--- a/solution.py
+++ b/solution.py
@@ -99,10 +99,11 @@
     row = jnp.sum(jnp.where(lane % MODES == k, column, 0.0), axis=0, keepdims=True)
     norm_out[...] = jnp.broadcast_to(row, (SLOT - OWN, TILE))
     other[NSPACE // NC] = jnp.broadcast_to(row, (OWN, TILE))
+    turn = 1 - 2 * lax.rem(me, 2)
     steps = near + [4]
     first = lax.axis_index("core") == 0
     for i, step in enumerate(steps):
-        source = lax.rem(me + step, NY)
+        source = lax.rem(me + step * turn + NY, NY)
         part = early[i] if i < len(near) else product
         for o in range(TILE // OWN // NC):
             one = part[2 * o * OWN : (2 * o + 1) * OWN]
@@ -154,8 +155,9 @@
     return result[0] if single else result
 
 
-def shift(value, step):
-    return lax.ppermute(value, "y", [(i, (i + step) % NY) for i in range(NY)])
+def swap(value, first):
+    pairs = [(i, (i + 1) % NY) for i in range(first, NY, 2)]
+    return lax.ppermute(value, "y", pairs + [(j, i) for i, j in pairs])
 
 
 def local(snapshots, mass_blocks, block_cols, coefficients, lumped):
@@ -167,8 +169,8 @@
 
     mass = mass_blocks.reshape(blocks, BPR, BLOCK, BLOCK).transpose(1, 0, 2, 3)
     up, down = [tile], [tile]
-    up.append(shift(tile, -1))
-    down.append(shift(tile, 1))
+    up.append(swap(tile, 0))
+    down.append(swap(tile, 1))
     edge = ((REACH, BLOCK, 3 * TILE), F32)
     low, mid, high, weight = call(
         dual_kernel,
@@ -181,19 +183,19 @@
         smem=1,
     )
     first, low, high = lax.optimization_barrier((up[1], low, high))
-    up.append(shift(first, -1))
-    down.append(shift(down[1], 1))
+    down.append(swap(first, 1))
+    up.append(swap(down[1], 0))
     low, high, down[1] = lax.optimization_barrier((low, high, down[1]))
     from_next = lax.ppermute(low, SPACE, [(i + 1, i) for i in range(NSPACE - 1)])
     from_prev = lax.ppermute(high, SPACE, [(i, i + 1) for i in range(NSPACE - 1)])
     raw = call(first_kernel, ((MODES, 3 * nodes), F32), tile, up[1], down[1])
-    second, raw = lax.optimization_barrier((up[2], raw))
-    up.append(shift(second, -1))
-    down.append(shift(down[2], 1))
+    second, raw = lax.optimization_barrier((down[2], raw))
+    up.append(swap(second, 0))
+    down.append(swap(up[2], 1))
     dual = call(join_kernel, ((3 * nodes, 2 * TILE), BF16), mid, from_next, from_prev)
 
-    half_a = shift(up[3][:cut], -1)
-    half_b = shift(down[3][cut:], 1)
+    half_a = swap(down[3][:cut], 0)
+    half_b = swap(up[3][cut:], 1)
 
     near = [0, 1, NY - 1, 2, NY - 2, 3, NY - 3]
     early, raw = call(

time: 86.5 us -> 83.4 us (0.964)
  starting transfers between devices: 43.6 us -> 40.5 us
  blocking collectives: 23.7 us -> 21.2 us
  waiting for transfers between devices: 9.11 us -> 11.4 us
    ppermute x8, waiting for transfers between devices: 7.59 us -> 10.2 us  [swap(): return lax.ppermute(value, 'y', pairs + [(j, i) for i, j in pairs])]
    all_to_all x1, blocking collectives: 23.7 us -> 21.2 us  [local(): lax.all_to_all(slots, ('x', 'z'), split_axis=0, concat_axis=0, tiled=True)]
    ppermute x1, starting transfers between devices: 6.24 us -> 4.79 us  [local(): lax.ppermute(low, SPACE, [(i + 1, i) for i in range(NSPACE - 1)])]
    ppermute x1, starting transfers between devices: 5.87 us -> 4.57 us  [local(): lax.ppermute(high, SPACE, [(i, i + 1) for i in range(NSPACE - 1)])]
  transfers between devices with their start and end apart: 11 -> 11, of which waited for: 4 -> 5; matrix products, arithmetic and copies ran while one was open for 1% -> 1% of each run, Pallas kernels for 5% -> 5%
where the time goes in v6:
time: 83.4 us; the launch traced here: 82 us
  starting transfers between devices  40.5 us (49%)
  blocking collectives  21.2 us (25%)
  waiting for transfers between devices  11.4 us (14%)
  Pallas kernels  5.32 us (6%)
  local copies, waits for them, and re-layouts  1.7 us (2%)
  other arithmetic  1.1 us (1%)
  between operations  0.88 us (1%)
    ppermute x8, starting transfers between devices, swap(): return lax.ppermute(value, 'y', pairs + [(j, i) for i, j in pairs])  28.7 us
    all_to_all x1, blocking collectives, local(): lax.all_to_all(slots, ('x', 'z'), split_axis=0, concat_axis=0, tiled=True)  21.2 us
    ppermute x8, waiting for transfers between devices, swap(): return lax.ppermute(value, 'y', pairs + [(j, i) for i, j in pairs])  10.2 us
    pallas_call x7, Pallas kernels, call(): pl.pallas_call(kernel, out_shape=[jax.ShapeDtypeStruct(*s) for s in outs]...  5.32 us
    ppermute x1, starting transfers between devices, local(): lax.ppermute(low, SPACE, [(i + 1, i) for i in range(NSPACE - 1)])  4.79 us
    ppermute x1, starting transfers between devices, local(): lax.ppermute(high, SPACE, [(i, i + 1) for i in range(NSPACE - 1)])  4.57 us
    ppermute x1, starting transfers between devices, local(): other = lax.ppermute(other, 'core', [(0, 1), (1, 0)])  2.41 us
  transfers between devices with their start and end apart: 11, of which 5 were waited for; matrix products, arithmetic and copies ran while one was open for 1% of the time, Pallas kernels for 5%

profile of v6, /device:TPU:1, one launch (start us, length us, event | category | flops | bytes accessed | tf_op | source)
XLA Modules:
  0.0 82.0 jit_solution(11738088902946053081)
XLA Ops:
  0.6 0.0 copy-start.3
  0.6 1.1 %pad_maximum_fusion.own.refs_2_ = bf16[1600,128]{1,0:T(8,128)(2,1)S(1)} fusion(bf16[64,128]{1,0:T(8,128)(2,1)} %bitcast.14, bf16[1536,128]{1,0:T(8,128)(2,1)} %bitcast.11), kind=kLoop, calls=%fused_computation | loop fusion | flops 819200 | bytes 819200 | tf_op jit(solution)/shard_map/concatenate | solution.py:167
  1.7 0.0 copy-start
  1.8 4.2 %collective-permute-start = (bf16[1600,128]{1,0:T(8,128)(2,1)S(1)}, bf16[1600,128]{1,0:T(8,128)(2,1)S(1)}, u32[]{:S(2)}, u32[]{:S(2)}) collective-permute-start(bf16[1600,128]{1,0:T(8,128)(2,1)S(1)} %pad_maximum_fusion.own.refs_2_), channel_id=1, source_target_pairs={{0,1},{2,3},{4,5},{6,7},{1,0},{3,2},{5,4},{7,6},{8,9},{10,11},{12,... | collective-permute-start | bytes 1228808 | tf_op jit(solution)/shard_map/ppermute | solution.py:160
  5.9 4.9 %collective-permute-start.1 = (bf16[1600,128]{1,0:T(8,128)(2,1)S(1)}, bf16[1600,128]{1,0:T(8,128)(2,1)S(1)}, u32[]{:S(2)}, u32[]{:S(2)}) collective-permute-start(bf16[1600,128]{1,0:T(8,128)(2,1)S(1)} %pad_maximum_fusion.own.refs_2_), channel_id=1, source_target_pairs={{1,2},{3,4},{5,6},{7,0},{2,1},{4,3},{6,5},{0,7},{9,10},{11,12},{13... | collective-permute-start | bytes 1228808 | tf_op jit(solution)/shard_map/ppermute | solution.py:160
  10.8 0.0 copy-done.3
  10.8 0.0 copy-start.2
  10.8 1.0 %reshape.13 = bf16[8,7,64,64]{3,2,0,1:T(8,128)(2,1)S(1)} reshape(bf16[8,7,4096]{2,0,1:T(8,128)(2,1)S(1)} %copy-done.3) | data formatting | bytes 917504 | tf_op jit(solution)/shard_map/reshape | solution.py:170
  11.8 0.0 copy-start.1
  11.8 0.0 copy-done
  11.8 0.0 copy-done.2
  11.9 0.7 copy-done.1
  12.5 1.8 %shard_map.68 = (f32[3,64,384]{2,1,0:T(8,128)S(1)}, f32[8,64,384]{2,1,0:T(8,128)S(1)}, f32[3,64,384]{2,1,0:T(8,128)S(1)}, f32[1,512]{1,0:T(1,128)S(1)}) custom-call(s32[8,7]{1,0:T(8,128)S(1)} %copy-done.1, bf16[7,8,64,64]{3,2,1,0:T(8,128)(2,1)S(1)} %bitcast.10, bf16[3,512,128]{2,1,0:T(8,128)(2,1)S(1)} %bitcast.12, f32[1,512]{1,0:T(1,128)S(1)} %bitcast.13), custom_call_target="tpu_custom_call" | custom-call | tf_op jit(solution)/shard_map/pallas_call | solution.py:147
  14.3 0.0 collective-permute-done.one.refs_3_
  14.4 5.7 %collective-permute-start.4 = (bf16[1600,128]{1,0:T(8,128)(2,1)S(1)}, bf16[1600,128]{1,0:T(8,128)(2,1)S(1)}, u32[]{:S(2)}, u32[]{:S(2)}) collective-permute-start(bf16[1600,128]{1,0:T(8,128)(2,1)S(1)} %collective-permute-done.one.refs_3_), channel_id=1, source_target_pairs={{1,2},{3,4},{5,6},{7,0},{2,1},{4,3},{6,5},{0,7},{9,10},{11,12},{13... | collective-permute-start | bytes 1228808 | tf_op jit(solution)/shard_map/ppermute | solution.py:160
  20.0 0.0 collective-permute-done.1.two.refs_4_
  20.0 1.9 %collective-permute-start.5 = (bf16[1600,128]{1,0:T(8,128)(2,1)S(1)}, bf16[1600,128]{1,0:T(8,128)(2,1)S(1)}, u32[]{:S(2)}, u32[]{:S(2)}) collective-permute-start(bf16[1600,128]{1,0:T(8,128)(2,1)S(1)} %collective-permute-done.1.two.refs_4_), channel_id=1, source_target_pairs={{0,1},{2,3},{4,5},{6,7},{1,0},{3,2},{5,4},{7,6},{8,9},{10,11},{12,... | collective-permute-start | bytes 1228808 | tf_op jit(solution)/shard_map/ppermute | solution.py:160
  22.0 0.5 shard_map.70.refs_1_
  22.5 4.7 %collective-permute-done.4.refs_6_ = bf16[1600,128]{1,0:T(8,128)(2,1)S(1)} collective-permute-done((bf16[1600,128]{1,0:T(8,128)(2,1)S(1)}, bf16[1600,128]{1,0:T(8,128)(2,1)S(1)}, u32[]{:S(2)}, u32[]{:S(2)}) %collective-permute-start.4) | collective-permute-done | bytes 409632 | tf_op jit(solution)/shard_map/ppermute | solution.py:160
  27.2 3.7 %collective-permute-start.6 = (bf16[1600,128]{1,0:T(8,128)(2,1)S(1)}, bf16[1600,128]{1,0:T(8,128)(2,1)S(1)}, u32[]{:S(2)}, u32[]{:S(2)}) collective-permute-start(bf16[1600,128]{1,0:T(8,128)(2,1)S(1)} %collective-permute-done.4.refs_6_), channel_id=1, source_target_pairs={{0,1},{2,3},{4,5},{6,7},{1,0},{3,2},{5,4},{7,6},{8,9},{10,11},{12,... | collective-permute-start | bytes 1228808 | tf_op jit(solution)/shard_map/ppermute | solution.py:160
  31.0 0.1 collective-permute-done.5.refs_5_
  31.1 3.4 %collective-permute-start.7 = (bf16[1600,128]{1,0:T(8,128)(2,1)S(1)}, bf16[1600,128]{1,0:T(8,128)(2,1)S(1)}, u32[]{:S(2)}, u32[]{:S(2)}) collective-permute-start(bf16[1600,128]{1,0:T(8,128)(2,1)S(1)} %collective-permute-done.5.refs_5_), channel_id=1, source_target_pairs={{1,2},{3,4},{5,6},{7,0},{2,1},{4,3},{6,5},{0,7},{9,10},{11,12},{13... | collective-permute-start | bytes 1228808 | tf_op jit(solution)/shard_map/ppermute | solution.py:160
  34.5 4.8 %collective-permute-start.2 = (f32[3,64,384]{2,1,0:T(8,128)S(1)}, f32[3,64,384]{2,1,0:T(8,128)S(1)}, u32[]{:S(2)}, u32[]{:S(2)}) collective-permute-start(f32[3,64,384]{2,1,0:T(8,128)S(1)} %get-tuple-element.27), channel_id=1, source_target_pairs={{8,0},{16,8},{24,16},{32,24},{40,32},{48,40},{56,48},{64,56},{72,6... | collective-permute-start | bytes 884744 | tf_op jit(solution)/shard_map/ppermute | solution.py:189
  39.3 4.6 %collective-permute-start.3 = (f32[3,64,384]{2,1,0:T(8,128)S(1)}, f32[3,64,384]{2,1,0:T(8,128)S(1)}, u32[]{:S(2)}, u32[]{:S(2)}) collective-permute-start(f32[3,64,384]{2,1,0:T(8,128)S(1)} %get-tuple-element.28), channel_id=1, source_target_pairs={{0,8},{8,16},{16,24},{24,32},{32,40},{40,48},{48,56},{56,64},{64,7... | collective-permute-start | bytes 884744 | tf_op jit(solution)/shard_map/ppermute | solution.py:190
  43.9 0.0 collective-permute-done.6.refs_7_
  43.9 3.1 %collective-permute-start.9 = (bf16[800,128]{1,0:T(8,128)(2,1)S(1)}, bf16[800,128]{1,0:T(8,128)(2,1)S(1)}, u32[]{:S(2)}, u32[]{:S(2)}) collective-permute-start(bf16[800,128]{1,0:T(8,128)(2,1)S(1)} %slice.9), channel_id=1, source_target_pairs={{1,2},{3,4},{5,6},{7,0},{2,1},{4,3},{6,5},{0,7},{9,10},{11,12},{13... | collective-permute-start | bytes 614408 | tf_op jit(solution)/shard_map/ppermute | solution.py:160
  47.0 0.0 collective-permute-done.7.refs_8_
  47.0 1.9 %collective-permute-start.8 = (bf16[800,128]{1,0:T(8,128)(2,1)S(1)}, bf16[800,128]{1,0:T(8,128)(2,1)S(1)}, u32[]{:S(2)}, u32[]{:S(2)}) collective-permute-start(bf16[800,128]{1,0:T(8,128)(2,1)S(1)} %slice.8), channel_id=1, source_target_pairs={{0,1},{2,3},{4,5},{6,7},{1,0},{3,2},{5,4},{7,6},{8,9},{10,11},{12,... | collective-permute-start | bytes 614408 | tf_op jit(solution)/shard_map/ppermute | solution.py:160
  48.9 0.0 collective-permute-done.2.from_next
  48.9 0.0 collective-permute-done.3.from_prev
  49.0 0.2 shard_map.69.refs_0_
  49.1 1.4 %shard_map.71 = (f32[7,128,128]{2,1,0:T(8,128)S(1)}, f32[64,1536]{1,0:T(8,128)S(1)}) custom-call(bf16[1536,256]{1,0:T(8,128)(2,1)S(1)} %shard_map.69.refs_0_, f32[64,1536]{1,0:T(8,128)S(1)} %shard_map.70.refs_1_, bf16[1600,128]{1,0:T(8,128)(2,1)S(1)} %pad_maximum_fusion.own.refs_2_, bf16[1600,128]{1,0:T(8,128)(2,1)S(1)} %collective-permute-done.one.refs_3_, ...), custom_call_target="tpu_custom_call" | custom-call | tf_op jit(solution)/shard_map/pallas_call | solution.py:147
  50.5 2.5 %collective-permute-done.9.refs_5_ = bf16[800,128]{1,0:T(8,128)(2,1)S(1)} collective-permute-done((bf16[800,128]{1,0:T(8,128)(2,1)S(1)}, bf16[800,128]{1,0:T(8,128)(2,1)S(1)}, u32[]{:S(2)}, u32[]{:S(2)}) %collective-permute-start.9) | collective-permute-done | bytes 204832 | tf_op jit(solution)/shard_map/ppermute | solution.py:160
  53.0 2.9 %collective-permute-done.8.refs_4_ = bf16[800,128]{1,0:T(8,128)(2,1)S(1)} collective-permute-done((bf16[800,128]{1,0:T(8,128)(2,1)S(1)}, bf16[800,128]{1,0:T(8,128)(2,1)S(1)}, u32[]{:S(2)}, u32[]{:S(2)}) %collective-permute-start.8) | collective-permute-done | bytes 204832 | tf_op jit(solution)/shard_map/ppermute | solution.py:160
  55.9 0.5 shard_map.72
  56.4 2.4 %collective-permute-start.10 = (f32[33,16,128]{2,1,0:T(8,128)S(1)}, f32[33,16,128]{2,1,0:T(8,128)S(1)}, u32[]{:S(2)}, u32[]{:S(2)}) collective-permute-start(f32[33,16,128]{2,1,0:T(8,128)S(1)} %get-tuple-element.37), channel_id=1, source_target_pairs={{0,8},{8,0},{1,9},{9,1},{2,10},{10,2},{3,11},{11,3},{4,12},{12,4},... | collective-permute-start | bytes 811016 | tf_op jit(solution)/shard_map/ppermute | solution.py:226
  58.8 1.2 %collective-permute-done.10.other = f32[33,16,128]{2,1,0:T(8,128)S(1)} collective-permute-done((f32[33,16,128]{2,1,0:T(8,128)S(1)}, f32[33,16,128]{2,1,0:T(8,128)S(1)}, u32[]{:S(2)}, u32[]{:S(2)}) %collective-permute-start.10) | collective-permute-done | bytes 270368 | tf_op jit(solution)/shard_map/ppermute | solution.py:226
  60.0 21.2 %all_to_all.5.refs_0_ = bf16[32,24,128]{2,1,0:T(8,128)(2,1)S(1)} all-to-all(bf16[32,24,128]{2,1,0:T(8,128)(2,1)S(1)} %shard_map.73), channel_id=1, replica_groups=mesh['x'=4,'z'=8,'core'=2,'y'=8] {'x','z'}, dimensions={0} | all-to-all | bytes 393216 | tf_op jit(solution)/shard_map/all_to_all | solution.py:228
  81.1 0.9 %shard_map.74 = (f32[16,128]{1,0:T(8,128)}, bf16[3,64,512]{2,1,0:T(8,128)(2,1)}) custom-call(bf16[32,24,128]{2,1,0:T(8,128)(2,1)S(1)} %all_to_all.5.refs_0_, f32[3,64,512]{2,1,0:T(8,128)S(1)} %get-tuple-element.39.refs_1_), custom_call_target="tpu_custom_call" | custom-call | tf_op jit(solution)/shard_map/pallas_call | solution.py:147
  (3 shorter events, 0.1 us)
Async XLA Ops:
  0.6 10.2 %copy-start.3 = (bf16[8,7,4096]{2,0,1:T(8,128)(2,1)S(1)}, bf16[8,7,4096]{2,0,1:T(8,128)(2,1)}, u32[]{:S(2)}) copy-start(bf16[8,7,4096]{2,0,1:T(8,128)(2,1)} %param.6) | copy-start | bytes 1376260
  1.7 10.1 %copy-start = (bf16[512,3,128]{2,0,1:T(8,128)(2,1)S(1)}, bf16[512,3,128]{2,0,1:T(8,128)(2,1)}, u32[]{:S(2)}) copy-start(bf16[512,3,128]{2,0,1:T(8,128)(2,1)} %param.5) | copy-start | bytes 1179652
  1.8 12.6 %collective-permute-start = (bf16[1600,128]{1,0:T(8,128)(2,1)S(1)}, bf16[1600,128]{1,0:T(8,128)(2,1)S(1)}, u32[]{:S(2)}, u32[]{:S(2)}) collective-permute-start(bf16[1600,128]{1,0:T(8,128)(2,1)S(1)} %pad_maximum_fusion.own.refs_2_), channel_id=1, source_target_pairs={{0,1},{2,3},{4,5},{6,7},{1,0},{3,2},{5,4},{7,6},{8,9},{10,11},{12,... | collective-permute-start | bytes 1228808 | tf_op jit(solution)/shard_map/ppermute | solution.py:160
  5.9 14.1 %collective-permute-start.1 = (bf16[1600,128]{1,0:T(8,128)(2,1)S(1)}, bf16[1600,128]{1,0:T(8,128)(2,1)S(1)}, u32[]{:S(2)}, u32[]{:S(2)}) collective-permute-start(bf16[1600,128]{1,0:T(8,128)(2,1)S(1)} %pad_maximum_fusion.own.refs_2_), channel_id=1, source_target_pairs={{1,2},{3,4},{5,6},{7,0},{2,1},{4,3},{6,5},{0,7},{9,10},{11,12},{13... | collective-permute-start | bytes 1228808 | tf_op jit(solution)/shard_map/ppermute | solution.py:160
  10.8 1.0 %copy-start.2 = (f32[512]{0:T(512)S(1)}, f32[512]{0:T(512)}, u32[]{:S(2)}) copy-start(f32[512]{0:T(512)} %param.9) | copy-start | bytes 6148
  11.8 0.7 copy-start.1
  14.4 12.9 %collective-permute-start.4 = (bf16[1600,128]{1,0:T(8,128)(2,1)S(1)}, bf16[1600,128]{1,0:T(8,128)(2,1)S(1)}, u32[]{:S(2)}, u32[]{:S(2)}) collective-permute-start(bf16[1600,128]{1,0:T(8,128)(2,1)S(1)} %collective-permute-done.one.refs_3_), channel_id=1, source_target_pairs={{1,2},{3,4},{5,6},{7,0},{2,1},{4,3},{6,5},{0,7},{9,10},{11,12},{13... | collective-permute-start | bytes 1228808 | tf_op jit(solution)/shard_map/ppermute | solution.py:160
  20.0 11.0 %collective-permute-start.5 = (bf16[1600,128]{1,0:T(8,128)(2,1)S(1)}, bf16[1600,128]{1,0:T(8,128)(2,1)S(1)}, u32[]{:S(2)}, u32[]{:S(2)}) collective-permute-start(bf16[1600,128]{1,0:T(8,128)(2,1)S(1)} %collective-permute-done.1.two.refs_4_), channel_id=1, source_target_pairs={{0,1},{2,3},{4,5},{6,7},{1,0},{3,2},{5,4},{7,6},{8,9},{10,11},{12,... | collective-permute-start | bytes 1228808 | tf_op jit(solution)/shard_map/ppermute | solution.py:160
  27.2 16.6 %collective-permute-start.6 = (bf16[1600,128]{1,0:T(8,128)(2,1)S(1)}, bf16[1600,128]{1,0:T(8,128)(2,1)S(1)}, u32[]{:S(2)}, u32[]{:S(2)}) collective-permute-start(bf16[1600,128]{1,0:T(8,128)(2,1)S(1)} %collective-permute-done.4.refs_6_), channel_id=1, source_target_pairs={{0,1},{2,3},{4,5},{6,7},{1,0},{3,2},{5,4},{7,6},{8,9},{10,11},{12,... | collective-permute-start | bytes 1228808 | tf_op jit(solution)/shard_map/ppermute | solution.py:160
  31.1 15.9 %collective-permute-start.7 = (bf16[1600,128]{1,0:T(8,128)(2,1)S(1)}, bf16[1600,128]{1,0:T(8,128)(2,1)S(1)}, u32[]{:S(2)}, u32[]{:S(2)}) collective-permute-start(bf16[1600,128]{1,0:T(8,128)(2,1)S(1)} %collective-permute-done.5.refs_5_), channel_id=1, source_target_pairs={{1,2},{3,4},{5,6},{7,0},{2,1},{4,3},{6,5},{0,7},{9,10},{11,12},{13... | collective-permute-start | bytes 1228808 | tf_op jit(solution)/shard_map/ppermute | solution.py:160
  34.5 14.5 %collective-permute-start.2 = (f32[3,64,384]{2,1,0:T(8,128)S(1)}, f32[3,64,384]{2,1,0:T(8,128)S(1)}, u32[]{:S(2)}, u32[]{:S(2)}) collective-permute-start(f32[3,64,384]{2,1,0:T(8,128)S(1)} %get-tuple-element.27), channel_id=1, source_target_pairs={{8,0},{16,8},{24,16},{32,24},{40,32},{48,40},{56,48},{64,56},{72,6... | collective-permute-start | bytes 884744 | tf_op jit(solution)/shard_map/ppermute | solution.py:189
  39.3 9.7 %collective-permute-start.3 = (f32[3,64,384]{2,1,0:T(8,128)S(1)}, f32[3,64,384]{2,1,0:T(8,128)S(1)}, u32[]{:S(2)}, u32[]{:S(2)}) collective-permute-start(f32[3,64,384]{2,1,0:T(8,128)S(1)} %get-tuple-element.28), channel_id=1, source_target_pairs={{0,8},{8,16},{16,24},{24,32},{32,40},{40,48},{48,56},{56,64},{64,7... | collective-permute-start | bytes 884744 | tf_op jit(solution)/shard_map/ppermute | solution.py:190
  43.9 9.1 %collective-permute-start.9 = (bf16[800,128]{1,0:T(8,128)(2,1)S(1)}, bf16[800,128]{1,0:T(8,128)(2,1)S(1)}, u32[]{:S(2)}, u32[]{:S(2)}) collective-permute-start(bf16[800,128]{1,0:T(8,128)(2,1)S(1)} %slice.9), channel_id=1, source_target_pairs={{1,2},{3,4},{5,6},{7,0},{2,1},{4,3},{6,5},{0,7},{9,10},{11,12},{13... | collective-permute-start | bytes 614408 | tf_op jit(solution)/shard_map/ppermute | solution.py:160
  47.0 8.9 %collective-permute-start.8 = (bf16[800,128]{1,0:T(8,128)(2,1)S(1)}, bf16[800,128]{1,0:T(8,128)(2,1)S(1)}, u32[]{:S(2)}, u32[]{:S(2)}) collective-permute-start(bf16[800,128]{1,0:T(8,128)(2,1)S(1)} %slice.8), channel_id=1, source_target_pairs={{0,1},{2,3},{4,5},{6,7},{1,0},{3,2},{5,4},{7,6},{8,9},{10,11},{12,... | collective-permute-start | bytes 614408 | tf_op jit(solution)/shard_map/ppermute | solution.py:160
  56.4 3.6 %collective-permute-start.10 = (f32[33,16,128]{2,1,0:T(8,128)S(1)}, f32[33,16,128]{2,1,0:T(8,128)S(1)}, u32[]{:S(2)}, u32[]{:S(2)}) collective-permute-start(f32[33,16,128]{2,1,0:T(8,128)S(1)} %get-tuple-element.37), channel_id=1, source_target_pairs={{0,8},{8,0},{1,9},{9,1},{2,10},{10,2},{3,11},{11,3},{4,12},{12,4},... | collective-permute-start | bytes 811016 | tf_op jit(solution)/shard_map/ppermute | solution.py:226

commit v7 on v6

--- a/solution.py
+++ b/solution.py
@@ -165,7 +165,7 @@
     blocks = nodes // BLOCK
     own = jnp.transpose(snapshots, (1, 0, 2))
     tile = jnp.concatenate([own.reshape(3 * nodes, TILE), coefficients.T], axis=0)
-    cut = tile.shape[0] // 2
+    cut = tile.shape[0] * 2 // 5
 
     mass = mass_blocks.reshape(blocks, BPR, BLOCK, BLOCK).transpose(1, 0, 2, 3)
     up, down = [tile], [tile]

time: 83.4 us -> 82.5 us (0.989)
  waiting for transfers between devices: 11.4 us -> 10.5 us
    ppermute x8, waiting for transfers between devices: 10.2 us -> 9.33 us  [swap(): return lax.ppermute(value, 'y', pairs + [(j, i) for i, j in pairs])]
  transfers between devices with their start and end apart: 11 -> 11, of which waited for: 5 -> 4; matrix products, arithmetic and copies ran while one was open for 1% -> 1% of each run, Pallas kernels for 5% -> 5%
where the time goes in v7:
time: 82.5 us; the launch traced here: 81.2 us
  starting transfers between devices  40.5 us (49%)
  blocking collectives  21.2 us (26%)
  waiting for transfers between devices  10.5 us (13%)
  Pallas kernels  5.31 us (6%)
  local copies, waits for them, and re-layouts  1.7 us (2%)
  other arithmetic  1.1 us (1%)
  between operations  0.88 us (1%)
    ppermute x8, starting transfers between devices, swap(): return lax.ppermute(value, 'y', pairs + [(j, i) for i, j in pairs])  28.7 us
    all_to_all x1, blocking collectives, local(): lax.all_to_all(slots, ('x', 'z'), split_axis=0, concat_axis=0, tiled=True)  21.2 us
    ppermute x8, waiting for transfers between devices, swap(): return lax.ppermute(value, 'y', pairs + [(j, i) for i, j in pairs])  9.33 us
    pallas_call x7, Pallas kernels, call(): pl.pallas_call(kernel, out_shape=[jax.ShapeDtypeStruct(*s) for s in outs]...  5.31 us
    ppermute x1, starting transfers between devices, local(): lax.ppermute(low, SPACE, [(i + 1, i) for i in range(NSPACE - 1)])  4.79 us
    ppermute x1, starting transfers between devices, local(): lax.ppermute(high, SPACE, [(i, i + 1) for i in range(NSPACE - 1)])  4.57 us
    ppermute x1, starting transfers between devices, local(): other = lax.ppermute(other, 'core', [(0, 1), (1, 0)])  2.41 us
  transfers between devices with their start and end apart: 11, of which 4 were waited for; matrix products, arithmetic and copies ran while one was open for 1% of the time, Pallas kernels for 5%

profile of v7, /device:TPU:1, one launch (start us, length us, event | category | flops | bytes accessed | tf_op | source)
XLA Modules:
  0.0 81.2 jit_solution(13211935448869324107)
XLA Ops:
  0.6 0.0 copy-start.3
  0.6 1.1 %pad_maximum_fusion.own.refs_2_ = bf16[1600,128]{1,0:T(8,128)(2,1)S(1)} fusion(bf16[64,128]{1,0:T(8,128)(2,1)} %bitcast.14, bf16[1536,128]{1,0:T(8,128)(2,1)} %bitcast.11), kind=kLoop, calls=%fused_computation | loop fusion | flops 819200 | bytes 819200 | tf_op jit(solution)/shard_map/concatenate | solution.py:167
  1.7 0.0 copy-start
  1.8 4.2 %collective-permute-start = (bf16[1600,128]{1,0:T(8,128)(2,1)S(1)}, bf16[1600,128]{1,0:T(8,128)(2,1)S(1)}, u32[]{:S(2)}, u32[]{:S(2)}) collective-permute-start(bf16[1600,128]{1,0:T(8,128)(2,1)S(1)} %pad_maximum_fusion.own.refs_2_), channel_id=1, source_target_pairs={{0,1},{2,3},{4,5},{6,7},{1,0},{3,2},{5,4},{7,6},{8,9},{10,11},{12,... | collective-permute-start | bytes 1228808 | tf_op jit(solution)/shard_map/ppermute | solution.py:160
  5.9 4.9 %collective-permute-start.1 = (bf16[1600,128]{1,0:T(8,128)(2,1)S(1)}, bf16[1600,128]{1,0:T(8,128)(2,1)S(1)}, u32[]{:S(2)}, u32[]{:S(2)}) collective-permute-start(bf16[1600,128]{1,0:T(8,128)(2,1)S(1)} %pad_maximum_fusion.own.refs_2_), channel_id=1, source_target_pairs={{1,2},{3,4},{5,6},{7,0},{2,1},{4,3},{6,5},{0,7},{9,10},{11,12},{13... | collective-permute-start | bytes 1228808 | tf_op jit(solution)/shard_map/ppermute | solution.py:160
  10.8 0.0 copy-done.3
  10.8 0.0 copy-start.2
  10.8 1.0 %reshape.13 = bf16[8,7,64,64]{3,2,0,1:T(8,128)(2,1)S(1)} reshape(bf16[8,7,4096]{2,0,1:T(8,128)(2,1)S(1)} %copy-done.3) | data formatting | bytes 917504 | tf_op jit(solution)/shard_map/reshape | solution.py:170
  11.8 0.0 copy-start.1
  11.8 0.0 copy-done
  11.8 0.0 copy-done.2
  11.9 0.7 copy-done.1
  12.5 1.8 %shard_map.68 = (f32[3,64,384]{2,1,0:T(8,128)S(1)}, f32[8,64,384]{2,1,0:T(8,128)S(1)}, f32[3,64,384]{2,1,0:T(8,128)S(1)}, f32[1,512]{1,0:T(1,128)S(1)}) custom-call(s32[8,7]{1,0:T(8,128)S(1)} %copy-done.1, bf16[7,8,64,64]{3,2,1,0:T(8,128)(2,1)S(1)} %bitcast.10, bf16[3,512,128]{2,1,0:T(8,128)(2,1)S(1)} %bitcast.12, f32[1,512]{1,0:T(1,128)S(1)} %bitcast.13), custom_call_target="tpu_custom_call" | custom-call | tf_op jit(solution)/shard_map/pallas_call | solution.py:147
  14.3 0.0 collective-permute-done.one.refs_3_
  14.4 5.7 %collective-permute-start.4 = (bf16[1600,128]{1,0:T(8,128)(2,1)S(1)}, bf16[1600,128]{1,0:T(8,128)(2,1)S(1)}, u32[]{:S(2)}, u32[]{:S(2)}) collective-permute-start(bf16[1600,128]{1,0:T(8,128)(2,1)S(1)} %collective-permute-done.one.refs_3_), channel_id=1, source_target_pairs={{1,2},{3,4},{5,6},{7,0},{2,1},{4,3},{6,5},{0,7},{9,10},{11,12},{13... | collective-permute-start | bytes 1228808 | tf_op jit(solution)/shard_map/ppermute | solution.py:160
  20.0 0.0 collective-permute-done.1.two.refs_4_
  20.0 1.9 %collective-permute-start.5 = (bf16[1600,128]{1,0:T(8,128)(2,1)S(1)}, bf16[1600,128]{1,0:T(8,128)(2,1)S(1)}, u32[]{:S(2)}, u32[]{:S(2)}) collective-permute-start(bf16[1600,128]{1,0:T(8,128)(2,1)S(1)} %collective-permute-done.1.two.refs_4_), channel_id=1, source_target_pairs={{0,1},{2,3},{4,5},{6,7},{1,0},{3,2},{5,4},{7,6},{8,9},{10,11},{12,... | collective-permute-start | bytes 1228808 | tf_op jit(solution)/shard_map/ppermute | solution.py:160
  22.0 0.5 shard_map.70.refs_1_
  22.5 4.7 %collective-permute-done.4.refs_6_ = bf16[1600,128]{1,0:T(8,128)(2,1)S(1)} collective-permute-done((bf16[1600,128]{1,0:T(8,128)(2,1)S(1)}, bf16[1600,128]{1,0:T(8,128)(2,1)S(1)}, u32[]{:S(2)}, u32[]{:S(2)}) %collective-permute-start.4) | collective-permute-done | bytes 409632 | tf_op jit(solution)/shard_map/ppermute | solution.py:160
  27.2 3.7 %collective-permute-start.6 = (bf16[1600,128]{1,0:T(8,128)(2,1)S(1)}, bf16[1600,128]{1,0:T(8,128)(2,1)S(1)}, u32[]{:S(2)}, u32[]{:S(2)}) collective-permute-start(bf16[1600,128]{1,0:T(8,128)(2,1)S(1)} %collective-permute-done.4.refs_6_), channel_id=1, source_target_pairs={{0,1},{2,3},{4,5},{6,7},{1,0},{3,2},{5,4},{7,6},{8,9},{10,11},{12,... | collective-permute-start | bytes 1228808 | tf_op jit(solution)/shard_map/ppermute | solution.py:160
  31.0 0.1 collective-permute-done.5.refs_5_
  31.1 3.4 %collective-permute-start.7 = (bf16[1600,128]{1,0:T(8,128)(2,1)S(1)}, bf16[1600,128]{1,0:T(8,128)(2,1)S(1)}, u32[]{:S(2)}, u32[]{:S(2)}) collective-permute-start(bf16[1600,128]{1,0:T(8,128)(2,1)S(1)} %collective-permute-done.5.refs_5_), channel_id=1, source_target_pairs={{1,2},{3,4},{5,6},{7,0},{2,1},{4,3},{6,5},{0,7},{9,10},{11,12},{13... | collective-permute-start | bytes 1228808 | tf_op jit(solution)/shard_map/ppermute | solution.py:160
  34.5 4.8 %collective-permute-start.2 = (f32[3,64,384]{2,1,0:T(8,128)S(1)}, f32[3,64,384]{2,1,0:T(8,128)S(1)}, u32[]{:S(2)}, u32[]{:S(2)}) collective-permute-start(f32[3,64,384]{2,1,0:T(8,128)S(1)} %get-tuple-element.27), channel_id=1, source_target_pairs={{8,0},{16,8},{24,16},{32,24},{40,32},{48,40},{56,48},{64,56},{72,6... | collective-permute-start | bytes 884744 | tf_op jit(solution)/shard_map/ppermute | solution.py:189
  39.3 4.6 %collective-permute-start.3 = (f32[3,64,384]{2,1,0:T(8,128)S(1)}, f32[3,64,384]{2,1,0:T(8,128)S(1)}, u32[]{:S(2)}, u32[]{:S(2)}) collective-permute-start(f32[3,64,384]{2,1,0:T(8,128)S(1)} %get-tuple-element.28), channel_id=1, source_target_pairs={{0,8},{8,16},{16,24},{24,32},{32,40},{40,48},{48,56},{56,64},{64,7... | collective-permute-start | bytes 884744 | tf_op jit(solution)/shard_map/ppermute | solution.py:190
  43.9 0.0 collective-permute-done.6.refs_7_
  43.9 3.1 %collective-permute-start.9 = (bf16[960,128]{1,0:T(8,128)(2,1)S(1)}, bf16[960,128]{1,0:T(8,128)(2,1)S(1)}, u32[]{:S(2)}, u32[]{:S(2)}) collective-permute-start(bf16[960,128]{1,0:T(8,128)(2,1)S(1)} %slice.9), channel_id=1, source_target_pairs={{1,2},{3,4},{5,6},{7,0},{2,1},{4,3},{6,5},{0,7},{9,10},{11,12},{13... | collective-permute-start | bytes 737288 | tf_op jit(solution)/shard_map/ppermute | solution.py:160
  47.0 0.0 collective-permute-done.7.refs_8_
  47.0 1.9 %collective-permute-start.8 = (bf16[640,128]{1,0:T(8,128)(2,1)S(1)}, bf16[640,128]{1,0:T(8,128)(2,1)S(1)}, u32[]{:S(2)}, u32[]{:S(2)}) collective-permute-start(bf16[640,128]{1,0:T(8,128)(2,1)S(1)} %slice.8), channel_id=1, source_target_pairs={{0,1},{2,3},{4,5},{6,7},{1,0},{3,2},{5,4},{7,6},{8,9},{10,11},{12,... | collective-permute-start | bytes 491528 | tf_op jit(solution)/shard_map/ppermute | solution.py:160
  48.9 0.0 collective-permute-done.2.from_next
  48.9 0.0 collective-permute-done.3.from_prev
  49.0 0.2 shard_map.69.refs_0_
  49.1 1.4 %shard_map.71 = (f32[7,128,128]{2,1,0:T(8,128)S(1)}, f32[64,1536]{1,0:T(8,128)S(1)}) custom-call(bf16[1536,256]{1,0:T(8,128)(2,1)S(1)} %shard_map.69.refs_0_, f32[64,1536]{1,0:T(8,128)S(1)} %shard_map.70.refs_1_, bf16[1600,128]{1,0:T(8,128)(2,1)S(1)} %pad_maximum_fusion.own.refs_2_, bf16[1600,128]{1,0:T(8,128)(2,1)S(1)} %collective-permute-done.one.refs_3_, ...), custom_call_target="tpu_custom_call" | custom-call | tf_op jit(solution)/shard_map/pallas_call | solution.py:147
  50.5 4.5 %collective-permute-done.8.refs_4_ = bf16[640,128]{1,0:T(8,128)(2,1)S(1)} collective-permute-done((bf16[640,128]{1,0:T(8,128)(2,1)S(1)}, bf16[640,128]{1,0:T(8,128)(2,1)S(1)}, u32[]{:S(2)}, u32[]{:S(2)}) %collective-permute-start.8) | collective-permute-done | bytes 163872 | tf_op jit(solution)/shard_map/ppermute | solution.py:160
  55.0 0.0 collective-permute-done.9.refs_5_
  55.0 0.5 shard_map.72
  55.5 2.4 %collective-permute-start.10 = (f32[33,16,128]{2,1,0:T(8,128)S(1)}, f32[33,16,128]{2,1,0:T(8,128)S(1)}, u32[]{:S(2)}, u32[]{:S(2)}) collective-permute-start(f32[33,16,128]{2,1,0:T(8,128)S(1)} %get-tuple-element.37), channel_id=1, source_target_pairs={{0,8},{8,0},{1,9},{9,1},{2,10},{10,2},{3,11},{11,3},{4,12},{12,4},... | collective-permute-start | bytes 811016 | tf_op jit(solution)/shard_map/ppermute | solution.py:226
  57.9 1.2 %collective-permute-done.10.other = f32[33,16,128]{2,1,0:T(8,128)S(1)} collective-permute-done((f32[33,16,128]{2,1,0:T(8,128)S(1)}, f32[33,16,128]{2,1,0:T(8,128)S(1)}, u32[]{:S(2)}, u32[]{:S(2)}) %collective-permute-start.10) | collective-permute-done | bytes 270368 | tf_op jit(solution)/shard_map/ppermute | solution.py:226
  59.1 21.2 %all_to_all.5.refs_0_ = bf16[32,24,128]{2,1,0:T(8,128)(2,1)S(1)} all-to-all(bf16[32,24,128]{2,1,0:T(8,128)(2,1)S(1)} %shard_map.73), channel_id=1, replica_groups=mesh['x'=4,'z'=8,'core'=2,'y'=8] {'x','z'}, dimensions={0} | all-to-all | bytes 393216 | tf_op jit(solution)/shard_map/all_to_all | solution.py:228
  80.3 0.9 %shard_map.74 = (f32[16,128]{1,0:T(8,128)}, bf16[3,64,512]{2,1,0:T(8,128)(2,1)}) custom-call(bf16[32,24,128]{2,1,0:T(8,128)(2,1)S(1)} %all_to_all.5.refs_0_, f32[3,64,512]{2,1,0:T(8,128)S(1)} %get-tuple-element.39.refs_1_), custom_call_target="tpu_custom_call" | custom-call | tf_op jit(solution)/shard_map/pallas_call | solution.py:147
  (3 shorter events, 0.1 us)
Async XLA Ops:
  0.6 10.2 %copy-start.3 = (bf16[8,7,4096]{2,0,1:T(8,128)(2,1)S(1)}, bf16[8,7,4096]{2,0,1:T(8,128)(2,1)}, u32[]{:S(2)}) copy-start(bf16[8,7,4096]{2,0,1:T(8,128)(2,1)} %param.6) | copy-start | bytes 1376260
  1.7 10.1 %copy-start = (bf16[512,3,128]{2,0,1:T(8,128)(2,1)S(1)}, bf16[512,3,128]{2,0,1:T(8,128)(2,1)}, u32[]{:S(2)}) copy-start(bf16[512,3,128]{2,0,1:T(8,128)(2,1)} %param.5) | copy-start | bytes 1179652
  1.8 12.6 %collective-permute-start = (bf16[1600,128]{1,0:T(8,128)(2,1)S(1)}, bf16[1600,128]{1,0:T(8,128)(2,1)S(1)}, u32[]{:S(2)}, u32[]{:S(2)}) collective-permute-start(bf16[1600,128]{1,0:T(8,128)(2,1)S(1)} %pad_maximum_fusion.own.refs_2_), channel_id=1, source_target_pairs={{0,1},{2,3},{4,5},{6,7},{1,0},{3,2},{5,4},{7,6},{8,9},{10,11},{12,... | collective-permute-start | bytes 1228808 | tf_op jit(solution)/shard_map/ppermute | solution.py:160
  5.9 14.1 %collective-permute-start.1 = (bf16[1600,128]{1,0:T(8,128)(2,1)S(1)}, bf16[1600,128]{1,0:T(8,128)(2,1)S(1)}, u32[]{:S(2)}, u32[]{:S(2)}) collective-permute-start(bf16[1600,128]{1,0:T(8,128)(2,1)S(1)} %pad_maximum_fusion.own.refs_2_), channel_id=1, source_target_pairs={{1,2},{3,4},{5,6},{7,0},{2,1},{4,3},{6,5},{0,7},{9,10},{11,12},{13... | collective-permute-start | bytes 1228808 | tf_op jit(solution)/shard_map/ppermute | solution.py:160
  10.8 1.0 %copy-start.2 = (f32[512]{0:T(512)S(1)}, f32[512]{0:T(512)}, u32[]{:S(2)}) copy-start(f32[512]{0:T(512)} %param.9) | copy-start | bytes 6148
  11.8 0.7 copy-start.1
  14.4 12.9 %collective-permute-start.4 = (bf16[1600,128]{1,0:T(8,128)(2,1)S(1)}, bf16[1600,128]{1,0:T(8,128)(2,1)S(1)}, u32[]{:S(2)}, u32[]{:S(2)}) collective-permute-start(bf16[1600,128]{1,0:T(8,128)(2,1)S(1)} %collective-permute-done.one.refs_3_), channel_id=1, source_target_pairs={{1,2},{3,4},{5,6},{7,0},{2,1},{4,3},{6,5},{0,7},{9,10},{11,12},{13... | collective-permute-start | bytes 1228808 | tf_op jit(solution)/shard_map/ppermute | solution.py:160
  20.0 11.0 %collective-permute-start.5 = (bf16[1600,128]{1,0:T(8,128)(2,1)S(1)}, bf16[1600,128]{1,0:T(8,128)(2,1)S(1)}, u32[]{:S(2)}, u32[]{:S(2)}) collective-permute-start(bf16[1600,128]{1,0:T(8,128)(2,1)S(1)} %collective-permute-done.1.two.refs_4_), channel_id=1, source_target_pairs={{0,1},{2,3},{4,5},{6,7},{1,0},{3,2},{5,4},{7,6},{8,9},{10,11},{12,... | collective-permute-start | bytes 1228808 | tf_op jit(solution)/shard_map/ppermute | solution.py:160
  27.2 16.6 %collective-permute-start.6 = (bf16[1600,128]{1,0:T(8,128)(2,1)S(1)}, bf16[1600,128]{1,0:T(8,128)(2,1)S(1)}, u32[]{:S(2)}, u32[]{:S(2)}) collective-permute-start(bf16[1600,128]{1,0:T(8,128)(2,1)S(1)} %collective-permute-done.4.refs_6_), channel_id=1, source_target_pairs={{0,1},{2,3},{4,5},{6,7},{1,0},{3,2},{5,4},{7,6},{8,9},{10,11},{12,... | collective-permute-start | bytes 1228808 | tf_op jit(solution)/shard_map/ppermute | solution.py:160
  31.1 15.9 %collective-permute-start.7 = (bf16[1600,128]{1,0:T(8,128)(2,1)S(1)}, bf16[1600,128]{1,0:T(8,128)(2,1)S(1)}, u32[]{:S(2)}, u32[]{:S(2)}) collective-permute-start(bf16[1600,128]{1,0:T(8,128)(2,1)S(1)} %collective-permute-done.5.refs_5_), channel_id=1, source_target_pairs={{1,2},{3,4},{5,6},{7,0},{2,1},{4,3},{6,5},{0,7},{9,10},{11,12},{13... | collective-permute-start | bytes 1228808 | tf_op jit(solution)/shard_map/ppermute | solution.py:160
  34.5 14.5 %collective-permute-start.2 = (f32[3,64,384]{2,1,0:T(8,128)S(1)}, f32[3,64,384]{2,1,0:T(8,128)S(1)}, u32[]{:S(2)}, u32[]{:S(2)}) collective-permute-start(f32[3,64,384]{2,1,0:T(8,128)S(1)} %get-tuple-element.27), channel_id=1, source_target_pairs={{8,0},{16,8},{24,16},{32,24},{40,32},{48,40},{56,48},{64,56},{72,6... | collective-permute-start | bytes 884744 | tf_op jit(solution)/shard_map/ppermute | solution.py:189
  39.3 9.7 %collective-permute-start.3 = (f32[3,64,384]{2,1,0:T(8,128)S(1)}, f32[3,64,384]{2,1,0:T(8,128)S(1)}, u32[]{:S(2)}, u32[]{:S(2)}) collective-permute-start(f32[3,64,384]{2,1,0:T(8,128)S(1)} %get-tuple-element.28), channel_id=1, source_target_pairs={{0,8},{8,16},{16,24},{24,32},{32,40},{40,48},{48,56},{56,64},{64,7... | collective-permute-start | bytes 884744 | tf_op jit(solution)/shard_map/ppermute | solution.py:190
  43.9 11.1 %collective-permute-start.9 = (bf16[960,128]{1,0:T(8,128)(2,1)S(1)}, bf16[960,128]{1,0:T(8,128)(2,1)S(1)}, u32[]{:S(2)}, u32[]{:S(2)}) collective-permute-start(bf16[960,128]{1,0:T(8,128)(2,1)S(1)} %slice.9), channel_id=1, source_target_pairs={{1,2},{3,4},{5,6},{7,0},{2,1},{4,3},{6,5},{0,7},{9,10},{11,12},{13... | collective-permute-start | bytes 737288 | tf_op jit(solution)/shard_map/ppermute | solution.py:160
  47.0 8.0 %collective-permute-start.8 = (bf16[640,128]{1,0:T(8,128)(2,1)S(1)}, bf16[640,128]{1,0:T(8,128)(2,1)S(1)}, u32[]{:S(2)}, u32[]{:S(2)}) collective-permute-start(bf16[640,128]{1,0:T(8,128)(2,1)S(1)} %slice.8), channel_id=1, source_target_pairs={{0,1},{2,3},{4,5},{6,7},{1,0},{3,2},{5,4},{7,6},{8,9},{10,11},{12,... | collective-permute-start | bytes 491528 | tf_op jit(solution)/shard_map/ppermute | solution.py:160
  55.5 3.6 %collective-permute-start.10 = (f32[33,16,128]{2,1,0:T(8,128)S(1)}, f32[33,16,128]{2,1,0:T(8,128)S(1)}, u32[]{:S(2)}, u32[]{:S(2)}) collective-permute-start(f32[33,16,128]{2,1,0:T(8,128)S(1)} %get-tuple-element.37), channel_id=1, source_target_pairs={{0,8},{8,0},{1,9},{9,1},{2,10},{10,2},{3,11},{11,3},{4,12},{12,4},... | collective-permute-start | bytes 811016 | tf_op jit(solution)/shard_map/ppermute | solution.py:226
